TPU v7x, 256 devices: a whole 4x4x8 slice. The times are simulated.
256 devices in a mesh: narrow: 8 (over y_hi, x), wide: 32 (over y_lo, z, core).
Axes of the slice: x: 4, y: 4 (y_hi: 2, y_lo: 2; y = y_hi * 2 + y_lo), z: 8, core: 2. Of those that a mesh axis runs over, the one named last changes fastest.
Arguments:
- order_and_alloy_stack: float32 [2, 32, 2048, 512], P(None, 'narrow', 'wide'), may hold values from -1 to 1
- crystal_identifier: int32 [8, 512, 128], P('narrow', 'wide'), may hold values from 0 to 63
- frozen_indicator: int32 [8, 512, 128], P('narrow', 'wide'), may hold values 0 or 1
- supercool_grid: float32 [8, 512, 128], P('narrow', 'wide'), may hold values from -5 to 5
- crystal_rotation_radians: float32 [64], replicated, may hold values from -3.140625 to 3.140625
Outputs:
- state_new: float32 [2, 32, 2048, 512], P(None, 'narrow', 'wide')
- adjusted_supercool: float32 [8, 512, 128], P('narrow', 'wide')
Inputs may be any that keep to these rules, and one draw needn't show every extreme that they name: `crystal_identifier`: grain ids index crystal_rotation_radians.
All inputs are finite; a program needn't handle non-finite values. No bound on the sum of `frozen_indicator` on one device may be relied on, other than what follows from the above.
Results may differ from a plain program's by a relative error of at most 0.0003.
Values sent between devices are 32-bit elements; how exact they have to be, the bound alone decides.
No kernel may reach another device: no remote copies, remote signals or barrier semaphores. Data moves between devices by JAX's collectives and lax.ppermute only.
A program may use at most 192 MiB of HBM per device.

v0:
```python
import jax
import jax.numpy as jnp
from jax import lax
from jax.sharding import PartitionSpec as P

COARSEN = 4
FRINGE_BINS = 4


DT = 0.15
EPS4 = 0.15
COUPLING_FACTOR = 1.5
DLIQ = 1.0
DSOL = 0.05
KPART = 0.15
KLIQ = 1.0
KSOL = 0.5
SIGMA = 0.05
KBAR = 0.75
HIGHEST = lax.Precision.HIGHEST


def extended(array, sides, width):
    for axis, dim in sides:
        size, length = (lax.axis_size(axis), array.shape[dim])
        up = [(i, (i + 1) % size) for i in range(size - 1)]
        down = [(j, i) for i, j in up]
        last = lax.slice_in_dim(array, length - width, length, axis=dim)
        initial = lax.slice_in_dim(array, 0, width, axis=dim)
        before = lax.ppermute(last, axis, up)
        after = lax.ppermute(initial, axis, down)
        array = jnp.concatenate([before, array, after], axis=dim)
    return array


def shift_last(values, offset):
    filler = jnp.zeros_like(values[..., :1])
    if offset > 0:
        return jnp.concatenate([values[..., 1:], filler], -1)
    return jnp.concatenate([filler, values[..., :-1]], -1)


def orient(grain_ids, crystal_rotation_radians):
    labels = jnp.arange(crystal_rotation_radians.shape[0], dtype=jnp.int32)
    matches = grain_ids[..., None] == labels
    cos_c = jnp.sum(jnp.where(matches, jnp.cos(crystal_rotation_radians), 0.0), -1)
    sin_c = jnp.sum(jnp.where(matches, jnp.sin(crystal_rotation_radians), 0.0), -1)
    return (cos_c, sin_c)


def refine_onto_grid(coarse):
    rough_sheets, rough_verticals, length = coarse.shape
    tiled_up = jnp.broadcast_to(
        coarse[:, None, :, None, :, None],
        (rough_sheets, COARSEN, rough_verticals, COARSEN, length, COARSEN),
    )
    return tiled_up.reshape(rough_sheets * COARSEN, rough_verticals * COARSEN, length * COARSEN)


def restrict(fine_field):
    planes_f, columns_f, length = fine_field.shape
    blocks = fine_field.reshape(
        planes_f // COARSEN, COARSEN, columns_f // COARSEN, COARSEN, length // COARSEN, COARSEN
    )
    return jnp.mean(blocks, axis=(1, 3, 5))


def flux_of(order_parameter_padded, cosine, sine_t):
    centre = order_parameter_padded[1:-1, 1:-1]
    grad_z = 0.5 * (order_parameter_padded[2:, 1:-1] - order_parameter_padded[:-2, 1:-1])
    grad_x = 0.5 * (order_parameter_padded[1:-1, 2:] - order_parameter_padded[1:-1, :-2])
    grad_y = 0.5 * (shift_last(centre, 1) - shift_last(centre, -1))
    rotated_u = cosine * grad_x + sine_t * grad_y
    rotated_v = cosine * grad_y - sine_t * grad_x
    square = grad_z * grad_z + grad_x * grad_x + grad_y * grad_y
    quartic = (grad_z**4 + rotated_u**4 + rotated_v**4) / (square + 1.0) ** 2
    anisotropy = 1.0 + EPS4 * (4.0 * quartic - 3.0)
    blending_factor = anisotropy * anisotropy
    return (
        (blending_factor * grad_z, blending_factor * grad_x, blending_factor * grad_y),
        blending_factor,
    )


def divergence(transport_third, transport_first, transport_second):
    return (
        0.5 * (transport_third[2:, 1:-1] - transport_third[:-2, 1:-1])
        + 0.5 * (transport_first[1:-1, 2:] - transport_first[1:-1, :-2])
        + 0.5 * (shift_last(transport_second, 1) - shift_last(transport_second, -1))
    )


def diffuse(order_parameter_padded, alloy_padded):
    order_parameter = order_parameter_padded[1:-1, 1:-1]
    alloy_concentration = alloy_padded[1:-1, 1:-1]
    mobile = DSOL + 0.5 * DLIQ * (1.0 - order_parameter)
    neighbours = [
        (order_parameter_padded[2:, 1:-1], alloy_padded[2:, 1:-1]),
        (order_parameter_padded[:-2, 1:-1], alloy_padded[:-2, 1:-1]),
        (order_parameter_padded[1:-1, 2:], alloy_padded[1:-1, 2:]),
        (order_parameter_padded[1:-1, :-2], alloy_padded[1:-1, :-2]),
        (shift_last(order_parameter, 1), shift_last(alloy_concentration, 1)),
        (shift_last(order_parameter, -1), shift_last(alloy_concentration, -1)),
    ]
    accumulated_pieces = jnp.zeros_like(alloy_concentration)
    for near_phase, near_solute in neighbours:
        accumulated_pieces = accumulated_pieces + 0.5 * (
            mobile + DSOL + 0.5 * DLIQ * (1.0 - near_phase)
        ) * (near_solute - alloy_concentration)
    return accumulated_pieces


def march_forward(
    order_parameter_padded,
    alloy_padded,
    transport_third,
    transport_first,
    transport_second,
    blending_factor,
    supercool_refined,
):
    order_parameter = order_parameter_padded[1:-1, 1:-1]
    alloy_concentration = alloy_padded[1:-1, 1:-1]
    distribute_values = divergence(transport_third, transport_first, transport_second)
    driving_force = (
        distribute_values
        + order_parameter
        - order_parameter**3
        - COUPLING_FACTOR
        * (alloy_concentration + supercool_refined)
        * (1.0 - order_parameter * order_parameter) ** 2
    )
    order_parameter_next = order_parameter + DT * driving_force / blending_factor
    alloy_next = (
        alloy_concentration
        + DT * diffuse(order_parameter_padded, alloy_padded)
        + 0.5
        * (1.0 + (1.0 - KPART) * alloy_concentration)
        * (order_parameter_next - order_parameter)
    )
    return (order_parameter_next, alloy_next)


def diffusive_contribution(temp_p, extra_p):
    inner = (slice(1, -1), slice(1, -1), slice(1, -1))
    centre_t = temp_p[inner]
    centre_k = extra_p[inner]
    accumulated_pieces = jnp.zeros_like(centre_t)
    for direction in range(3):
        for offset in (0, 2):
            window = [slice(1, -1), slice(1, -1), slice(1, -1)]
            window[direction] = slice(offset, offset + centre_t.shape[direction])
            window = tuple(window)
            accumulated_pieces = accumulated_pieces + (
                KLIQ + 0.5 * (centre_k + extra_p[window])
            ) * (temp_p[window] - centre_t)
    return accumulated_pieces


def sine_basis(points):
    ordinal = jnp.arange(points, dtype=jnp.float32) + 1.0
    angles = jnp.pi * ordinal[:, None] * ordinal[None, :] / (points + 1.0)
    basis = jnp.sqrt(2.0 / (points + 1.0)) * jnp.sin(angles)
    levels = 2.0 - 2.0 * jnp.cos(jnp.pi * ordinal / (points + 1.0))
    return (basis, levels)


def transform(values, basis_z, basis_x, basis_y):
    values = jnp.einsum("ab,bxy->axy", basis_z, values, precision=HIGHEST)
    values = jnp.einsum("ab,zby->zay", basis_x, values, precision=HIGHEST)
    return jnp.einsum("zxb,ab->zxa", values, basis_y, precision=HIGHEST)


def fdm_solve(right_side):
    basis_z, level_z = sine_basis(right_side.shape[0])
    basis_x, level_x = sine_basis(right_side.shape[1])
    basis_y, level_y = sine_basis(right_side.shape[2])
    divisor = SIGMA + KBAR * (
        level_z[:, None, None] + level_x[None, :, None] + level_y[None, None, :]
    )
    spectral = transform(right_side, basis_z, basis_x, basis_y) / divisor
    return transform(spectral, basis_z, basis_x, basis_y)


def on_device(
    order_and_alloy_stack,
    crystal_identifier,
    frozen_indicator,
    supercool_grid,
    crystal_rotation_radians,
):
    rough_sheets, rough_verticals, rough_extent = supercool_grid.shape
    narrow_at = lax.axis_index("narrow")
    wide_at = lax.axis_index("wide")
    cos_c, sin_c = orient(crystal_identifier, crystal_rotation_radians)
    supercool_refined = refine_onto_grid(supercool_grid)
    adjacent_values = extended(order_and_alloy_stack, (("narrow", 1), ("wide", 2)), 1)
    transport_rates, blending_factor = flux_of(
        adjacent_values[0], refine_onto_grid(cos_c), refine_onto_grid(sin_c)
    )
    incoming_values = extended(
        jnp.stack([transport_rates[0], transport_rates[1]]), (("narrow", 1), ("wide", 2)), 1
    )
    order_parameter_next, alloy_next = march_forward(
        adjacent_values[0],
        adjacent_values[1],
        incoming_values[0],
        incoming_values[1],
        transport_rates[2],
        blending_factor,
        supercool_refined,
    )
    state_new = jnp.stack([order_parameter_next, alloy_next])
    latent_release = restrict(order_parameter_next - order_and_alloy_stack[0])
    diffusive_fringe = (KSOL - KLIQ) * frozen_indicator.astype(jnp.float32)
    bundled_pieces = jnp.stack([latent_release, supercool_grid, diffusive_fringe])
    gathered = lax.all_gather(bundled_pieces, "narrow", axis=1, tiled=True)
    column = extended(gathered, (("wide", 2),), FRINGE_BINS + 1)
    zy_rim = ((1, 1), (0, 0), (1, 1))
    energy_imbalance = column[0][:, 1:-1] + diffusive_contribution(
        jnp.pad(column[1], zy_rim), jnp.pad(column[2], zy_rim)
    )
    sub_columns = energy_imbalance.shape[1]
    column_pos = jnp.arange(sub_columns, dtype=jnp.int32) + wide_at * rough_verticals - FRINGE_BINS
    column_in = (column_pos >= 0) & (column_pos < rough_verticals * lax.axis_size("wide"))
    energy_imbalance = (
        energy_imbalance * jnp.where(column_in, 1.0, 0.0).astype(jnp.float32)[None, :, None]
    )
    solved = fdm_solve(energy_imbalance)
    own_planes = lax.dynamic_slice_in_dim(solved, narrow_at * rough_sheets, rough_sheets, 0)
    rim_pair = jnp.concatenate(
        [own_planes[:, :FRINGE_BINS], own_planes[:, sub_columns - FRINGE_BINS :]], 1
    )
    returned = extended(rim_pair, (("wide", 1),), FRINGE_BINS)
    schwarz_adjustment = own_planes[:, FRINGE_BINS : FRINGE_BINS + rough_verticals]
    schwarz_adjustment = schwarz_adjustment.at[:, :FRINGE_BINS].add(returned[:, :FRINGE_BINS])
    schwarz_adjustment = schwarz_adjustment.at[:, rough_verticals - FRINGE_BINS :].add(
        returned[:, 3 * FRINGE_BINS :]
    )
    adjusted_supercool = supercool_grid + schwarz_adjustment
    return (state_new, adjusted_supercool)


def solution(mesh):
    return jax.shard_map(
        on_device,
        mesh=mesh,
        in_specs=(
            P(None, "narrow", "wide", None),
            P("narrow", "wide", None),
            P("narrow", "wide", None),
            P("narrow", "wide", None),
            P(),
        ),
        out_specs=(P(None, "narrow", "wide", None), P("narrow", "wide", None)),
        check_vma=False,
    )
```

profile of v0, /device:TPU:24, one launch (start us, length us, event | category | flops | bytes accessed | tf_op | source)
XLA Modules:
  0.0 147.6 jit_solution(8377283690014976220)
XLA Ops:
  0.6 1.2 fusion.111
  1.8 3.4 %collective-permute-start = (f32[2,1,64,512]{3,2,1,0:T(8,128)S(1)}, f32[2,1,64,512]{3,2,1,0:T(8,128)S(1)}, u32[]{:S(2)}, u32[]{:S(2)}) collective-permute-start(f32[2,1,64,512]{3,2,1,0:T(8,128)S(1)} %get-tuple-element.45), channel_id=1, source_target_pairs={{0,32},{32,64},{64,96},{96,128},{128,160},{160,192},{192,224},{1,3... | collective-permute-start | bytes 786440 | tf_op jit(solution)/shard_map/ppermute | solution.py:30
  5.2 6.1 %collective-permute-start.1 = (f32[2,1,64,512]{3,2,1,0:T(8,128)S(1)}, f32[2,1,64,512]{3,2,1,0:T(8,128)S(1)}, u32[]{:S(2)}, u32[]{:S(2)}) collective-permute-start(f32[2,1,64,512]{3,2,1,0:T(8,128)S(1)} %get-tuple-element.44), channel_id=1, source_target_pairs={{32,0},{64,32},{96,64},{128,96},{160,128},{192,160},{224,192},{33,... | collective-permute-start | bytes 786440 | tf_op jit(solution)/shard_map/ppermute | solution.py:31
  13.2 2.2 %collective-permute-done = f32[2,1,64,512]{3,2,1,0:T(8,128)S(1)} collective-permute-done((f32[2,1,64,512]{3,2,1,0:T(8,128)S(1)}, f32[2,1,64,512]{3,2,1,0:T(8,128)S(1)}, u32[]{:S(2)}, u32[]{:S(2)}) %collective-permute-start) | collective-permute-done | bytes 262176 | tf_op jit(solution)/shard_map/ppermute | solution.py:30
  16.6 6.2 %collective-permute-start.3 = (f32[2,6,1,512]{3,2,1,0:T(1,128)S(1)}, f32[2,6,1,512]{3,2,1,0:T(1,128)S(1)}, u32[]{:S(2)}, u32[]{:S(2)}) collective-permute-start(f32[2,6,1,512]{3,2,1,0:T(1,128)S(1)} %get-tuple-element.39), channel_id=1, source_target_pairs={{1,0},{2,1},{3,2},{4,3},{5,4},{6,5},{7,6},{8,7},{9,8},{10,9},{11,1... | collective-permute-start | bytes 73736 | tf_op jit(solution)/shard_map/ppermute | solution.py:31
  22.8 1.9 %collective-permute-start.2 = (f32[2,6,1,512]{3,2,1,0:T(1,128)S(1)}, f32[2,6,1,512]{3,2,1,0:T(1,128)S(1)}, u32[]{:S(2)}, u32[]{:S(2)}) collective-permute-start(f32[2,6,1,512]{3,2,1,0:T(1,128)S(1)} %get-tuple-element.38), channel_id=1, source_target_pairs={{0,1},{1,2},{2,3},{3,4},{4,5},{5,6},{6,7},{7,8},{8,9},{9,10},{10,1... | collective-permute-start | bytes 73736 | tf_op jit(solution)/shard_map/ppermute | solution.py:30
  24.8 2.5 %broadcast_in_dim.60 = f32[16,4,128,4]{3,2,1,0:T(8,128)} broadcast(f32[16,128]{1,0:T(8,128)S(1)} %get-tuple-element.63), dimensions={0,2} | broadcast | bytes 139264 | tf_op jit(solution)/shard_map/broadcast_in_dim | solution.py:53
  27.3 4.9 %mul.381 = f32[64,512]{1,0:T(8,128)S(1)} reshape(f32[16,4,128,4]{3,2,1,0:T(8,128)} %broadcast_in_dim.60) | data formatting | bytes 262144 | tf_op jit(solution)/shard_map/mul | solution.py:73
  32.2 2.5 %broadcast_in_dim.58 = f32[16,4,128,4]{3,2,1,0:T(8,128)} broadcast(f32[16,128]{1,0:T(8,128)S(1)} %get-tuple-element.64), dimensions={0,2} | broadcast | bytes 139264 | tf_op jit(solution)/shard_map/broadcast_in_dim | solution.py:53
  34.8 5.6 %mul.377 = f32[64,512]{1,0:T(8,128)} reshape(f32[16,4,128,4]{3,2,1,0:T(8,128)} %broadcast_in_dim.58) | data formatting | bytes 262144 | tf_op jit(solution)/shard_map/mul | solution.py:73
  40.8 1.4 fusion.112
  42.2 1.5 %multiply_multiply_fusion.1 = (f32[4,64,512]{2,1,0:T(8,128)}, f32[4,64,512]{2,1,0:T(8,128)S(1)}) fusion(f32[4,64,511]{2,1,0:T(8,128)S(1)} %get-tuple-element.61, f32[4,64,511]{2,1,0:T(8,128)S(1)} %get-tuple-element.62, f32[64,512]{1,0:T(8,128)S(1)} %mul.381, f32[64,512]{1,0:T(8,128)S(1)} %copy-done.7, f32[6,66,512]{2,1,0:T(8,128)S(1)} %get-tuple-element.34), kind=kLoop, calls=%fused_computation.60 | loop fusion | flops 4325376 | bytes 4454400 | tf_op jit(solution)/shard_map/mul | solution.py:80
  44.8 8.6 %collective-permute-start.5 = (f32[2,1,64,512]{3,2,1,0:T(8,128)}, f32[2,1,64,512]{3,2,1,0:T(8,128)}, u32[]{:S(2)}, u32[]{:S(2)}) collective-permute-start(f32[2,1,64,512]{3,2,1,0:T(8,128)} %get-tuple-element.43), channel_id=1, source_target_pairs={{32,0},{64,32},{96,64},{128,96},{160,128},{192,160},{224,192},{33,... | collective-permute-start | bytes 786440 | tf_op jit(solution)/shard_map/ppermute | solution.py:31
  53.4 1.9 %collective-permute-start.4 = (f32[2,1,64,512]{3,2,1,0:T(8,128)}, f32[2,1,64,512]{3,2,1,0:T(8,128)}, u32[]{:S(2)}, u32[]{:S(2)}) collective-permute-start(f32[2,1,64,512]{3,2,1,0:T(8,128)} %get-tuple-element.42), channel_id=1, source_target_pairs={{0,32},{32,64},{64,96},{96,128},{128,160},{160,192},{192,224},{1,3... | collective-permute-start | bytes 786440 | tf_op jit(solution)/shard_map/ppermute | solution.py:30
  55.3 2.5 %broadcast_in_dim.62 = f32[16,4,128,4]{3,2,1,0:T(8,128)} broadcast(f32[16,128]{1,0:T(8,128)S(1)} %bitcast.60), dimensions={0,2} | broadcast | bytes 139264 | tf_op jit(solution)/shard_map/broadcast_in_dim | solution.py:53
  57.9 5.0 %broadcast_in_dim.63 = f32[64,512]{1,0:T(8,128)S(1)} reshape(f32[16,4,128,4]{3,2,1,0:T(8,128)} %broadcast_in_dim.62) | data formatting | bytes 262144 | tf_op jit(solution)/shard_map/broadcast_in_dim | solution.py:53
  62.9 2.7 %collective-permute-done.4 = f32[2,1,64,512]{3,2,1,0:T(8,128)} collective-permute-done((f32[2,1,64,512]{3,2,1,0:T(8,128)}, f32[2,1,64,512]{3,2,1,0:T(8,128)}, u32[]{:S(2)}, u32[]{:S(2)}) %collective-permute-start.4) | collective-permute-done | bytes 262176 | tf_op jit(solution)/shard_map/ppermute | solution.py:30
  66.4 5.8 %collective-permute-start.7 = (f32[2,6,1,512]{3,2,1,0:T(1,128)S(1)}, f32[2,6,1,512]{3,2,1,0:T(1,128)S(1)}, u32[]{:S(2)}, u32[]{:S(2)}) collective-permute-start(f32[2,6,1,512]{3,2,1,0:T(1,128)S(1)} %get-tuple-element.37), channel_id=1, source_target_pairs={{1,0},{2,1},{3,2},{4,3},{5,4},{6,5},{7,6},{8,7},{9,8},{10,9},{11,1... | collective-permute-start | bytes 73736 | tf_op jit(solution)/shard_map/ppermute | solution.py:31
  72.2 2.1 %collective-permute-start.6 = (f32[2,6,1,512]{3,2,1,0:T(1,128)S(1)}, f32[2,6,1,512]{3,2,1,0:T(1,128)S(1)}, u32[]{:S(2)}, u32[]{:S(2)}) collective-permute-start(f32[2,6,1,512]{3,2,1,0:T(1,128)S(1)} %get-tuple-element.36), channel_id=1, source_target_pairs={{0,1},{1,2},{2,3},{3,4},{4,5},{5,6},{6,7},{7,8},{8,9},{9,10},{10,1... | collective-permute-start | bytes 73736 | tf_op jit(solution)/shard_map/ppermute | solution.py:30
  74.5 4.9 %collective-permute-done.6 = f32[2,6,1,512]{3,2,1,0:T(1,128)S(1)} collective-permute-done((f32[2,6,1,512]{3,2,1,0:T(1,128)S(1)}, f32[2,6,1,512]{3,2,1,0:T(1,128)S(1)}, u32[]{:S(2)}, u32[]{:S(2)}) %collective-permute-start.6) | collective-permute-done | bytes 24608 | tf_op jit(solution)/shard_map/ppermute | solution.py:30
  79.5 1.3 pad_maximum_fusion.1
  80.9 1.1 copy-done.6
  82.6 5.6 %reduce_sum.37 = f32[16,4,128,4]{3,2,1,0:T(8,128)} reshape(f32[64,512]{1,0:T(8,128)S(1)} %get-tuple-element.28) | data formatting | bytes 262144 | tf_op jit(solution)/shard_map/reduce_sum | solution.py:65
  88.3 2.6 %reduce_sum.38 = f32[16,128]{1,0:T(8,128)S(1)} reduce(f32[16,4,128,4]{3,2,1,0:T(8,128)} %reduce_sum.37, f32[]{:T(128)} %constant.118.clone.1), dimensions={1,3}, to_apply=%region_3.4 | reduce | flops 30720 | bytes 139268 | tf_op jit(solution)/shard_map/reduce_sum | solution.py:65
  90.9 34.3 %all_gather.3 = f32[3,8,16,128]{3,2,1,0:T(8,128)S(1)} all-gather(f32[3,1,16,128]{3,2,1,0:T(8,128)S(1)} %pad_maximum_fusion.10), channel_id=1, replica_groups=mesh['narrow'=8,'wide'=32] {'narrow'}, dimensions={1}, use_global_device_ids=true | all-gather | bytes 221184 | tf_op jit(solution)/shard_map/all_gather | solution.py:217
  125.2 1.9 %collective-permute-start.9 = (f32[3,8,5,128]{3,2,1,0:T(8,128)S(1)}, f32[3,8,5,128]{3,2,1,0:T(8,128)S(1)}, u32[]{:S(2)}, u32[]{:S(2)}) collective-permute-start(f32[3,8,5,128]{3,2,1,0:T(8,128)S(1)} %get-tuple-element.56), channel_id=1, source_target_pairs={{1,0},{2,1},{3,2},{4,3},{5,4},{6,5},{7,6},{8,7},{9,8},{10,9},{11,1... | collective-permute-start | bytes 184328 | tf_op jit(solution)/shard_map/ppermute | solution.py:31
  127.2 2.4 %collective-permute-start.8 = (f32[3,8,5,128]{3,2,1,0:T(8,128)S(1)}, f32[3,8,5,128]{3,2,1,0:T(8,128)S(1)}, u32[]{:S(2)}, u32[]{:S(2)}) collective-permute-start(f32[3,8,5,128]{3,2,1,0:T(8,128)S(1)} %get-tuple-element.55), channel_id=1, source_target_pairs={{0,1},{1,2},{2,3},{3,4},{4,5},{5,6},{6,7},{7,8},{8,9},{9,10},{10,1... | collective-permute-start | bytes 184328 | tf_op jit(solution)/shard_map/ppermute | solution.py:30
  129.6 2.3 %fusion.14 = f32[1,4,64,512]{3,2,1,0:T(8,128)S(1)} fusion(f32[6,66,512]{2,1,0:T(8,128)S(1)} %get-tuple-element.35, f32[4,64,512]{2,1,0:T(8,128)S(1)} %get-tuple-element.29, f32[4,64,511]{2,1,0:T(8,128)} %get-tuple-element.47, f32[4,64,511]{2,1,0:T(8,128)} %get-tuple-element.46, f32[6,66,512]{2,1,0:T(8,128)S(1)} %get-tuple-element.34, ...), kind=kLoop, calls=%fused_computation.35 | loop fusion | flops 6815744 | bytes 8384512 | tf_op jit(solution)/shard_map/stack | solution.py:213
  133.0 2.3 %collective-permute-done.8 = f32[3,8,5,128]{3,2,1,0:T(8,128)S(1)} collective-permute-done((f32[3,8,5,128]{3,2,1,0:T(8,128)S(1)}, f32[3,8,5,128]{3,2,1,0:T(8,128)S(1)}, u32[]{:S(2)}, u32[]{:S(2)}) %collective-permute-start.8) | collective-permute-done | bytes 61472 | tf_op jit(solution)/shard_map/ppermute | solution.py:30
  138.0 1.9 %collective-permute-start.10 = (f32[1,4,128]{2,1,0:T(4,128)S(1)}, f32[1,4,128]{2,1,0:T(4,128)S(1)}, u32[]{:S(2)}, u32[]{:S(2)}) collective-permute-start(f32[1,4,128]{2,1,0:T(4,128)S(1)} %get-tuple-element.58), channel_id=1, source_target_pairs={{0,1},{1,2},{2,3},{3,4},{4,5},{5,6},{6,7},{7,8},{8,9},{9,10},{10,1... | collective-permute-start | bytes 6152 | tf_op jit(solution)/shard_map/ppermute | solution.py:30
  140.0 5.8 %collective-permute-start.11 = (f32[1,4,128]{2,1,0:T(4,128)S(1)}, f32[1,4,128]{2,1,0:T(4,128)S(1)}, u32[]{:S(2)}, u32[]{:S(2)}) collective-permute-start(f32[1,4,128]{2,1,0:T(4,128)S(1)} %get-tuple-element.57), channel_id=1, source_target_pairs={{1,0},{2,1},{3,2},{4,3},{5,4},{6,5},{7,6},{8,7},{9,8},{10,9},{11,1... | collective-permute-start | bytes 6152 | tf_op jit(solution)/shard_map/ppermute | solution.py:31
  145.8 1.3 collective-permute-done.11
  (68 shorter events, 10.9 us)
Async XLA Ops:
  0.6 14.8 %copy-start.5 = (f32[2,4,64,512]{3,2,1,0:T(8,128)S(1)}, f32[2,4,64,512]{3,2,1,0:T(8,128)}, u32[]{:S(2)}) copy-start(f32[2,4,64,512]{3,2,1,0:T(8,128)} %param.9) | copy-start | bytes 3145732
  1.8 13.6 %collective-permute-start = (f32[2,1,64,512]{3,2,1,0:T(8,128)S(1)}, f32[2,1,64,512]{3,2,1,0:T(8,128)S(1)}, u32[]{:S(2)}, u32[]{:S(2)}) collective-permute-start(f32[2,1,64,512]{3,2,1,0:T(8,128)S(1)} %get-tuple-element.45), channel_id=1, source_target_pairs={{0,32},{32,64},{64,96},{96,128},{128,160},{160,192},{192,224},{1,3... | collective-permute-start | bytes 786440 | tf_op jit(solution)/shard_map/ppermute | solution.py:30
  5.2 11.3 %collective-permute-start.1 = (f32[2,1,64,512]{3,2,1,0:T(8,128)S(1)}, f32[2,1,64,512]{3,2,1,0:T(8,128)S(1)}, u32[]{:S(2)}, u32[]{:S(2)}) collective-permute-start(f32[2,1,64,512]{3,2,1,0:T(8,128)S(1)} %get-tuple-element.44), channel_id=1, source_target_pairs={{32,0},{64,32},{96,64},{128,96},{160,128},{192,160},{224,192},{33,... | collective-permute-start | bytes 786440 | tf_op jit(solution)/shard_map/ppermute | solution.py:31
  16.6 23.7 %collective-permute-start.3 = (f32[2,6,1,512]{3,2,1,0:T(1,128)S(1)}, f32[2,6,1,512]{3,2,1,0:T(1,128)S(1)}, u32[]{:S(2)}, u32[]{:S(2)}) collective-permute-start(f32[2,6,1,512]{3,2,1,0:T(1,128)S(1)} %get-tuple-element.39), channel_id=1, source_target_pairs={{1,0},{2,1},{3,2},{4,3},{5,4},{6,5},{7,6},{8,7},{9,8},{10,9},{11,1... | collective-permute-start | bytes 73736 | tf_op jit(solution)/shard_map/ppermute | solution.py:31
  22.8 17.5 %collective-permute-start.2 = (f32[2,6,1,512]{3,2,1,0:T(1,128)S(1)}, f32[2,6,1,512]{3,2,1,0:T(1,128)S(1)}, u32[]{:S(2)}, u32[]{:S(2)}) collective-permute-start(f32[2,6,1,512]{3,2,1,0:T(1,128)S(1)} %get-tuple-element.38), channel_id=1, source_target_pairs={{0,1},{1,2},{2,3},{3,4},{4,5},{5,6},{6,7},{7,8},{8,9},{9,10},{10,1... | collective-permute-start | bytes 73736 | tf_op jit(solution)/shard_map/ppermute | solution.py:30
  40.8 1.4 copy-start.7
  42.2 1.5 %copy-start.1 = (f32[4,64,511]{2,1,0:T(8,128)}, f32[4,64,511]{2,1,0:T(8,128)S(1)}, u32[]{:S(2)}) copy-start(f32[4,64,511]{2,1,0:T(8,128)S(1)} %get-tuple-element.61) | copy-start | bytes 1569796
  42.2 1.5 %copy-start.3 = (f32[4,64,511]{2,1,0:T(8,128)}, f32[4,64,511]{2,1,0:T(8,128)S(1)}, u32[]{:S(2)}) copy-start(f32[4,64,511]{2,1,0:T(8,128)S(1)} %get-tuple-element.62) | copy-start | bytes 1569796
  43.7 11.6 %copy-start.8 = (f32[1,16,128]{2,1,0:T(8,128)S(1)}, f32[1,16,128]{2,1,0:T(8,128)}, u32[]{:S(2)}) copy-start(f32[1,16,128]{2,1,0:T(8,128)} %param.12) | copy-start | bytes 24580
  44.8 18.1 %collective-permute-start.5 = (f32[2,1,64,512]{3,2,1,0:T(8,128)}, f32[2,1,64,512]{3,2,1,0:T(8,128)}, u32[]{:S(2)}, u32[]{:S(2)}) collective-permute-start(f32[2,1,64,512]{3,2,1,0:T(8,128)} %get-tuple-element.43), channel_id=1, source_target_pairs={{32,0},{64,32},{96,64},{128,96},{160,128},{192,160},{224,192},{33,... | collective-permute-start | bytes 786440 | tf_op jit(solution)/shard_map/ppermute | solution.py:31
  53.4 12.2 %collective-permute-start.4 = (f32[2,1,64,512]{3,2,1,0:T(8,128)}, f32[2,1,64,512]{3,2,1,0:T(8,128)}, u32[]{:S(2)}, u32[]{:S(2)}) collective-permute-start(f32[2,1,64,512]{3,2,1,0:T(8,128)} %get-tuple-element.42), channel_id=1, source_target_pairs={{0,32},{32,64},{64,96},{96,128},{128,160},{160,192},{192,224},{1,3... | collective-permute-start | bytes 786440 | tf_op jit(solution)/shard_map/ppermute | solution.py:30
  57.9 5.0 %copy-start.9 = (s32[1,16,128]{2,1,0:T(8,128)S(1)}, s32[1,16,128]{2,1,0:T(8,128)}, u32[]{:S(2)}) copy-start(s32[1,16,128]{2,1,0:T(8,128)} %param.11) | copy-start | bytes 24580
  62.8 11.5 %copy-start = (f32[4,64,512]{2,1,0:T(8,128)S(1)}, f32[4,64,512]{2,1,0:T(8,128)}, u32[]{:S(2)}) copy-start(f32[4,64,512]{2,1,0:T(8,128)} %get-tuple-element.30) | copy-start | bytes 1572868
  66.4 8.1 %collective-permute-start.7 = (f32[2,6,1,512]{3,2,1,0:T(1,128)S(1)}, f32[2,6,1,512]{3,2,1,0:T(1,128)S(1)}, u32[]{:S(2)}, u32[]{:S(2)}) collective-permute-start(f32[2,6,1,512]{3,2,1,0:T(1,128)S(1)} %get-tuple-element.37), channel_id=1, source_target_pairs={{1,0},{2,1},{3,2},{4,3},{5,4},{6,5},{7,6},{8,7},{9,8},{10,9},{11,1... | collective-permute-start | bytes 73736 | tf_op jit(solution)/shard_map/ppermute | solution.py:31
  72.2 7.3 %collective-permute-start.6 = (f32[2,6,1,512]{3,2,1,0:T(1,128)S(1)}, f32[2,6,1,512]{3,2,1,0:T(1,128)S(1)}, u32[]{:S(2)}, u32[]{:S(2)}) collective-permute-start(f32[2,6,1,512]{3,2,1,0:T(1,128)S(1)} %get-tuple-element.36), channel_id=1, source_target_pairs={{0,1},{1,2},{2,3},{3,4},{4,5},{5,6},{6,7},{7,8},{8,9},{9,10},{10,1... | collective-permute-start | bytes 73736 | tf_op jit(solution)/shard_map/ppermute | solution.py:30
  80.7 1.2 copy-start.6
  88.3 41.3 %copy-start.2 = (f32[4,64,511]{2,1,0:T(8,128)S(1)}, f32[4,64,511]{2,1,0:T(8,128)}, u32[]{:S(2)}) copy-start(f32[4,64,511]{2,1,0:T(8,128)} %copy-done.1) | copy-start | bytes 1569796
  88.3 41.3 %copy-start.4 = (f32[4,64,511]{2,1,0:T(8,128)S(1)}, f32[4,64,511]{2,1,0:T(8,128)}, u32[]{:S(2)}) copy-start(f32[4,64,511]{2,1,0:T(8,128)} %copy-done.3) | copy-start | bytes 1569796
  125.2 7.7 %collective-permute-start.9 = (f32[3,8,5,128]{3,2,1,0:T(8,128)S(1)}, f32[3,8,5,128]{3,2,1,0:T(8,128)S(1)}, u32[]{:S(2)}, u32[]{:S(2)}) collective-permute-start(f32[3,8,5,128]{3,2,1,0:T(8,128)S(1)} %get-tuple-element.56), channel_id=1, source_target_pairs={{1,0},{2,1},{3,2},{4,3},{5,4},{6,5},{7,6},{8,7},{9,8},{10,9},{11,1... | collective-permute-start | bytes 184328 | tf_op jit(solution)/shard_map/ppermute | solution.py:31
  127.2 8.0 %collective-permute-start.8 = (f32[3,8,5,128]{3,2,1,0:T(8,128)S(1)}, f32[3,8,5,128]{3,2,1,0:T(8,128)S(1)}, u32[]{:S(2)}, u32[]{:S(2)}) collective-permute-start(f32[3,8,5,128]{3,2,1,0:T(8,128)S(1)} %get-tuple-element.55), channel_id=1, source_target_pairs={{0,1},{1,2},{2,3},{3,4},{4,5},{5,6},{6,7},{7,8},{8,9},{9,10},{10,1... | collective-permute-start | bytes 184328 | tf_op jit(solution)/shard_map/ppermute | solution.py:30
  138.0 7.7 %collective-permute-start.10 = (f32[1,4,128]{2,1,0:T(4,128)S(1)}, f32[1,4,128]{2,1,0:T(4,128)S(1)}, u32[]{:S(2)}, u32[]{:S(2)}) collective-permute-start(f32[1,4,128]{2,1,0:T(4,128)S(1)} %get-tuple-element.58), channel_id=1, source_target_pairs={{0,1},{1,2},{2,3},{3,4},{4,5},{5,6},{6,7},{7,8},{8,9},{9,10},{10,1... | collective-permute-start | bytes 6152 | tf_op jit(solution)/shard_map/ppermute | solution.py:30
  140.0 7.0 %collective-permute-start.11 = (f32[1,4,128]{2,1,0:T(4,128)S(1)}, f32[1,4,128]{2,1,0:T(4,128)S(1)}, u32[]{:S(2)}, u32[]{:S(2)}) collective-permute-start(f32[1,4,128]{2,1,0:T(4,128)S(1)} %get-tuple-element.57), channel_id=1, source_target_pairs={{1,0},{2,1},{3,2},{4,3},{5,4},{6,5},{7,6},{8,7},{9,8},{10,9},{11,1... | collective-permute-start | bytes 6152 | tf_op jit(solution)/shard_map/ppermute | solution.py:31
where the time goes:
time: 148 us
  starting transfers between devices  48 us (32%)
  blocking collectives  34.3 us (23%)
  local copies, waits for them, and re-layouts  33.8 us (23%)
  waiting for transfers between devices  14.4 us (10%)
  other arithmetic  13.6 us (9%)
  matrix products  2.44 us (2%)
    ppermute x6, starting transfers between devices, extended(): after = lax.ppermute(initial, axis, down)  34.3 us
    all_gather x1, blocking collectives, on_device(): gathered = lax.all_gather(bundled_pieces, 'narrow', axis=1, tiled=True)  34.3 us
    ppermute x6, starting transfers between devices, extended(): before = lax.ppermute(last, axis, up)  13.7 us
    broadcast_in_dim x4, local copies, waits for them, and re-layouts, refine_onto_grid(): jnp.broadcast_to(coarse[:, None, :, None, :, None], (rough_sheets, COARSE...  12.5 us
    ppermute x6, waiting for transfers between devices, extended(): before = lax.ppermute(last, axis, up)  12.1 us
    mul x2, local copies, waits for them, and re-layouts, flux_of(): rotated_u = cosine * grad_x + sine_t * grad_y  10.5 us
    reduce_sum x1, local copies, waits for them, and re-layouts, restrict(): return jnp.mean(blocks, axis=(1, 3, 5))  5.65 us
    another operation x2, other arithmetic, on_device(): state_new = jnp.stack([order_parameter_next, alloy_next])  3.35 us
  transfers between devices with their start and end apart: 12, of which 6 were waited for; matrix products, arithmetic and copies ran while one was open for 19% of the time, Pallas kernels for 0%

commit v1 on v0

v1 whole, which is shorter than its diff:
```python
import functools

import jax
import jax.numpy as jnp
import numpy as np
from jax import lax
from jax.experimental import pallas as pl
from jax.experimental.pallas import tpu as pltpu
from jax.sharding import PartitionSpec as P

F32 = jnp.float32
HI = lax.Precision.HIGHEST
NNAR, NWIDE = 8, 32
NPL, BX, NY = 4, 64, 512
CX, CY = 16, 128
SUBX = 24
SIGMA, KBAR = 0.05, 0.75
DT = 0.15
VMEM = pl.BlockSpec(memory_space=pltpu.VMEM)
HBM = pl.BlockSpec(memory_space=pl.ANY)


def sds(*shape):
    return jax.ShapeDtypeStruct(shape, F32)


def params():
    return pltpu.CompilerParams(vmem_limit_bytes=32 * 1024 * 1024)


def sine(points):
    k = np.arange(1, points + 1)
    return np.sqrt(2.0 / (points + 1)) * np.sin(np.pi * np.outer(k, k) / (points + 1))


def level(points):
    return 2.0 - 2.0 * np.cos(np.pi * np.arange(1, points + 1) / (points + 1))


SZ, SY = sine(8), sine(CY)
SPREAD_Y = np.kron(np.eye(CY), np.ones((1, 4)))
SUM_X = np.kron(np.eye(CX), np.ones((1, 4)))
MEAN_Y = SPREAD_Y.T @ SY / 64.0
SZ_ROWS = np.repeat(SZ[:, :, None], CY, 2)


def elimination():
    diag = SIGMA + KBAR * (level(8)[:, None] + level(CY)[None, :] + 2.0)
    inv = [1.0 / diag]
    for _ in range(SUBX - 1):
        inv.append(1.0 / (diag - KBAR * KBAR * inv[-1]))
    return np.stack(inv)


INVERSE = elimination()


def wide_ring(k):
    return [(i, (i + k) % NWIDE) for i in range(NWIDE)]


PAIR_A = [(i, i ^ 1) for i in range(NNAR)]
PAIR_B = [(i, (((i + 1) ^ 1) - 1) % NNAR) for i in range(NNAR)]
CORES = [(i, i ^ 1) for i in range(NWIDE)]


def lanes(v):
    return lax.broadcasted_iota(jnp.int32, v.shape, v.ndim - 1)


def rows_of(v):
    return lax.broadcasted_iota(jnp.int32, v.shape, v.ndim - 2)


def y_up(v):
    n = v.shape[-1]
    return jnp.where(lanes(v) == n - 1, 0.0, pltpu.roll(v, n - 1, v.ndim - 1))


def y_down(v):
    return jnp.where(lanes(v) == 0, 0.0, pltpu.roll(v, 1, v.ndim - 1))


def x_up(v, after):
    return pltpu.roll(jnp.where(rows_of(v) == 0, after, v), 7, v.ndim - 2)


def x_down(v, before):
    return pltpu.roll(jnp.where(rows_of(v) == 7, before, v), 1, v.ndim - 2)


def inverse(v):
    guess = pl.reciprocal(v, approx=True)
    guess = guess * (2.0 - v * guess)
    return guess * (2.0 - v * guess)


def weigh(gz, gx, gy, c2, s2):
    q0, a, b = gz * gz, gx * gx, gy * gy
    r = a + b
    uv = s2 * (b - a) + c2 * (gx * gy)
    num = q0 * q0 + r * r - 2.0 * (uv * uv)
    over = inverse(q0 + r + 1.0)
    return 0.55 + 0.6 * (num * (over * over))


def flag(cond):
    return jnp.where(cond, 1.0, 0.0).astype(F32)


def dot(a, b):
    return jnp.dot(a, b, precision=HI, preferred_element_type=F32)


def pack_kernel(state, ids, frozen, temp, angles, za, zb, xr, xl, coarse):
    n = lax.axis_index("narrow")
    even = lax.rem(n, 2) == 0
    for ref, top in ((za, even), (zb, jnp.logical_not(even))):
        first = jnp.where(top, 2, 0)
        last = jnp.where(top, 3, 0)
        ref[0:2] = state[0, pl.ds(first, 2)]
        ref[2] = state[1, last]
    table = jnp.broadcast_to(angles[...], (CX, CY))
    cos_t, sin_t = jnp.cos(table), jnp.sin(table)
    ident = ids[0]
    c = jnp.take_along_axis(cos_t, ident, axis=1)
    s = jnp.take_along_axis(sin_t, ident, axis=1)
    coarse[0] = c * c - s * s
    coarse[1] = c * s
    coarse[2] = temp[0]
    coarse[3] = -0.5 * frozen[0].astype(F32)
    for ref, edge, inner, cell in ((xr, BX - 1, BX - 2, CX - 1), (xl, 0, 1, 0)):
        for z in range(NPL):
            ref[z : z + 1] = state[0, z, edge : edge + 1]
            ref[4 + z : 5 + z] = state[0, z, inner : inner + 1]
            ref[8 + z : 9 + z] = state[1, z, edge : edge + 1]
        for k in range(4):
            ref[12:13, k * CY : (k + 1) * CY] = coarse[k, cell : cell + 1]
        ref[13:16] = jnp.zeros((3, NY), F32)


def corner_kernel(coarse, left, right, ca, cb):
    n = lax.axis_index("narrow")
    even = lax.rem(n, 2) == 0
    for ref, top in ((ca, even), (cb, jnp.logical_not(even))):
        pick = jnp.where(top, 1.0, 0.0).astype(F32)
        for row, side in ((0, left), (1, right)):
            ref[row : row + 1] = jnp.where(pick > 0.5, side[3:4], side[0:1])
        ref[2:8] = jnp.zeros((6, NY), F32)
        for k in range(4):
            ref[8:24, k * CY : (k + 1) * CY] = coarse[k]


def widen(ref, at, rough):
    for k in range(CX):
        ref[at, 4 * k : 4 * k + 4] = jnp.broadcast_to(rough[k : k + 1], (4, NY))


def prepare_kernel(state, coarse, left, right, spread_y, own, fine, rims):
    w = lax.axis_index("wide")
    has_left, has_right = flag(w > 0), flag(w < NWIDE - 1)
    for z in range(NPL):
        own[z, 8 : 8 + BX] = state[0, z]
        own[z, 7:8] = left[z : z + 1] * has_left
        own[z, 8 + BX : 9 + BX] = right[z : z + 1] * has_right
    for k in range(3):
        widen(fine, k, dot(coarse[k], spread_y[...]))
    rows = [side[12:13, k * CY : (k + 1) * CY] for side in (left, right) for k in (0, 1)]
    rims[...] = dot(jnp.concatenate(rows + rows, 0), spread_y[...])


def edge_kernel(coarse, left, right, ca, cb, spread_y, sy, sides, base):
    n, w = lax.axis_index("narrow"), lax.axis_index("wide")
    even = lax.rem(n, 2) == 0
    has_left, has_right = flag(w > 0), flag(w < NWIDE - 1)
    has_low, has_high = flag(n > 0), flag(n < NNAR - 1)
    low = jnp.where(even, cb[8:24], ca[8:24])
    high = jnp.where(even, ca[8:24], cb[8:24])
    for at, message in ((0, low), (2, high)):
        for k in range(2):
            widen(sides, at + k, dot(message[:, k * CY : (k + 1) * CY], spread_y[...]))
    t, e = coarse[2], coarse[3]
    near = []
    for message, there in ((low, has_low), (high, has_high)):
        near.append((message[:, 2 * CY : 3 * CY] * there, message[:, 3 * CY :] * there))
    row = rows_of(t)
    down, up = [], []
    for k, own in ((2, t), (3, e)):
        before = left[12:13, k * CY : (k + 1) * CY] * has_left
        after = right[12:13, k * CY : (k + 1) * CY] * has_right
        down.append(jnp.where(row == 0, before, pltpu.roll(own, 1, 0)))
        up.append(jnp.where(row == CX - 1, after, pltpu.roll(own, CX - 1, 0)))
    near += [tuple(down), tuple(up), (y_up(t), y_up(e)), (y_down(t), y_down(e))]
    total = jnp.zeros_like(t)
    for tn, en in near:
        total = total + (1.0 + 0.5 * (e + en)) * (tn - t)
    base[...] = dot(total, sy[...])


def phase_kernel(
    state, own, fine, rims, sides, left, right, za, zb, ca, cb, base, sum_x, mean_y,
    fresh, spectral,
    halo, fx, fz, known, scale, change,
):
    n, w = lax.axis_index("narrow"), lax.axis_index("wide")
    even = lax.rem(n, 2) == 0
    has_left, has_right = flag(w > 0), flag(w < NWIDE - 1)
    has_low, has_high = flag(n > 0), flag(n < NNAR - 1)
    for message, corner, at, there in (
        (za, ca, jnp.where(even, 2, 0), jnp.where(even, has_high, has_low)),
        (zb, cb, jnp.where(even, 0, 2), jnp.where(even, has_low, has_high)),
    ):
        for k in range(2):
            halo[at + k, 8 : 8 + BX] = message[k] * there
            halo[at + k, 7:8] = corner[0:1] * (there * has_left)
            halo[at + k, 8 + BX : 9 + BX] = corner[1:2] * (there * has_right)
    planes = [(halo, 0), (halo, 1), (own, 0), (own, 1), (own, 2), (own, 3), (halo, 2), (halo, 3)]

    def get(k, rows):
        ref, z = planes[k]
        return ref[z, rows]

    def fluxes(c, carry):
        r0 = pl.multiple_of(c * 8, 8)
        here, at, after = pl.ds(r0, 8), pl.ds(r0 + 8, 8), pl.ds(r0 + 16, 8)
        for zz in range(6):
            v = get(zz + 1, at)
            gz = 0.5 * (get(zz + 2, at) - get(zz, at))
            gx = 0.5 * (x_up(v, get(zz + 1, after)) - x_down(v, get(zz + 1, here)))
            gy = 0.5 * (y_up(v) - y_down(v))
            if zz in (0, 5):
                k = 0 if zz == 0 else 2
                an = weigh(gz, gx, gy, sides[k, here], sides[k + 1, here])
                fz[zz, here] = (has_low if zz == 0 else has_high) * (an * an * gz)
                continue
            an = weigh(gz, gx, gy, fine[0, here], fine[1, here])
            wt = an * an
            fz[zz, here] = wt * gz
            fx[zz - 1, at] = wt * gx
            fy = wt * gy
            m = 1.0 - v * v
            drive = m * (v - 1.5 * (state[1, zz - 1, here] + fine[2, here]) * m)
            known[zz - 1, here] = 0.5 * (y_up(fy) - y_down(fy)) + drive
            scale[zz - 1, here] = DT * inverse(wt)
        return carry

    lax.fori_loop(0, BX // 8, fluxes, 0)

    def column(pick):
        return jnp.concatenate([pick(z, s) for s in (0, 1) for z in range(NPL)], 0)

    rim = (slice(7, 8), slice(8 + BX, 9 + BX))
    centre = column(lambda z, s: get(z + 2, rim[s]))
    below = column(lambda z, s: get(z + 1, rim[s]))
    above = column(lambda z, s: get(z + 3, rim[s]))
    x_hi = column(lambda z, s: right[4 + z : 5 + z] if s else own[z, 8:9])
    x_lo = column(lambda z, s: own[z, 7 + BX : 8 + BX] if s else left[4 + z : 5 + z])
    first = rows_of(centre) < NPL
    c2 = jnp.where(first, rims[0:1], rims[2:3])
    s2 = jnp.where(first, rims[1:2], rims[3:4])
    gx = 0.5 * (x_hi - x_lo)
    an = weigh(0.5 * (above - below), gx, 0.5 * (y_up(centre) - y_down(centre)), c2, s2)
    rim_flux = jnp.where(first, has_left, has_right) * (an * an * gx)
    for z in range(NPL):
        fx[z, 7:8] = rim_flux[z : z + 1]
        fx[z, 8 + BX : 9 + BX] = rim_flux[NPL + z : NPL + z + 1]

    def step(c, carry):
        r0 = pl.multiple_of(c * 8, 8)
        here, at, after = pl.ds(r0, 8), pl.ds(r0 + 8, 8), pl.ds(r0 + 16, 8)
        total = jnp.zeros((8, NY), F32)
        for z in range(NPL):
            p, f = own[z, at], fx[z, at]
            spread = (
                known[z, here]
                + 0.5 * (fz[z + 2, here] - fz[z, here])
                + 0.5 * (x_up(f, fx[z, after]) - x_down(f, fx[z, here]))
            )
            rise = scale[z, here] * spread
            fresh[z, here] = p + rise
            total = total + rise
        change[here] = total
        return carry

    lax.fori_loop(0, BX // 8, step, 0)
    spectral[...] = base[...] + dot(dot(sum_x[...], change[...]), mean_y[...])


def solute_kernel(state, own, left, right, za, zb, fresh, out, sown):
    n, w = lax.axis_index("narrow"), lax.axis_index("wide")
    even = lax.rem(n, 2) == 0
    has_left, has_right = flag(w > 0), flag(w < NWIDE - 1)
    has_low, has_high = flag(n > 0), flag(n < NNAR - 1)
    for z in range(NPL):
        sown[z, 8 : 8 + BX] = state[1, z]
        sown[z, 7:8] = left[8 + z : 9 + z] * has_left
        sown[z, 8 + BX : 9 + BX] = right[8 + z : 9 + z] * has_right

    def step(c, carry):
        r0 = pl.multiple_of(c * 8, 8)
        here, at, after = pl.ds(r0, 8), pl.ds(r0 + 8, 8), pl.ds(r0 + 16, 8)

        def outer(k_low, k_high, high):
            if high:
                return has_high * jnp.where(even, za[k_high, here], zb[k_high, here])
            return has_low * jnp.where(even, zb[k_low, here], za[k_low, here])

        ps = [outer(1, 0, False)] + [own[z, at] for z in range(NPL)] + [outer(1, 0, True)]
        ss = [outer(2, 2, False)] + [sown[z, at] for z in range(NPL)] + [outer(2, 2, True)]
        for z in range(NPL):
            p, s = ps[z + 1], ss[z + 1]
            q = 0.55 - 0.25 * p
            near = [
                (ps[z], ss[z]),
                (ps[z + 2], ss[z + 2]),
                (x_up(p, own[z, after]), x_up(s, sown[z, after])),
                (x_down(p, own[z, here]), x_down(s, sown[z, here])),
                (y_up(p), y_up(s)),
                (y_down(p), y_down(s)),
            ]
            total = jnp.zeros_like(p)
            for pn, sn in near:
                total = total + (q - 0.25 * pn) * (sn - s)
            grown = fresh[z, here]
            out[0, z, here] = grown
            out[1, z, here] = s + DT * total + (0.5 + 0.425 * s) * (grown - p)
        return carry

    lax.fori_loop(0, BX // 8, step, 0)


def window_kernel(before, here, after, out):
    w = lax.axis_index("wide")
    core, chip = lax.rem(w, 2), lax.div(w, 2)
    has_before, has_after = flag(chip > 0), flag(chip < NWIDE // 2 - 1)

    def put(first):
        view = [
            before[first:32] * has_before,
            here[...],
            after[0 : first - 8] * has_after,
        ]
        for m in range(NNAR):
            at = 0
            for part in view:
                out[m, at : at + part.shape[0]] = part
                at += part.shape[0]

    @pl.when(core == 0)
    def _():
        put(12)

    @pl.when(core == 1)
    def _():
        put(28)


def solve_kernel(planes, temp, inv, sz_rows, sy, out, modes, rows):
    n, w = lax.axis_index("narrow"), lax.axis_index("wide")
    has_left, has_right = flag(w > 0), flag(w < NWIDE - 1)
    values = [planes[m] for m in range(NNAR)]
    for k in range(NNAR):
        total = float(SZ[k, 0]) * values[0]
        for m in range(1, NNAR):
            total = total + float(SZ[k, m]) * values[m]
        modes[k * 56 : (k + 1) * 56] = total
    f = [modes[pl.ds(j, 8, stride=56), :] for j in range(56)]
    inv_of = [inv[i] for i in range(SUBX)]
    link = [KBAR * v for v in inv_of]

    def solve(order, keep):
        h = [inv_of[0] * f[order[0]]]
        for i in range(1, SUBX):
            h.append(inv_of[i] * f[order[i]] + link[i] * h[-1])
        x = h[-1]
        found = {order[-1]: x}
        for i in range(SUBX - 2, -1, -1):
            if order[i] not in keep:
                break
            x = h[i] + link[i] * x
            found[order[i]] = x
        return found

    mine = solve(list(range(16, 40)), set(range(20, 40)))
    lower = solve(list(range(0, 24)), set(range(20, 24)))
    upper = solve(list(range(55, 31, -1)), set(range(32, 36)))
    weight = sz_rows[n]
    for j in range(CX):
        x = mine[20 + j]
        if 20 + j in lower:
            x = x + has_left * lower[20 + j]
        if 20 + j in upper:
            x = x + has_right * upper[20 + j]
        rows[j : j + 1] = jnp.sum(x * weight, axis=0, keepdims=True)
    out[0] = temp[0] + dot(rows[...], sy[...])


def kernel(body, outs, scratch=(), cost=0):
    many = isinstance(outs, (list, tuple))

    def call(*args):
        return pl.pallas_call(
            body,
            out_shape=outs,
            in_specs=[VMEM] * len(args),
            out_specs=[VMEM] * len(outs) if many else VMEM,
            scratch_shapes=list(scratch),
            compiler_params=params(),
            cost_estimate=pl.CostEstimate(flops=cost, bytes_accessed=0, transcendentals=0),
            name=body.__name__,
        )(*args)

    return call


def on_device(state, ids, frozen, temp, angles):
    spread_y = jnp.asarray(SPREAD_Y, F32)
    sy = jnp.asarray(SY, F32)
    table = jnp.pad(angles, (0, CY - angles.shape[0])).reshape(1, CY)
    send_a, send_b, to_right, to_left, coarse = kernel(
        pack_kernel, [sds(3, BX, NY)] * 2 + [sds(16, NY)] * 2 + [sds(4, CX, CY)]
    )(state, ids, frozen, temp, table)
    za = lax.ppermute(send_a, "narrow", PAIR_A)
    zb = lax.ppermute(send_b, "narrow", PAIR_B)
    left = lax.ppermute(to_right, "wide", wide_ring(1))
    right = lax.ppermute(to_left, "wide", wide_ring(-1))
    corner_a, corner_b = kernel(corner_kernel, [sds(24, NY)] * 2)(coarse, left, right)
    ca = lax.ppermute(corner_a, "narrow", PAIR_A)
    cb = lax.ppermute(corner_b, "narrow", PAIR_B)
    own, fine, rims = kernel(
        prepare_kernel, [sds(NPL, BX + 16, NY), sds(3, BX, NY), sds(8, NY)]
    )(state, coarse, left, right, spread_y)
    sides, base = kernel(edge_kernel, [sds(4, BX, NY), sds(CX, CY)])(
        coarse, left, right, ca, cb, spread_y, sy
    )
    fresh, spectral = kernel(
        phase_kernel,
        [sds(NPL, BX, NY), sds(CX, CY)],
        [
            pltpu.VMEM((4, BX + 16, NY), F32),
            pltpu.VMEM((NPL, BX + 16, NY), F32),
            pltpu.VMEM((6, BX, NY), F32),
            pltpu.VMEM((NPL, BX, NY), F32),
            pltpu.VMEM((NPL, BX, NY), F32),
            pltpu.VMEM((BX, NY), F32),
        ],
    )(
        state, own, fine, rims, sides, left, right, za, zb, ca, cb, base,
        jnp.asarray(SUM_X, F32), jnp.asarray(MEAN_Y, F32),
    )
    partner = lax.ppermute(spectral, "wide", CORES)
    core = lax.rem(lax.axis_index("wide"), 2)
    here = jnp.where(
        core == 0,
        jnp.concatenate([spectral, partner], 0),
        jnp.concatenate([partner, spectral], 0),
    )
    before = lax.ppermute(here, "wide", wide_ring(2))
    after = lax.ppermute(here, "wide", wide_ring(-2))
    state_new = kernel(
        solute_kernel, sds(2, NPL, BX, NY), [pltpu.VMEM((NPL, BX + 16, NY), F32)]
    )(state, own, left, right, za, zb, fresh)
    windows = kernel(window_kernel, sds(NNAR, 56, CY))(before, here, after)
    planes = lax.all_to_all(windows, "narrow", 0, 0)
    adjusted = kernel(
        solve_kernel,
        sds(1, CX, CY),
        [pltpu.VMEM((NNAR * 56, CY), F32), pltpu.VMEM((CX, CY), F32)],
    )(planes, temp, jnp.asarray(INVERSE, F32), jnp.asarray(SZ_ROWS, F32), sy)
    return state_new, adjusted


def solution(mesh):
    return jax.shard_map(
        on_device,
        mesh=mesh,
        in_specs=(
            P(None, "narrow", "wide", None),
            P("narrow", "wide", None),
            P("narrow", "wide", None),
            P("narrow", "wide", None),
            P(),
        ),
        out_specs=(P(None, "narrow", "wide", None), P("narrow", "wide", None)),
        check_vma=False,
    )
```

time: 148 us -> 52 us (0.35)
  the two profiles are of different devices: /device:TPU:24 before, /device:TPU:96 now
where the time goes in v1:
time: 52 us; the launch traced here: 51.6 us
  starting transfers between devices  18.5 us (36%)
  waiting for transfers between devices  18.5 us (36%)
  Pallas kernels  8.32 us (16%)
  local copies, waits for them, and re-layouts  5.61 us (11%)
  between operations  0.73 us (1%)
    pallas_call x8, Pallas kernels, call(): pl.pallas_call(body, out_shape=outs, in_specs=[VMEM] * len(args), out_spe...  8.32 us
    all_to_all x1, waiting for transfers between devices, on_device(): planes = lax.all_to_all(windows, 'narrow', 0, 0)  6.38 us
    unnamed x24, local copies, waits for them, and re-layouts  4.95 us
    ppermute x1, starting transfers between devices, on_device(): zb = lax.ppermute(send_b, 'narrow', PAIR_B)  4.73 us
    all_to_all x1, starting transfers between devices, on_device(): planes = lax.all_to_all(windows, 'narrow', 0, 0)  4.05 us
    ppermute x1, waiting for transfers between devices, on_device(): cb = lax.ppermute(corner_b, 'narrow', PAIR_B)  3.71 us
    ppermute x1, starting transfers between devices, on_device(): partner = lax.ppermute(spectral, 'wide', CORES)  3.08 us
    ppermute x1, waiting for transfers between devices, on_device(): after = lax.ppermute(here, 'wide', wide_ring(-2))  2.31 us
  transfers between devices with their start and end apart: 10, of which 8 were waited for; matrix products, arithmetic and copies ran while one was open for 0% of the time, Pallas kernels for 7%

profile of v1, /device:TPU:96, one launch (start us, length us, event | category | flops | bytes accessed | tf_op | source)
XLA Modules:
  0.0 51.6 jit_solution(6774235150745947565)
XLA Ops:
  0.6 0.7 %pad_bitcast_fusion.angles = f32[1,128]{1,0:T(1,128)S(1)} fusion(f32[64]{0:T(128)} %param.15), kind=kLoop, calls=%fused_computation.1 | loop fusion | bytes 768 | tf_op jit(solution)/shard_map/reshape | solution.py:419
  1.3 1.2 %copy-done = f32[2,4,64,512]{3,2,1,0:T(8,128)S(1)} copy-done((f32[2,4,64,512]{3,2,1,0:T(8,128)S(1)}, f32[2,4,64,512]{3,2,1,0:T(8,128)}, u32[]{:S(2)}) %copy-start) | copy-done | bytes 1048600
  2.5 0.7 %copy-done.6 = f32[1,16,128]{2,1,0:T(8,128)S(1)} copy-done((f32[1,16,128]{2,1,0:T(8,128)S(1)}, f32[1,16,128]{2,1,0:T(8,128)}, u32[]{:S(2)}) %copy-start.6) | copy-done | bytes 8216
  3.2 0.7 %copy-done.9 = s32[1,16,128]{2,1,0:T(8,128)S(1)} copy-done((s32[1,16,128]{2,1,0:T(8,128)S(1)}, s32[1,16,128]{2,1,0:T(8,128)}, u32[]{:S(2)}) %copy-start.9) | copy-done | bytes 8216
  3.9 0.7 %copy-done.10 = s32[1,16,128]{2,1,0:T(8,128)S(1)} copy-done((s32[1,16,128]{2,1,0:T(8,128)S(1)}, s32[1,16,128]{2,1,0:T(8,128)}, u32[]{:S(2)}) %copy-start.10) | copy-done | bytes 8216
  4.6 0.1 pack_kernel.1
  4.7 1.5 %collective-permute-start.2 = (f32[3,64,512]{2,1,0:T(8,128)S(1)}, f32[3,64,512]{2,1,0:T(8,128)S(1)}, u32[]{:S(2)}, u32[]{:S(2)}) collective-permute-start(f32[3,64,512]{2,1,0:T(8,128)S(1)} %get-tuple-element.20), channel_id=1, source_target_pairs={{0,32},{32,0},{64,96},{96,64},{128,160},{160,128},{192,224},{224,1... | collective-permute-start | bytes 1179656 | tf_op jit(solution)/shard_map/ppermute | solution.py:423
  6.3 4.7 %collective-permute-start.3 = (f32[3,64,512]{2,1,0:T(8,128)S(1)}, f32[3,64,512]{2,1,0:T(8,128)S(1)}, u32[]{:S(2)}, u32[]{:S(2)}) collective-permute-start(f32[3,64,512]{2,1,0:T(8,128)S(1)} %get-tuple-element.21), channel_id=1, source_target_pairs={{0,224},{32,64},{64,32},{96,128},{128,96},{160,192},{192,160},{224... | collective-permute-start | bytes 1179656 | tf_op jit(solution)/shard_map/ppermute | solution.py:424
  11.0 1.7 %collective-permute-start.1 = (f32[16,512]{1,0:T(8,128)S(1)}, f32[16,512]{1,0:T(8,128)S(1)}, u32[]{:S(2)}, u32[]{:S(2)}) collective-permute-start(f32[16,512]{1,0:T(8,128)S(1)} %get-tuple-element.18), channel_id=1, source_target_pairs={{0,31},{1,0},{2,1},{3,2},{4,3},{5,4},{6,5},{7,6},{8,7},{9,8},{10,9... | collective-permute-start | bytes 98312 | tf_op jit(solution)/shard_map/ppermute | solution.py:426
  12.8 1.6 %collective-permute-done.left = f32[16,512]{1,0:T(8,128)S(1)} collective-permute-done((f32[16,512]{1,0:T(8,128)S(1)}, f32[16,512]{1,0:T(8,128)S(1)}, u32[]{:S(2)}, u32[]{:S(2)}) %collective-permute-start) | collective-permute-done | bytes 32800 | tf_op jit(solution)/shard_map/ppermute | solution.py:425
  14.3 0.6 %collective-permute-done.1.right = f32[16,512]{1,0:T(8,128)S(1)} collective-permute-done((f32[16,512]{1,0:T(8,128)S(1)}, f32[16,512]{1,0:T(8,128)S(1)}, u32[]{:S(2)}, u32[]{:S(2)}) %collective-permute-start.1) | collective-permute-done | bytes 32800 | tf_op jit(solution)/shard_map/ppermute | solution.py:426
  15.0 0.1 collective-permute-start.4
  15.1 1.2 %collective-permute-start.5 = (f32[24,512]{1,0:T(8,128)S(1)}, f32[24,512]{1,0:T(8,128)S(1)}, u32[]{:S(2)}, u32[]{:S(2)}) collective-permute-start(f32[24,512]{1,0:T(8,128)S(1)} %get-tuple-element.25), channel_id=1, source_target_pairs={{0,224},{32,64},{64,32},{96,128},{128,96},{160,192},{192,160},{224... | collective-permute-start | bytes 147464 | tf_op jit(solution)/shard_map/ppermute | solution.py:429
  16.3 0.9 %copy-done.2 = f32[128,512]{1,0:T(8,128)S(1)} copy-done((f32[128,512]{1,0:T(8,128)S(1)}, f32[128,512]{1,0:T(8,128)}, u32[]{:S(2)}) %copy-start.2) | copy-done | bytes 262168
  17.2 0.6 %prepare_kernel.1 = (f32[4,80,512]{2,1,0:T(8,128)S(1)}, f32[3,64,512]{2,1,0:T(8,128)S(1)}, f32[8,512]{1,0:T(8,128)S(1)}) custom-call(f32[2,4,64,512]{3,2,1,0:T(8,128)S(1)} %copy-done.1, f32[4,16,128]{2,1,0:T(8,128)S(1)} %get-tuple-element.16.coarse, f32[16,512]{1,0:T(8,128)S(1)} %collective-permute-done.left, f32[16,512]{1,0:T(8,128)S(1)} %collective-permute-done.1.right, ...), custom_call_target="tpu_custom_call" | custom-call | tf_op jit(solution)/shard_map/prepare_kernel/pallas_call | solution.py:402
  17.8 1.3 %collective-permute-done.4.ca = f32[24,512]{1,0:T(8,128)S(1)} collective-permute-done((f32[24,512]{1,0:T(8,128)S(1)}, f32[24,512]{1,0:T(8,128)S(1)}, u32[]{:S(2)}, u32[]{:S(2)}) %collective-permute-start.4) | collective-permute-done | bytes 49184 | tf_op jit(solution)/shard_map/ppermute | solution.py:428
  19.1 3.7 %collective-permute-done.5.cb = f32[24,512]{1,0:T(8,128)S(1)} collective-permute-done((f32[24,512]{1,0:T(8,128)S(1)}, f32[24,512]{1,0:T(8,128)S(1)}, u32[]{:S(2)}, u32[]{:S(2)}) %collective-permute-start.5) | collective-permute-done | bytes 49184 | tf_op jit(solution)/shard_map/ppermute | solution.py:429
  22.9 0.6 %edge_kernel.1 = (f32[4,64,512]{2,1,0:T(8,128)S(1)}, f32[16,128]{1,0:T(8,128)S(1)}) custom-call(f32[4,16,128]{2,1,0:T(8,128)S(1)} %get-tuple-element.16.coarse, f32[16,512]{1,0:T(8,128)S(1)} %collective-permute-done.left, f32[16,512]{1,0:T(8,128)S(1)} %collective-permute-done.1.right, f32[24,512]{1,0:T(8,128)S(1)} %collective-permute-done.4.ca, ...), custom_call_target="tpu_custom_call" | custom-call | tf_op jit(solution)/shard_map/edge_kernel/pallas_call | solution.py:402
  23.5 0.0 copy-start.11
  23.5 0.7 %copy-done.11 = f32[16,64]{1,0:T(8,128)S(1)} copy-done((f32[16,64]{1,0:T(8,128)S(1)}, f32[16,64]{1,0:T(8,128)}, u32[]{:S(2)}) %copy-start.11) | copy-done | bytes 4120
  24.2 3.0 %phase_kernel.1 = (f32[4,64,512]{2,1,0:T(8,128)S(1)}, f32[16,128]{1,0:T(8,128)S(1)}) custom-call(f32[2,4,64,512]{3,2,1,0:T(8,128)S(1)} %copy-done.1, f32[4,80,512]{2,1,0:T(8,128)S(1)} %get-tuple-element.19.own, f32[3,64,512]{2,1,0:T(8,128)S(1)} %get-tuple-element.22.fine, f32[8,512]{1,0:T(8,128)S(1)} %get-tuple-element.23.rims, ...), custom_call_target="tpu_custom_call" | custom-call | tf_op jit(solution)/shard_map/phase_kernel/pallas_call | solution.py:402
  27.2 3.1 %collective-permute-start.6 = (f32[16,128]{1,0:T(8,128)S(1)}, f32[16,128]{1,0:T(8,128)S(1)}, u32[]{:S(2)}, u32[]{:S(2)}) collective-permute-start(f32[16,128]{1,0:T(8,128)S(1)} %get-tuple-element.29), channel_id=1, source_target_pairs={{0,1},{1,0},{2,3},{3,2},{4,5},{5,4},{6,7},{7,6},{8,9},{9,8},{10,11... | collective-permute-start | bytes 24584 | tf_op jit(solution)/shard_map/ppermute | solution.py:451
  30.3 0.8 %collective-permute-done.6 = f32[16,128]{1,0:T(8,128)S(1)} collective-permute-done((f32[16,128]{1,0:T(8,128)S(1)}, f32[16,128]{1,0:T(8,128)S(1)}, u32[]{:S(2)}, u32[]{:S(2)}) %collective-permute-start.6) | collective-permute-done | bytes 8224 | tf_op jit(solution)/shard_map/ppermute | solution.py:451
  31.1 1.1 %collective-permute-start.7 = (f32[32,128]{1,0:T(8,128)S(1)}, f32[32,128]{1,0:T(8,128)S(1)}, u32[]{:S(2)}, u32[]{:S(2)}) collective-permute-start(f32[32,128]{1,0:T(8,128)S(1)} %maximum_select_fusion.here), channel_id=1, source_target_pairs={{0,2},{1,3},{2,4},{3,5},{4,6},{5,7},{6,8},{7,9},{8,10},{9,11},{10,... | collective-permute-start | bytes 49160 | tf_op jit(solution)/shard_map/ppermute | solution.py:458
  32.2 0.9 %collective-permute-start.8 = (f32[32,128]{1,0:T(8,128)S(1)}, f32[32,128]{1,0:T(8,128)S(1)}, u32[]{:S(2)}, u32[]{:S(2)}) collective-permute-start(f32[32,128]{1,0:T(8,128)S(1)} %maximum_select_fusion.here), channel_id=1, source_target_pairs={{0,30},{1,31},{2,0},{3,1},{4,2},{5,3},{6,4},{7,5},{8,6},{9,7},{10,... | collective-permute-start | bytes 49160 | tf_op jit(solution)/shard_map/ppermute | solution.py:459
  33.2 1.7 %collective-permute-done.7.before = f32[32,128]{1,0:T(8,128)S(1)} collective-permute-done((f32[32,128]{1,0:T(8,128)S(1)}, f32[32,128]{1,0:T(8,128)S(1)}, u32[]{:S(2)}, u32[]{:S(2)}) %collective-permute-start.7) | collective-permute-done | bytes 16416 | tf_op jit(solution)/shard_map/ppermute | solution.py:458
  34.9 2.3 %collective-permute-done.8.after = f32[32,128]{1,0:T(8,128)S(1)} collective-permute-done((f32[32,128]{1,0:T(8,128)S(1)}, f32[32,128]{1,0:T(8,128)S(1)}, u32[]{:S(2)}, u32[]{:S(2)}) %collective-permute-start.8) | collective-permute-done | bytes 16416 | tf_op jit(solution)/shard_map/ppermute | solution.py:459
  37.2 0.7 %window_kernel.1 = f32[8,56,128]{2,1,0:T(8,128)} custom-call(f32[32,128]{1,0:T(8,128)S(1)} %collective-permute-done.7.before, f32[32,128]{1,0:T(8,128)S(1)} %maximum_select_fusion.here, f32[32,128]{1,0:T(8,128)S(1)} %collective-permute-done.8.after), custom_call_target="tpu_custom_call" | custom-call | tf_op jit(solution)/shard_map/window_kernel/pallas_call | solution.py:402
  37.9 4.0 %all-to-all-start = ((f32[8,56,128]{2,1,0:T(8,128)}), f32[8,56,128]{2,1,0:T(8,128)S(1)}, u32[]{:S(2)}, u32[]{:S(2)}) async-start(f32[8,56,128]{2,1,0:T(8,128)} %window_kernel.1), calls=%async_computation | async-start | bytes 458752 | tf_op jit(solution)/shard_map/all_to_all | solution.py:464
  42.0 2.2 %solute_kernel.1 = f32[2,4,64,512]{3,2,1,0:T(8,128)} custom-call(f32[2,4,64,512]{3,2,1,0:T(8,128)S(1)} %copy-done.1, f32[4,80,512]{2,1,0:T(8,128)S(1)} %get-tuple-element.19.own, f32[16,512]{1,0:T(8,128)S(1)} %collective-permute-done.left, f32[16,512]{1,0:T(8,128)S(1)} %collective-permute-done.1.right, f32[3,64,512]{2,1,0:T(8,128)S(1)} %collective-permute-done.2.za, ...), custom_call_target="tpu_custom_call" | custom-call | tf_op jit(solution)/shard_map/solute_kernel/pallas_call | solution.py:402
  44.2 6.4 %all-to-all-done.planes = f32[8,56,128]{2,1,0:T(8,128)S(1)} async-done(((f32[8,56,128]{2,1,0:T(8,128)}), f32[8,56,128]{2,1,0:T(8,128)S(1)}, u32[]{:S(2)}, u32[]{:S(2)}) %all-to-all-start) | async-done | bytes 229408 | tf_op jit(solution)/shard_map/all_to_all | solution.py:464
  50.6 1.0 %solve_kernel.1 = f32[1,16,128]{2,1,0:T(8,128)} custom-call(f32[8,56,128]{2,1,0:T(8,128)S(1)} %all-to-all-done.planes, f32[1,16,128]{2,1,0:T(8,128)S(1)} %copy-done.7, f32[24,8,128]{2,1,0:T(8,128)S(1)} %copy-done.5, f32[8,8,128]{2,1,0:T(8,128)S(1)} %copy-done.8, f32[128,128]{1,0:T(8,128)S(1)} %copy-done.3), custom_call_target="tpu_custom_call" | custom-call | tf_op jit(solution)/shard_map/solve_kernel/pallas_call | solution.py:402
  (22 shorter events, 0.1 us)
Async XLA Ops:
  1.3 1.2 %copy-start = (f32[2,4,64,512]{3,2,1,0:T(8,128)S(1)}, f32[2,4,64,512]{3,2,1,0:T(8,128)}, u32[]{:S(2)}) copy-start(f32[2,4,64,512]{3,2,1,0:T(8,128)} %state.7) | copy-start | bytes 3145732
  2.5 0.7 %copy-start.6 = (f32[1,16,128]{2,1,0:T(8,128)S(1)}, f32[1,16,128]{2,1,0:T(8,128)}, u32[]{:S(2)}) copy-start(f32[1,16,128]{2,1,0:T(8,128)} %temp.3) | copy-start | bytes 24580
  3.2 0.7 %copy-start.9 = (s32[1,16,128]{2,1,0:T(8,128)S(1)}, s32[1,16,128]{2,1,0:T(8,128)}, u32[]{:S(2)}) copy-start(s32[1,16,128]{2,1,0:T(8,128)} %ids.1) | copy-start | bytes 24580
  3.9 0.7 %copy-start.10 = (s32[1,16,128]{2,1,0:T(8,128)S(1)}, s32[1,16,128]{2,1,0:T(8,128)}, u32[]{:S(2)}) copy-start(s32[1,16,128]{2,1,0:T(8,128)} %frozen.1) | copy-start | bytes 24580
  4.6 11.7 %copy-start.1 = (f32[2,4,64,512]{3,2,1,0:T(8,128)S(1)}, f32[2,4,64,512]{3,2,1,0:T(8,128)}, u32[]{:S(2)}) copy-start(f32[2,4,64,512]{3,2,1,0:T(8,128)} %state.7) | copy-start | bytes 3145732
  4.7 18.8 %collective-permute-start.2 = (f32[3,64,512]{2,1,0:T(8,128)S(1)}, f32[3,64,512]{2,1,0:T(8,128)S(1)}, u32[]{:S(2)}, u32[]{:S(2)}) collective-permute-start(f32[3,64,512]{2,1,0:T(8,128)S(1)} %get-tuple-element.20), channel_id=1, source_target_pairs={{0,32},{32,0},{64,96},{96,64},{128,160},{160,128},{192,224},{224,1... | collective-permute-start | bytes 1179656 | tf_op jit(solution)/shard_map/ppermute | solution.py:423
  6.3 17.2 %collective-permute-start.3 = (f32[3,64,512]{2,1,0:T(8,128)S(1)}, f32[3,64,512]{2,1,0:T(8,128)S(1)}, u32[]{:S(2)}, u32[]{:S(2)}) collective-permute-start(f32[3,64,512]{2,1,0:T(8,128)S(1)} %get-tuple-element.21), channel_id=1, source_target_pairs={{0,224},{32,64},{64,32},{96,128},{128,96},{160,192},{192,160},{224... | collective-permute-start | bytes 1179656 | tf_op jit(solution)/shard_map/ppermute | solution.py:424
  11.0 3.3 %collective-permute-start = (f32[16,512]{1,0:T(8,128)S(1)}, f32[16,512]{1,0:T(8,128)S(1)}, u32[]{:S(2)}, u32[]{:S(2)}) collective-permute-start(f32[16,512]{1,0:T(8,128)S(1)} %get-tuple-element.17), channel_id=1, source_target_pairs={{0,1},{1,2},{2,3},{3,4},{4,5},{5,6},{6,7},{7,8},{8,9},{9,10},{10,1... | collective-permute-start | bytes 98312 | tf_op jit(solution)/shard_map/ppermute | solution.py:425
  11.0 3.9 %collective-permute-start.1 = (f32[16,512]{1,0:T(8,128)S(1)}, f32[16,512]{1,0:T(8,128)S(1)}, u32[]{:S(2)}, u32[]{:S(2)}) collective-permute-start(f32[16,512]{1,0:T(8,128)S(1)} %get-tuple-element.18), channel_id=1, source_target_pairs={{0,31},{1,0},{2,1},{3,2},{4,3},{5,4},{6,5},{7,6},{8,7},{9,8},{10,9... | collective-permute-start | bytes 98312 | tf_op jit(solution)/shard_map/ppermute | solution.py:426
  15.0 4.2 %collective-permute-start.4 = (f32[24,512]{1,0:T(8,128)S(1)}, f32[24,512]{1,0:T(8,128)S(1)}, u32[]{:S(2)}, u32[]{:S(2)}) collective-permute-start(f32[24,512]{1,0:T(8,128)S(1)} %get-tuple-element.24), channel_id=1, source_target_pairs={{0,32},{32,0},{64,96},{96,64},{128,160},{160,128},{192,224},{224,1... | collective-permute-start | bytes 147464 | tf_op jit(solution)/shard_map/ppermute | solution.py:428
  15.1 7.8 %collective-permute-start.5 = (f32[24,512]{1,0:T(8,128)S(1)}, f32[24,512]{1,0:T(8,128)S(1)}, u32[]{:S(2)}, u32[]{:S(2)}) collective-permute-start(f32[24,512]{1,0:T(8,128)S(1)} %get-tuple-element.25), channel_id=1, source_target_pairs={{0,224},{32,64},{64,32},{96,128},{128,96},{160,192},{192,160},{224... | collective-permute-start | bytes 147464 | tf_op jit(solution)/shard_map/ppermute | solution.py:429
  16.3 1.0 %copy-start.2 = (f32[128,512]{1,0:T(8,128)S(1)}, f32[128,512]{1,0:T(8,128)}, u32[]{:S(2)}) copy-start(f32[128,512]{1,0:T(8,128)} %constant.24.clone.spread_y) | copy-start | bytes 786436
  17.2 5.7 %copy-start.3 = (f32[128,128]{1,0:T(8,128)S(1)}, f32[128,128]{1,0:T(8,128)}, u32[]{:S(2)}) copy-start(f32[128,128]{1,0:T(8,128)} %constant.25.clone.sy) | copy-start | bytes 196612
  17.8 5.7 %copy-start.4 = (f32[512,128]{1,0:T(8,128)S(1)}, f32[512,128]{1,0:T(8,128)}, u32[]{:S(2)}) copy-start(f32[512,128]{1,0:T(8,128)} %constant.27.clone.mean_y) | copy-start | bytes 786436
  23.5 0.7 %copy-start.11 = (f32[16,64]{1,0:T(8,128)S(1)}, f32[16,64]{1,0:T(8,128)}, u32[]{:S(2)}) copy-start(f32[16,64]{1,0:T(8,128)} %constant.26.clone.sum_x) | copy-start | bytes 12292
  27.2 3.9 %collective-permute-start.6 = (f32[16,128]{1,0:T(8,128)S(1)}, f32[16,128]{1,0:T(8,128)S(1)}, u32[]{:S(2)}, u32[]{:S(2)}) collective-permute-start(f32[16,128]{1,0:T(8,128)S(1)} %get-tuple-element.29), channel_id=1, source_target_pairs={{0,1},{1,0},{2,3},{3,2},{4,5},{5,4},{6,7},{7,6},{8,9},{9,8},{10,11... | collective-permute-start | bytes 24584 | tf_op jit(solution)/shard_map/ppermute | solution.py:451
  31.1 3.7 %collective-permute-start.7 = (f32[32,128]{1,0:T(8,128)S(1)}, f32[32,128]{1,0:T(8,128)S(1)}, u32[]{:S(2)}, u32[]{:S(2)}) collective-permute-start(f32[32,128]{1,0:T(8,128)S(1)} %maximum_select_fusion.here), channel_id=1, source_target_pairs={{0,2},{1,3},{2,4},{3,5},{4,6},{5,7},{6,8},{7,9},{8,10},{9,11},{10,... | collective-permute-start | bytes 49160 | tf_op jit(solution)/shard_map/ppermute | solution.py:458
  32.2 4.9 %collective-permute-start.8 = (f32[32,128]{1,0:T(8,128)S(1)}, f32[32,128]{1,0:T(8,128)S(1)}, u32[]{:S(2)}, u32[]{:S(2)}) collective-permute-start(f32[32,128]{1,0:T(8,128)S(1)} %maximum_select_fusion.here), channel_id=1, source_target_pairs={{0,30},{1,31},{2,0},{3,1},{4,2},{5,3},{6,4},{7,5},{8,6},{9,7},{10,... | collective-permute-start | bytes 49160 | tf_op jit(solution)/shard_map/ppermute | solution.py:459
  37.9 12.7 %all-to-all-start = ((f32[8,56,128]{2,1,0:T(8,128)}), f32[8,56,128]{2,1,0:T(8,128)S(1)}, u32[]{:S(2)}, u32[]{:S(2)}) async-start(f32[8,56,128]{2,1,0:T(8,128)} %window_kernel.1), calls=%async_computation | async-start | bytes 458752 | tf_op jit(solution)/shard_map/all_to_all | solution.py:464
  42.0 8.6 %copy-start.5 = (f32[24,8,128]{2,1,0:T(8,128)S(1)}, f32[24,8,128]{2,1,0:T(8,128)}, u32[]{:S(2)}) copy-start(f32[24,8,128]{2,1,0:T(8,128)} %constant.28.clone.inv) | copy-start | bytes 294916
  42.0 8.6 %copy-start.7 = (f32[1,16,128]{2,1,0:T(8,128)S(1)}, f32[1,16,128]{2,1,0:T(8,128)}, u32[]{:S(2)}) copy-start(f32[1,16,128]{2,1,0:T(8,128)} %temp.3) | copy-start | bytes 24580
  42.0 8.6 %copy-start.8 = (f32[8,8,128]{2,1,0:T(8,128)S(1)}, f32[8,8,128]{2,1,0:T(8,128)}, u32[]{:S(2)}) copy-start(f32[8,8,128]{2,1,0:T(8,128)} %constant.29.clone.sz_rows) | copy-start | bytes 98308

commit v2 on v1

v2 whole, which is shorter than its diff:
```python
import functools

import jax
import jax.numpy as jnp
import numpy as np
from jax import lax
from jax.experimental import pallas as pl
from jax.experimental.pallas import tpu as pltpu
from jax.sharding import PartitionSpec as P

F32 = jnp.float32
HI = lax.Precision.HIGHEST
NNAR, NWIDE = 8, 32
NPL, BX, NY = 4, 64, 512
CORNERS, ROUGH, FACE = 128, 136, 152
CX, CY = 16, 128
SUBX = 24
SIGMA, KBAR = 0.05, 0.75
DT = 0.15
VMEM = pl.BlockSpec(memory_space=pltpu.VMEM)
HBM = pl.BlockSpec(memory_space=pltpu.HBM)


def sds(*shape):
    return jax.ShapeDtypeStruct(shape, F32)


def params(mib):
    return pltpu.CompilerParams(vmem_limit_bytes=mib * 1024 * 1024)


def sine(points):
    k = np.arange(1, points + 1)
    return np.sqrt(2.0 / (points + 1)) * np.sin(np.pi * np.outer(k, k) / (points + 1))


def level(points):
    return 2.0 - 2.0 * np.cos(np.pi * np.arange(1, points + 1) / (points + 1))


SZ, SY = sine(8), sine(CY)
SPREAD_Y = np.kron(np.eye(CY), np.ones((1, 4)))
SUM_X = np.kron(np.eye(CX), np.ones((1, 4)))
MEAN_Y = SPREAD_Y.T @ SY / 64.0
SZ_ROWS = np.repeat(SZ[:, :, None], CY, 2)


def elimination():
    diag = SIGMA + KBAR * (level(8)[:, None] + level(CY)[None, :] + 2.0)
    inv = [1.0 / diag]
    for _ in range(SUBX - 1):
        inv.append(1.0 / (diag - KBAR * KBAR * inv[-1]))
    return np.stack(inv)


INVERSE = elimination()


CONSTS = np.concatenate([SY, MEAN_Y, INVERSE.reshape(-1, CY), SZ_ROWS.reshape(-1, CY)]).astype(np.float32)
SY_AT, MEAN_AT, INV_AT, SZ_AT = slice(0, 128), slice(128, 640), 640, 640 + 8 * SUBX


def wide_ring(k):
    return [(i, (i + k) % NWIDE) for i in range(NWIDE)]


PAIR_A = [(i, i ^ 1) for i in range(NNAR)]
PAIR_B = [(i, (((i + 1) ^ 1) - 1) % NNAR) for i in range(NNAR)]
CORES = [(i, i ^ 1) for i in range(NWIDE)]
CHIPS = [(i, (((i + 1) ^ 1) - 1) % NWIDE) for i in range(NWIDE)]
NEXT_CHIPS = [(i, (i + (2 if i % 2 else -2)) % NWIDE) for i in range(NWIDE)]


def lanes(v):
    return lax.broadcasted_iota(jnp.int32, v.shape, v.ndim - 1)


def rows_of(v):
    return lax.broadcasted_iota(jnp.int32, v.shape, v.ndim - 2)


def y_up(v):
    n = v.shape[-1]
    return jnp.where(lanes(v) == n - 1, 0.0, pltpu.roll(v, n - 1, v.ndim - 1))


def y_down(v):
    return jnp.where(lanes(v) == 0, 0.0, pltpu.roll(v, 1, v.ndim - 1))


def x_up(v, after):
    return pltpu.roll(jnp.where(rows_of(v) == 0, after, v), 7, v.ndim - 2)


def x_down(v, before):
    return pltpu.roll(jnp.where(rows_of(v) == 7, before, v), 1, v.ndim - 2)


def inverse(v):
    guess = pl.reciprocal(v, approx=True)
    guess = guess * (2.0 - v * guess)
    return guess * (2.0 - v * guess)


def weigh(gz, gx, gy, c2, s2):
    q0, a, b = gz * gz, gx * gx, gy * gy
    r = a + b
    uv = s2 * (b - a) + c2 * (gx * gy)
    num = q0 * q0 + r * r - 2.0 * (uv * uv)
    over = inverse(q0 + r + 1.0)
    return 0.55 + 0.6 * (num * (over * over))


def flag(cond):
    return jnp.where(cond, 1.0, 0.0).astype(F32)


def spread_lanes():
    lane = lax.broadcasted_iota(jnp.int32, (CY, NY), 1)
    row = lax.broadcasted_iota(jnp.int32, (CY, NY), 0)
    return flag(lax.shift_right_logical(lane, 2) == row)


def sum_rows():
    lane = lax.broadcasted_iota(jnp.int32, (CX, BX), 1)
    row = lax.broadcasted_iota(jnp.int32, (CX, BX), 0)
    return flag(lax.shift_right_logical(lane, 2) == row)


def dot(a, b):
    return jnp.dot(a, b, precision=HI, preferred_element_type=F32)


def stage_kernel(
    state_in, ids_in, frozen_in, temp_in, angles_in,
    x_chip, x_core, state, coarse,
    ids, frozen, temp, angles, sems,
):
    copies = [
        pltpu.make_async_copy(src, dst, sems.at[i])
        for i, (src, dst) in enumerate(
            [
                (state_in.at[0], state.at[0]),
                (state_in.at[1], state.at[1]),
                (ids_in, ids),
                (frozen_in, frozen),
                (temp_in, temp),
                (angles_in, angles),
            ]
        )
    ]
    for copy in copies:
        copy.start()
    for copy in copies[2:]:
        copy.wait()
    table = jnp.concatenate([angles[...], angles[...]], 1)
    c = jnp.take_along_axis(jnp.broadcast_to(jnp.cos(table), (CX, CY)), ids[0], axis=1)
    s = jnp.take_along_axis(jnp.broadcast_to(jnp.sin(table), (CX, CY)), ids[0], axis=1)
    coarse[0] = c * c - s * s
    coarse[1] = c * s
    coarse[2] = temp[0]
    coarse[3] = -0.5 * frozen[0].astype(F32)
    for copy in copies[:2]:
        copy.wait()
    core0 = lax.rem(lax.axis_index("wide"), 2) == 0
    for ref, low in ((x_chip, core0), (x_core, jnp.logical_not(core0))):
        for z in range(NPL):
            for at, ch, first, last in ((0, 0, 0, BX - 1), (4, 0, 1, BX - 2), (8, 1, 0, BX - 1)):
                ref[at + z : at + z + 1] = jnp.where(
                    low, state[ch, z, first : first + 1], state[ch, z, last : last + 1]
                )
        for k in range(4):
            ref[12:13, k * CY : (k + 1) * CY] = jnp.where(
                low, coarse[k, 0:1], coarse[k, CX - 1 : CX]
            )
        ref[13:16] = jnp.zeros((3, NY), F32)


def x_sides(x_chip, x_core, rows):
    w = lax.axis_index("wide")
    core0 = lax.rem(w, 2) == 0
    left = jnp.where(core0, x_chip[rows], x_core[rows]) * flag(w > 0)
    right = jnp.where(core0, x_core[rows], x_chip[rows]) * flag(w < NWIDE - 1)
    return left, right


def face_kernel(state, coarse, x_chip, x_core, face_b, face_a):
    n = lax.axis_index("narrow")
    even = lax.rem(n, 2) == 0
    left, right = x_sides(x_chip, x_core, slice(0, 8))
    for ref, top in ((face_b, jnp.logical_not(even)), (face_a, even)):
        first = jnp.where(top, 2, 0)
        ref[0:BX] = state[0, first]
        ref[BX : 2 * BX] = state[0, first + 1]
        ref[CORNERS : CORNERS + 1] = jnp.where(top, left[3:4], left[0:1])
        ref[CORNERS + 1 : CORNERS + 2] = jnp.where(top, right[3:4], right[0:1])
        ref[CORNERS + 2 : CORNERS + 8] = jnp.zeros((6, NY), F32)
        for k in range(4):
            ref[ROUGH : ROUGH + CX, k * CY : (k + 1) * CY] = coarse[k]


def late_kernel(state, base, late_b, late_a):
    even = lax.rem(lax.axis_index("narrow"), 2) == 0
    for ref, top in ((late_b, jnp.logical_not(even)), (late_a, even)):
        ref[...] = state[1, jnp.where(top, 3, 0)]


def widen(ref, at, rough):
    for k in range(CX):
        ref[at, 4 * k : 4 * k + 4] = jnp.broadcast_to(rough[k : k + 1], (4, NY))


def spread_kernel(coarse, consts_in, fine, consts, sem):
    fetch = pltpu.make_async_copy(consts_in, consts, sem)
    fetch.start()
    spread_y = spread_lanes()
    for k in range(3):
        widen(fine, k, dot(coarse[k], spread_y))
    fetch.wait()


def prepare_kernel(
    state, coarse, fine, x_chip, x_core,
    own, rims, fx, fz, known, scale, gxy, base,
):
    left, right = x_sides(x_chip, x_core, slice(0, 4))
    for z in range(NPL):
        own[z, 8 : 8 + BX] = state[0, z]
        own[z, 7:8] = left[z : z + 1]
        own[z, 8 + BX : 9 + BX] = right[z : z + 1]
    left, right = x_sides(x_chip, x_core, slice(12, 13))
    rows = [side[:, k * CY : (k + 1) * CY] for side in (left, right) for k in (0, 1)]
    rims[...] = dot(jnp.concatenate(rows + rows, 0), spread_lanes())

    def chunk(c, carry):
        r0 = pl.multiple_of(c * 8, 8)
        here, at, after = pl.ds(r0, 8), pl.ds(r0 + 8, 8), pl.ds(r0 + 16, 8)
        for z in range(NPL):
            v = own[z, at]
            gx = 0.5 * (x_up(v, own[z, after]) - x_down(v, own[z, here]))
            gy = 0.5 * (y_up(v) - y_down(v))
            m = 1.0 - v * v
            drive = m * (v - 1.5 * (state[1, z, here] + fine[2, here]) * m)
            if z in (0, NPL - 1):
                known[z, here] = drive
                gxy[z // 2, 0, here] = gx
                gxy[z // 2, 1, here] = gy
                continue
            gz = 0.5 * (own[z + 1, at] - own[z - 1, at])
            an = weigh(gz, gx, gy, fine[0, here], fine[1, here])
            wt = an * an
            fz[z - 1, here] = wt * gz
            fx[z - 1, here] = wt * gx
            fy = wt * gy
            known[z, here] = 0.5 * (y_up(fy) - y_down(fy)) + drive
            scale[z - 1, here] = DT * inverse(wt)
        return carry

    lax.fori_loop(0, BX // 8, chunk, 0)

    t, e = coarse[2], coarse[3]
    row = rows_of(t)
    down, up = [], []
    for k, v in ((2, t), (3, e)):
        before, after = left[:, k * CY : (k + 1) * CY], right[:, k * CY : (k + 1) * CY]
        down.append(jnp.where(row == 0, before, pltpu.roll(v, 1, 0)))
        up.append(jnp.where(row == CX - 1, after, pltpu.roll(v, CX - 1, 0)))
    near = [tuple(down), tuple(up), (y_up(t), y_up(e)), (y_down(t), y_down(e))]
    total = jnp.zeros_like(t)
    for tn, en in near:
        total = total + (1.0 + 0.5 * (e + en)) * (tn - t)
    base[...] = total


def phase_kernel(
    coarse, own, fine, rims, fx12, fz12, known, scale12, gxy, x_chip, x_core, zb, za, base, consts,
    out, spectral,
    sides, halo, fx, fz03, fzout, bent, scale03, change, fresh, sems,
):
    n, w = lax.axis_index("narrow"), lax.axis_index("wide")
    even = lax.rem(n, 2) == 0
    has_left, has_right = flag(w > 0), flag(w < NWIDE - 1)
    has_low, has_high = flag(n > 0), flag(n < NNAR - 1)
    left, right = x_sides(x_chip, x_core, slice(4, 8))
    for face, at, there in (
        (zb, jnp.where(even, 0, 2), jnp.where(even, has_low, has_high)),
        (za, jnp.where(even, 2, 0), jnp.where(even, has_high, has_low)),
    ):
        for k in range(2):
            halo[at + k, 8 : 8 + BX] = face[k * BX : (k + 1) * BX] * there
            halo[at + k, 7:8] = face[CORNERS : CORNERS + 1] * there
            halo[at + k, 8 + BX : 9 + BX] = face[CORNERS + 1 : CORNERS + 2] * there
    low = jnp.where(even, zb[ROUGH:FACE], za[ROUGH:FACE])
    high = jnp.where(even, za[ROUGH:FACE], zb[ROUGH:FACE])
    outer = jnp.concatenate([v[:, k * CY : (k + 1) * CY] for v in (low, high) for k in (0, 1)], 0)
    outer = dot(outer, spread_lanes())
    for k in range(4):
        widen(sides, k, outer[k * CX : (k + 1) * CX])
    t, e = coarse[2], coarse[3]
    still = base[...]
    for v, there in ((low, has_low), (high, has_high)):
        tn, en = v[:, 2 * CY : 3 * CY] * there, v[:, 3 * CY :] * there
        still = still + (1.0 + 0.5 * (e + en)) * (tn - t)
    still = dot(still, consts[SY_AT])
    for z in (1, 2):
        fx[z, 8 : 8 + BX] = fx12[z - 1]
    planes = [(halo, 0), (halo, 1), (own, 0), (own, 1), (own, 2), (own, 3), (halo, 2), (halo, 3)]

    def get(k, rows):
        ref, z = planes[k]
        return ref[z, rows]

    def fluxes(c, carry):
        r0 = pl.multiple_of(c * 8, 8)
        here, at, after = pl.ds(r0, 8), pl.ds(r0 + 8, 8), pl.ds(r0 + 16, 8)
        for side, (zz, there) in enumerate(((0, has_low), (5, has_high))):
            v = get(zz + 1, at)
            gz = 0.5 * (get(zz + 2, at) - get(zz, at))
            gx = 0.5 * (x_up(v, get(zz + 1, after)) - x_down(v, get(zz + 1, here)))
            gy = 0.5 * (y_up(v) - y_down(v))
            an = weigh(gz, gx, gy, sides[2 * side, here], sides[2 * side + 1, here])
            fzout[side, here] = there * (an * an * gz)
        for side, z in enumerate((0, NPL - 1)):
            gz = 0.5 * (get(z + 3, at) - get(z + 1, at))
            gx, gy = gxy[side, 0, here], gxy[side, 1, here]
            an = weigh(gz, gx, gy, fine[0, here], fine[1, here])
            wt = an * an
            fz03[side, here] = wt * gz
            fx[z, at] = wt * gx
            fy = wt * gy
            bent[side, here] = known[z, here] + 0.5 * (y_up(fy) - y_down(fy))
            scale03[side, here] = DT * inverse(wt)
        return carry

    lax.fori_loop(0, BX // 8, fluxes, 0)

    def column(pick):
        return jnp.concatenate([pick(z, s) for s in (0, 1) for z in range(NPL)], 0)

    rim = (slice(7, 8), slice(8 + BX, 9 + BX))
    centre = column(lambda z, s: get(z + 2, rim[s]))
    below = column(lambda z, s: get(z + 1, rim[s]))
    above = column(lambda z, s: get(z + 3, rim[s]))
    x_hi = column(lambda z, s: right[z : z + 1] if s else own[z, 8:9])
    x_lo = column(lambda z, s: own[z, 7 + BX : 8 + BX] if s else left[z : z + 1])
    first = rows_of(centre) < NPL
    c2 = jnp.where(first, rims[0:1], rims[2:3])
    s2 = jnp.where(first, rims[1:2], rims[3:4])
    gx = 0.5 * (x_hi - x_lo)
    an = weigh(0.5 * (above - below), gx, 0.5 * (y_up(centre) - y_down(centre)), c2, s2)
    rim_flux = jnp.where(first, has_left, has_right) * (an * an * gx)
    for z in range(NPL):
        fx[z, 7:8] = rim_flux[z : z + 1]
        fx[z, 8 + BX : 9 + BX] = rim_flux[NPL + z : NPL + z + 1]

    flux_z = [(fzout, 0), (fz03, 0), (fz12, 0), (fz12, 1), (fz03, 1), (fzout, 1)]
    rest = [(bent, 0), (known, 1), (known, 2), (bent, 1)]
    scales = [(scale03, 0), (scale12, 0), (scale12, 1), (scale03, 1)]

    def step(c, carry):
        r0 = pl.multiple_of(c * 8, 8)
        here, at, after = pl.ds(r0, 8), pl.ds(r0 + 8, 8), pl.ds(r0 + 16, 8)

        def of(pair):
            return pair[0][pair[1], here]

        total = jnp.zeros((8, NY), F32)
        for z in range(NPL):
            p, f = own[z, at], fx[z, at]
            spread = (
                of(rest[z])
                + 0.5 * (of(flux_z[z + 2]) - of(flux_z[z]))
                + 0.5 * (x_up(f, fx[z, after]) - x_down(f, fx[z, here]))
            )
            rise = of(scales[z]) * spread
            fresh[z, here] = p + rise
            total = total + rise
        change[here] = total
        store(c).start()
        return carry

    def store(c):
        rows = pl.ds(pl.multiple_of(c * 8, 8), 8)
        return pltpu.make_async_copy(fresh.at[:, rows], out.at[0, :, rows], sems.at[c])

    lax.fori_loop(0, BX // 8, step, 0)
    spectral[...] = still + dot(dot(sum_rows(), change[...]), consts[MEAN_AT])
    for c in range(BX // 8):
        store(c).wait()


def solute_kernel(state, own, x_chip, x_core, zb, za, lb, la, done, out, sown, fresh, grown, sems):
    fetch = pltpu.make_async_copy(done.at[0], fresh, sems.at[0])
    fetch.start()
    n = lax.axis_index("narrow")
    even = lax.rem(n, 2) == 0
    left, right = x_sides(x_chip, x_core, slice(8, 12))
    has_low, has_high = flag(n > 0), flag(n < NNAR - 1)
    for z in range(NPL):
        sown[z, 8 : 8 + BX] = state[1, z]
        sown[z, 7:8] = left[z : z + 1]
        sown[z, 8 + BX : 9 + BX] = right[z : z + 1]
    fetch.wait()

    def step(c, carry):
        r0 = pl.multiple_of(c * 8, 8)
        here, at, after = pl.ds(r0, 8), pl.ds(r0 + 8, 8), pl.ds(r0 + 16, 8)

        beyond = pl.ds(pl.multiple_of(r0 + BX, 8), 8)
        ps = (
            [has_low * jnp.where(even, zb[beyond], za[beyond])]
            + [own[z, at] for z in range(NPL)]
            + [has_high * jnp.where(even, za[here], zb[here])]
        )
        ss = (
            [has_low * jnp.where(even, lb[here], la[here])]
            + [sown[z, at] for z in range(NPL)]
            + [has_high * jnp.where(even, la[here], lb[here])]
        )
        for z in range(NPL):
            p, s = ps[z + 1], ss[z + 1]
            q = 0.55 - 0.25 * p
            near = [
                (ps[z], ss[z]),
                (ps[z + 2], ss[z + 2]),
                (x_up(p, own[z, after]), x_up(s, sown[z, after])),
                (x_down(p, own[z, here]), x_down(s, sown[z, here])),
                (y_up(p), y_up(s)),
                (y_down(p), y_down(s)),
            ]
            total = jnp.zeros_like(p)
            for pn, sn in near:
                total = total + (q - 0.25 * pn) * (sn - s)
            grown[z, here] = s + DT * total + (0.5 + 0.425 * s) * (fresh[z, here] - p)
        store(c).start()
        return carry

    def store(c):
        rows = pl.ds(pl.multiple_of(c * 8, 8), 8)
        return pltpu.make_async_copy(grown.at[:, rows], out.at[1, :, rows], sems.at[1 + c])

    lax.fori_loop(0, BX // 8, step, 0)
    for c in range(BX // 8):
        store(c).wait()


def chip_kernel(mine, partner, lb, la, here, message, far):
    core = lax.rem(lax.axis_index("wide"), 2)
    first, second = pl.ds(pl.multiple_of(core * CX, 8), CX), pl.ds(pl.multiple_of((1 - core) * CX, 8), CX)
    here[first] = mine[...]
    here[second] = partner[...]
    message[0:CX] = mine[...]
    near = jnp.where(core == 0, partner[0:8], pltpu.roll(partner[8:16], 4, 0))
    message[CX : CX + 8] = near
    far[...] = jnp.where(core == 0, mine[0:8], pltpu.roll(mine[8:16], 4, 0))


def window_kernel(here, across, shared, out, view, sems):
    w = lax.axis_index("wide")
    core, chip = lax.rem(w, 2), lax.div(w, 2)
    has_before, has_after = flag(chip > 0), flag(chip < NWIDE // 2 - 1)

    @pl.when(core == 0)
    def _():
        view[0:4] = across[CX : CX + 4] * has_before
        view[4:20] = across[0:CX] * has_before
        view[20:52] = here[...]
        view[52:56] = shared[0:4] * has_after

    @pl.when(core == 1)
    def _():
        view[0:4] = shared[0:4] * has_before
        view[4:36] = here[...]
        view[36:56] = across[0:20] * has_after

    copies = [pltpu.make_async_copy(view, out.at[m], sems.at[m]) for m in range(NNAR)]
    for copy in copies:
        copy.start()
    for copy in copies:
        copy.wait()


def solve_kernel(planes, coarse, consts, out, modes, rows):
    n, w = lax.axis_index("narrow"), lax.axis_index("wide")
    has_left, has_right = flag(w > 0), flag(w < NWIDE - 1)
    values = [planes[m] for m in range(NNAR)]
    for k in range(NNAR):
        total = float(SZ[k, 0]) * values[0]
        for m in range(1, NNAR):
            total = total + float(SZ[k, m]) * values[m]
        modes[k * 56 : (k + 1) * 56] = total
    f = [modes[pl.ds(j, 8, stride=56), :] for j in range(56)]
    inv_of = [consts[INV_AT + 8 * i : INV_AT + 8 * i + 8] for i in range(SUBX)]
    link = [KBAR * v for v in inv_of]

    def solve(order, keep):
        h = [inv_of[0] * f[order[0]]]
        for i in range(1, SUBX):
            h.append(inv_of[i] * f[order[i]] + link[i] * h[-1])
        x = h[-1]
        found = {order[-1]: x}
        for i in range(SUBX - 2, -1, -1):
            if order[i] not in keep:
                break
            x = h[i] + link[i] * x
            found[order[i]] = x
        return found

    mine = solve(list(range(16, 40)), set(range(20, 40)))
    lower = solve(list(range(0, 24)), set(range(20, 24)))
    upper = solve(list(range(55, 31, -1)), set(range(32, 36)))
    weight = consts[pl.ds(pl.multiple_of(SZ_AT + 8 * n, 8), 8)]
    for j in range(CX):
        x = mine[20 + j]
        if 20 + j in lower:
            x = x + has_left * lower[20 + j]
        if 20 + j in upper:
            x = x + has_right * upper[20 + j]
        rows[j : j + 1] = jnp.sum(x * weight, axis=0, keepdims=True)
    out[0] = coarse[2] + dot(rows[...], consts[SY_AT])


def kernel(body, outs, scratch=(), far=(), far_outs=(), aliases=None, mib=16):
    many = isinstance(outs, (list, tuple))

    def call(*args):
        return pl.pallas_call(
            body,
            out_shape=outs,
            in_specs=[HBM if i in far else VMEM for i in range(len(args))],
            out_specs=[HBM if i in far_outs else VMEM for i in range(len(outs))] if many else (HBM if far_outs else VMEM),
            input_output_aliases=aliases or {},
            scratch_shapes=list(scratch),
            compiler_params=params(mib),
            name=body.__name__,
        )(*args)

    return call


def afar(v):
    return pltpu.with_memory_space_constraint(v, pltpu.HBM)


def on_device(state_in, ids, frozen, temp, angles):
    inputs = [afar(v) for v in (state_in, ids, frozen, temp, angles.reshape(1, -1))]
    to_chip, to_core, state, coarse = kernel(
        stage_kernel,
        [sds(16, NY)] * 2 + [sds(2, NPL, BX, NY), sds(4, CX, CY)],
        [
            pltpu.VMEM((1, CX, CY), jnp.int32),
            pltpu.VMEM((1, CX, CY), jnp.int32),
            pltpu.VMEM((1, CX, CY), F32),
            pltpu.VMEM((1, 64), F32),
            pltpu.SemaphoreType.DMA((6,)),
        ],
        far=range(5),
    )(*inputs)
    x_chip = lax.ppermute(to_chip, "wide", CHIPS)
    x_core = lax.ppermute(to_core, "wide", CORES)
    fine, consts = kernel(
        spread_kernel, [sds(3, BX, NY), sds(*CONSTS.shape)], [pltpu.SemaphoreType.DMA], far=(1,)
    )(coarse, afar(jnp.asarray(CONSTS)))
    face_b, face_a = kernel(face_kernel, [sds(FACE, NY)] * 2)(state, coarse, x_chip, x_core)
    zb = lax.ppermute(face_b, "narrow", PAIR_B)
    za = lax.ppermute(face_a, "narrow", PAIR_A)
    own, rims, fx12, fz12, known, scale12, gxy, base = kernel(
        prepare_kernel,
        [
            sds(NPL, BX + 16, NY), sds(8, NY), sds(2, BX, NY), sds(2, BX, NY),
            sds(NPL, BX, NY), sds(2, BX, NY), sds(2, 2, BX, NY), sds(CX, CY),
        ],
    )(state, coarse, fine, x_chip, x_core)
    late_b, late_a = kernel(late_kernel, [sds(BX, NY)] * 2)(state, base)
    lb = lax.ppermute(late_b, "narrow", PAIR_B)
    la = lax.ppermute(late_a, "narrow", PAIR_A)
    result, spectral = kernel(
        phase_kernel,
        [sds(2, NPL, BX, NY), sds(CX, CY)],
        [
            pltpu.VMEM((4, BX, NY), F32),
            pltpu.VMEM((4, BX + 16, NY), F32),
            pltpu.VMEM((NPL, BX + 16, NY), F32),
            pltpu.VMEM((2, BX, NY), F32),
            pltpu.VMEM((2, BX, NY), F32),
            pltpu.VMEM((2, BX, NY), F32),
            pltpu.VMEM((2, BX, NY), F32),
            pltpu.VMEM((BX, NY), F32),
            pltpu.VMEM((NPL, BX, NY), F32),
            pltpu.SemaphoreType.DMA((BX // 8,)),
        ],
        far_outs=(0,),
    )(coarse, own, fine, rims, fx12, fz12, known, scale12, gxy, x_chip, x_core, zb, za, base, consts)
    partner = lax.ppermute(spectral, "wide", CORES)
    here, message, far = kernel(
        chip_kernel, [sds(2 * CX, CY), sds(CX + 8, CY), sds(8, CY)]
    )(
        spectral, partner, lb, la
    )
    across = lax.ppermute(message, "wide", CHIPS)
    shared = lax.ppermute(far, "wide", NEXT_CHIPS)
    windows = kernel(
        window_kernel,
        sds(NNAR, 56, CY),
        [pltpu.VMEM((56, CY), F32), pltpu.SemaphoreType.DMA((NNAR,))],
        far_outs=(0,),
    )(here, across, shared)
    planes = lax.all_to_all(windows, "narrow", 0, 0)
    state_new = kernel(
        solute_kernel,
        sds(2, NPL, BX, NY),
        [
            pltpu.VMEM((NPL, BX + 16, NY), F32),
            pltpu.VMEM((NPL, BX, NY), F32),
            pltpu.VMEM((NPL, BX, NY), F32),
            pltpu.SemaphoreType.DMA((1 + BX // 8,)),
        ],
        far=(8,),
        far_outs=(0,),
        aliases={8: 0},
    )(state, own, x_chip, x_core, zb, za, lb, la, result)
    adjusted = kernel(
        solve_kernel,
        sds(1, CX, CY),
        [pltpu.VMEM((NNAR * 56, CY), F32), pltpu.VMEM((CX, CY), F32)],
    )(planes, coarse, consts)
    return state_new, adjusted


def solution(mesh):
    return jax.shard_map(
        on_device,
        mesh=mesh,
        in_specs=(
            P(None, "narrow", "wide", None),
            P("narrow", "wide", None),
            P("narrow", "wide", None),
            P("narrow", "wide", None),
            P(),
        ),
        out_specs=(P(None, "narrow", "wide", None), P("narrow", "wide", None)),
        check_vma=False,
    )
```

time: 52 us -> 50.8 us (0.977)
  the two profiles are of different devices: /device:TPU:96 before, /device:TPU:2 now
where the time goes in v2:
time: 50.8 us; the launch traced here: 50.5 us
  starting transfers between devices  23.7 us (47%)
  waiting for transfers between devices  14.5 us (29%)
  Pallas kernels  11.7 us (23%)
  between operations  0.73 us (1%)
    pallas_call x10, Pallas kernels, call(): pl.pallas_call(body, out_shape=outs, in_specs=[HBM if i in far else VMEM...  11.7 us
    all_to_all x1, starting transfers between devices, on_device(): planes = lax.all_to_all(windows, 'narrow', 0, 0)  7.53 us
    ppermute x1, starting transfers between devices, on_device(): x_chip = lax.ppermute(to_chip, 'wide', CHIPS)  6.39 us
    all_to_all x1, waiting for transfers between devices, on_device(): planes = lax.all_to_all(windows, 'narrow', 0, 0)  4.52 us
    ppermute x1, starting transfers between devices, on_device(): za = lax.ppermute(face_a, 'narrow', PAIR_A)  4.14 us
    ppermute x1, waiting for transfers between devices, on_device(): za = lax.ppermute(face_a, 'narrow', PAIR_A)  3.71 us
    ppermute x1, waiting for transfers between devices, on_device(): shared = lax.ppermute(far, 'wide', NEXT_CHIPS)  3.47 us
    ppermute x1, starting transfers between devices, on_device(): across = lax.ppermute(message, 'wide', CHIPS)  2.35 us
  transfers between devices with their start and end apart: 10, of which 5 were waited for; matrix products, arithmetic and copies ran while one was open for 0% of the time, Pallas kernels for 17%

profile of v2, /device:TPU:2, one launch (start us, length us, event | category | flops | bytes accessed | tf_op | source)
XLA Modules:
  0.0 50.5 jit_solution(3222339000473167187)
XLA Ops:
  0.6 1.4 %stage_kernel.1 = (f32[16,512]{1,0:T(8,128)S(1)}, f32[16,512]{1,0:T(8,128)S(1)}, f32[2,4,64,512]{3,2,1,0:T(8,128)S(1)}, f32[4,16,128]{2,1,0:T(8,128)S(1)}) custom-call(f32[2,4,64,512]{3,2,1,0:T(8,128)} %state_in.1, s32[1,16,128]{2,1,0:T(8,128)} %ids_in.1, s32[1,16,128]{2,1,0:T(8,128)} %frozen_in.1, f32[1,16,128]{2,1,0:T(8,128)} %temp_in.1, f32[1,64]{1,0:T(1,128)} %bitcast.1), custom_call_target="tpu_custom_call" | custom-call | tf_op jit(solution)/shard_map/stage_kernel/pallas_call | solution.py:527
  2.0 6.4 %collective-permute-start = (f32[16,512]{1,0:T(8,128)S(1)}, f32[16,512]{1,0:T(8,128)S(1)}, u32[]{:S(2)}, u32[]{:S(2)}) collective-permute-start(f32[16,512]{1,0:T(8,128)S(1)} %get-tuple-element.28), channel_id=1, source_target_pairs={{0,31},{1,2},{2,1},{3,4},{4,3},{5,6},{6,5},{7,8},{8,7},{9,10},{10,... | collective-permute-start | bytes 98312 | tf_op jit(solution)/shard_map/ppermute | solution.py:559
  8.4 0.0 collective-permute-start.1
  8.4 1.6 %collective-permute-done.x_chip = f32[16,512]{1,0:T(8,128)S(1)} collective-permute-done((f32[16,512]{1,0:T(8,128)S(1)}, f32[16,512]{1,0:T(8,128)S(1)}, u32[]{:S(2)}, u32[]{:S(2)}) %collective-permute-start) | collective-permute-done | bytes 32800 | tf_op jit(solution)/shard_map/ppermute | solution.py:559
  10.0 0.0 collective-permute-done.1.x_core
  10.1 1.6 %collective-permute-start.2 = (f32[152,512]{1,0:T(8,128)S(1)}, f32[152,512]{1,0:T(8,128)S(1)}, u32[]{:S(2)}, u32[]{:S(2)}) collective-permute-start(f32[152,512]{1,0:T(8,128)S(1)} %get-tuple-element.31), channel_id=1, source_target_pairs={{0,224},{32,64},{64,32},{96,128},{128,96},{160,192},{192,160},{224... | collective-permute-start | bytes 933896 | tf_op jit(solution)/shard_map/ppermute | solution.py:565
  11.6 4.1 %collective-permute-start.3 = (f32[152,512]{1,0:T(8,128)S(1)}, f32[152,512]{1,0:T(8,128)S(1)}, u32[]{:S(2)}, u32[]{:S(2)}) collective-permute-start(f32[152,512]{1,0:T(8,128)S(1)} %get-tuple-element.32), channel_id=1, source_target_pairs={{0,32},{32,0},{64,96},{96,64},{128,160},{160,128},{192,224},{224,1... | collective-permute-start | bytes 933896 | tf_op jit(solution)/shard_map/ppermute | solution.py:566
  15.8 1.0 %spread_kernel.1 = (f32[3,64,512]{2,1,0:T(8,128)S(1)}, f32[896,128]{1,0:T(8,128)S(1)}) custom-call(f32[4,16,128]{2,1,0:T(8,128)S(1)} %get-tuple-element.26.coarse, f32[896,128]{1,0:T(8,128)} %constant.2.clone.consts_in), custom_call_target="tpu_custom_call" | custom-call | tf_op jit(solution)/shard_map/spread_kernel/pallas_call | solution.py:527
  16.8 2.0 %prepare_kernel.1 = (f32[4,80,512]{2,1,0:T(8,128)S(1)}, f32[8,512]{1,0:T(8,128)S(1)}, f32[2,64,512]{2,1,0:T(8,128)S(1)}, f32[2,64,512]{2,1,0:T(8,128)S(1)}, f32[...) custom-call(f32[2,4,64,512]{3,2,1,0:T(8,128)S(1)} %get-tuple-element.2, ...), custom_call_target="tpu_custom_call" | custom-call | tf_op jit(solution)/shard_map/prepare_kernel/pallas_call | solution.py:527
  18.9 0.1 collective-permute-start.4
  19.0 1.4 %collective-permute-start.5 = (f32[64,512]{1,0:T(8,128)S(1)}, f32[64,512]{1,0:T(8,128)S(1)}, u32[]{:S(2)}, u32[]{:S(2)}) collective-permute-start(f32[64,512]{1,0:T(8,128)S(1)} %get-tuple-element.35), channel_id=1, source_target_pairs={{0,32},{32,0},{64,96},{96,64},{128,160},{160,128},{192,224},{224,1... | collective-permute-start | bytes 393224 | tf_op jit(solution)/shard_map/ppermute | solution.py:576
  20.3 0.0 collective-permute-done.2.zb
  20.3 3.7 %collective-permute-done.3.za = f32[152,512]{1,0:T(8,128)S(1)} collective-permute-done((f32[152,512]{1,0:T(8,128)S(1)}, f32[152,512]{1,0:T(8,128)S(1)}, u32[]{:S(2)}, u32[]{:S(2)}) %collective-permute-start.3) | collective-permute-done | bytes 311328 | tf_op jit(solution)/shard_map/ppermute | solution.py:566
  24.0 2.5 %phase_kernel.1 = (f32[2,4,64,512]{3,2,1,0:T(8,128)}, f32[16,128]{1,0:T(8,128)S(1)}) custom-call(f32[4,16,128]{2,1,0:T(8,128)S(1)} %get-tuple-element.26.coarse, f32[4,80,512]{2,1,0:T(8,128)S(1)} %get-tuple-element.30.own, f32[3,64,512]{2,1,0:T(8,128)S(1)} %get-tuple-element.27.fine, f32[8,512]{1,0:T(8,128)S(1)} %get-tuple-element.36.rims, ...), custom_call_target="tpu_custom_call" | custom-call | tf_op jit(solution)/shard_map/phase_kernel/pallas_call | solution.py:527
  26.5 0.1 collective-permute-start.6
  26.6 0.0 collective-permute-done.4.lb
  26.6 0.0 collective-permute-done.5.la
  26.7 1.1 %collective-permute-done.6.partner = f32[16,128]{1,0:T(8,128)S(1)} collective-permute-done((f32[16,128]{1,0:T(8,128)S(1)}, f32[16,128]{1,0:T(8,128)S(1)}, u32[]{:S(2)}, u32[]{:S(2)}) %collective-permute-start.6) | collective-permute-done | bytes 8224 | tf_op jit(solution)/shard_map/ppermute | solution.py:594
  27.8 2.4 %collective-permute-start.7 = (f32[24,128]{1,0:T(8,128)S(1)}, f32[24,128]{1,0:T(8,128)S(1)}, u32[]{:S(2)}, u32[]{:S(2)}) collective-permute-start(f32[24,128]{1,0:T(8,128)S(1)} %get-tuple-element.46), channel_id=1, source_target_pairs={{0,31},{1,2},{2,1},{3,4},{4,3},{5,6},{6,5},{7,8},{8,7},{9,10},{10,... | collective-permute-start | bytes 36872 | tf_op jit(solution)/shard_map/ppermute | solution.py:600
  30.2 0.1 collective-permute-start.8
  30.3 3.5 %collective-permute-done.8.shared = f32[8,128]{1,0:T(8,128)S(1)} collective-permute-done((f32[8,128]{1,0:T(8,128)S(1)}, f32[8,128]{1,0:T(8,128)S(1)}, u32[]{:S(2)}, u32[]{:S(2)}) %collective-permute-start.8) | collective-permute-done | bytes 4128 | tf_op jit(solution)/shard_map/ppermute | solution.py:601
  33.8 0.0 collective-permute-done.7.across
  33.8 0.8 %window_kernel.1 = f32[8,56,128]{2,1,0:T(8,128)} custom-call(f32[32,128]{1,0:T(8,128)S(1)} %get-tuple-element.45.here, f32[24,128]{1,0:T(8,128)S(1)} %collective-permute-done.7.across, f32[8,128]{1,0:T(8,128)S(1)} %collective-permute-done.8.shared), custom_call_target="tpu_custom_call" | custom-call | tf_op jit(solution)/shard_map/window_kernel/pallas_call | solution.py:527
  34.5 7.5 %all-to-all-start = ((f32[8,56,128]{2,1,0:T(8,128)}), f32[8,56,128]{2,1,0:T(8,128)S(1)}, u32[]{:S(2)}, u32[]{:S(2)}) async-start(f32[8,56,128]{2,1,0:T(8,128)} %window_kernel.1), calls=%async_computation | async-start | bytes 458752 | tf_op jit(solution)/shard_map/all_to_all | solution.py:608
  42.1 2.9 %solute_kernel.1 = f32[2,4,64,512]{3,2,1,0:T(8,128)} custom-call(f32[2,4,64,512]{3,2,1,0:T(8,128)S(1)} %get-tuple-element.25.state, f32[4,80,512]{2,1,0:T(8,128)S(1)} %get-tuple-element.30.own, f32[16,512]{1,0:T(8,128)S(1)} %collective-permute-done.x_chip, f32[16,512]{1,0:T(8,128)S(1)} %collective-permute-done.1.x_core, ...), custom_call_target="tpu_custom_call", output_to_operand_aliasing={{}: (8, {})} | custom-call | tf_op jit(solution)/shard_map/solute_kernel/pallas_call | solution.py:527
  45.0 4.5 %all-to-all-done.planes = f32[8,56,128]{2,1,0:T(8,128)S(1)} async-done(((f32[8,56,128]{2,1,0:T(8,128)}), f32[8,56,128]{2,1,0:T(8,128)S(1)}, u32[]{:S(2)}, u32[]{:S(2)}) %all-to-all-start) | async-done | bytes 229408 | tf_op jit(solution)/shard_map/all_to_all | solution.py:608
  49.5 1.0 %solve_kernel.1 = f32[1,16,128]{2,1,0:T(8,128)} custom-call(f32[8,56,128]{2,1,0:T(8,128)S(1)} %all-to-all-done.planes, f32[4,16,128]{2,1,0:T(8,128)S(1)} %get-tuple-element.26.coarse, f32[896,128]{1,0:T(8,128)S(1)} %get-tuple-element.42.consts), custom_call_target="tpu_custom_call" | custom-call | tf_op jit(solution)/shard_map/solve_kernel/pallas_call | solution.py:527
  (3 shorter events, 0.1 us)
Async XLA Ops:
  2.0 8.0 %collective-permute-start = (f32[16,512]{1,0:T(8,128)S(1)}, f32[16,512]{1,0:T(8,128)S(1)}, u32[]{:S(2)}, u32[]{:S(2)}) collective-permute-start(f32[16,512]{1,0:T(8,128)S(1)} %get-tuple-element.28), channel_id=1, source_target_pairs={{0,31},{1,2},{2,1},{3,4},{4,3},{5,6},{6,5},{7,8},{8,7},{9,10},{10,... | collective-permute-start | bytes 98312 | tf_op jit(solution)/shard_map/ppermute | solution.py:559
  8.4 1.6 %collective-permute-start.1 = (f32[16,512]{1,0:T(8,128)S(1)}, f32[16,512]{1,0:T(8,128)S(1)}, u32[]{:S(2)}, u32[]{:S(2)}) collective-permute-start(f32[16,512]{1,0:T(8,128)S(1)} %get-tuple-element.29), channel_id=1, source_target_pairs={{0,1},{1,0},{2,3},{3,2},{4,5},{5,4},{6,7},{7,6},{8,9},{9,8},{10,11... | collective-permute-start | bytes 98312 | tf_op jit(solution)/shard_map/ppermute | solution.py:560
  10.1 10.2 %collective-permute-start.2 = (f32[152,512]{1,0:T(8,128)S(1)}, f32[152,512]{1,0:T(8,128)S(1)}, u32[]{:S(2)}, u32[]{:S(2)}) collective-permute-start(f32[152,512]{1,0:T(8,128)S(1)} %get-tuple-element.31), channel_id=1, source_target_pairs={{0,224},{32,64},{64,32},{96,128},{128,96},{160,192},{192,160},{224... | collective-permute-start | bytes 933896 | tf_op jit(solution)/shard_map/ppermute | solution.py:565
  11.6 12.4 %collective-permute-start.3 = (f32[152,512]{1,0:T(8,128)S(1)}, f32[152,512]{1,0:T(8,128)S(1)}, u32[]{:S(2)}, u32[]{:S(2)}) collective-permute-start(f32[152,512]{1,0:T(8,128)S(1)} %get-tuple-element.32), channel_id=1, source_target_pairs={{0,32},{32,0},{64,96},{96,64},{128,160},{160,128},{192,224},{224,1... | collective-permute-start | bytes 933896 | tf_op jit(solution)/shard_map/ppermute | solution.py:566
  18.9 7.8 %collective-permute-start.4 = (f32[64,512]{1,0:T(8,128)S(1)}, f32[64,512]{1,0:T(8,128)S(1)}, u32[]{:S(2)}, u32[]{:S(2)}) collective-permute-start(f32[64,512]{1,0:T(8,128)S(1)} %get-tuple-element.34), channel_id=1, source_target_pairs={{0,224},{32,64},{64,32},{96,128},{128,96},{160,192},{192,160},{224... | collective-permute-start | bytes 393224 | tf_op jit(solution)/shard_map/ppermute | solution.py:575
  19.0 7.7 %collective-permute-start.5 = (f32[64,512]{1,0:T(8,128)S(1)}, f32[64,512]{1,0:T(8,128)S(1)}, u32[]{:S(2)}, u32[]{:S(2)}) collective-permute-start(f32[64,512]{1,0:T(8,128)S(1)} %get-tuple-element.35), channel_id=1, source_target_pairs={{0,32},{32,0},{64,96},{96,64},{128,160},{160,128},{192,224},{224,1... | collective-permute-start | bytes 393224 | tf_op jit(solution)/shard_map/ppermute | solution.py:576
  26.5 1.3 %collective-permute-start.6 = (f32[16,128]{1,0:T(8,128)S(1)}, f32[16,128]{1,0:T(8,128)S(1)}, u32[]{:S(2)}, u32[]{:S(2)}) collective-permute-start(f32[16,128]{1,0:T(8,128)S(1)} %get-tuple-element.44.mine), channel_id=1, source_target_pairs={{0,1},{1,0},{2,3},{3,2},{4,5},{5,4},{6,7},{7,6},{8,9},{9,8},{10,11... | collective-permute-start | bytes 24584 | tf_op jit(solution)/shard_map/ppermute | solution.py:594
  27.8 6.0 %collective-permute-start.7 = (f32[24,128]{1,0:T(8,128)S(1)}, f32[24,128]{1,0:T(8,128)S(1)}, u32[]{:S(2)}, u32[]{:S(2)}) collective-permute-start(f32[24,128]{1,0:T(8,128)S(1)} %get-tuple-element.46), channel_id=1, source_target_pairs={{0,31},{1,2},{2,1},{3,4},{4,3},{5,6},{6,5},{7,8},{8,7},{9,10},{10,... | collective-permute-start | bytes 36872 | tf_op jit(solution)/shard_map/ppermute | solution.py:600
  30.2 3.6 %collective-permute-start.8 = (f32[8,128]{1,0:T(8,128)S(1)}, f32[8,128]{1,0:T(8,128)S(1)}, u32[]{:S(2)}, u32[]{:S(2)}) collective-permute-start(f32[8,128]{1,0:T(8,128)S(1)} %get-tuple-element.47), channel_id=1, source_target_pairs={{0,30},{1,3},{2,0},{3,5},{4,2},{5,7},{6,4},{7,9},{8,6},{9,11},{10,... | collective-permute-start | bytes 12296 | tf_op jit(solution)/shard_map/ppermute | solution.py:601
  34.5 15.0 %all-to-all-start = ((f32[8,56,128]{2,1,0:T(8,128)}), f32[8,56,128]{2,1,0:T(8,128)S(1)}, u32[]{:S(2)}, u32[]{:S(2)}) async-start(f32[8,56,128]{2,1,0:T(8,128)} %window_kernel.1), calls=%async_computation | async-start | bytes 458752 | tf_op jit(solution)/shard_map/all_to_all | solution.py:608

commit v3 on v2

v3 whole, which is shorter than its diff:
```python
import functools

import jax
import jax.numpy as jnp
import numpy as np
from jax import lax
from jax.experimental import pallas as pl
from jax.experimental.pallas import tpu as pltpu
from jax.sharding import PartitionSpec as P

F32 = jnp.float32
NNAR, NWIDE = 8, 32
NPL, BX, NY = 4, 64, 512
ROUGH, FACE, CORNERS, LATE = 128, 144, 64, 72
CX, CY = 16, 128
SUBX = 24
SIGMA, KBAR = 0.05, 0.75
DT = 0.15
VMEM = pl.BlockSpec(memory_space=pltpu.VMEM)
HBM = pl.BlockSpec(memory_space=pltpu.HBM)


def sds(*shape):
    return jax.ShapeDtypeStruct(shape, F32)


def params(mib):
    return pltpu.CompilerParams(vmem_limit_bytes=mib * 1024 * 1024)


def sine(points):
    k = np.arange(1, points + 1)
    return np.sqrt(2.0 / (points + 1)) * np.sin(np.pi * np.outer(k, k) / (points + 1))


def level(points):
    return 2.0 - 2.0 * np.cos(np.pi * np.arange(1, points + 1) / (points + 1))


SZ, SY = sine(8), sine(CY)
MEAN_Y = np.repeat(SY, 4, axis=0) / 64.0
SZ_ROWS = np.repeat(SZ[:, :, None], CY, 2)


def elimination():
    diag = SIGMA + KBAR * (level(8)[:, None] + level(CY)[None, :] + 2.0)
    inv = [1.0 / diag]
    for _ in range(SUBX - 1):
        inv.append(1.0 / (diag - KBAR * KBAR * inv[-1]))
    return np.stack(inv)


INVERSE = elimination()


CONSTS = np.concatenate([SY, MEAN_Y, INVERSE.reshape(-1, CY), SZ_ROWS.reshape(-1, CY)]).astype(np.float32)
SY_AT, MEAN_AT, INV_AT, SZ_AT = slice(0, 128), slice(128, 640), 640, 640 + 8 * SUBX


def wide_ring(k):
    return [(i, (i + k) % NWIDE) for i in range(NWIDE)]


PAIR_A = [(i, i ^ 1) for i in range(NNAR)]
PAIR_B = [(i, (((i + 1) ^ 1) - 1) % NNAR) for i in range(NNAR)]
CORES = [(i, i ^ 1) for i in range(NWIDE)]
CHIPS = [(i, (((i + 1) ^ 1) - 1) % NWIDE) for i in range(NWIDE)]
NEXT_CHIPS = [(i, (i + (2 if i % 2 else -2)) % NWIDE) for i in range(NWIDE)]


def lanes(v):
    return lax.broadcasted_iota(jnp.int32, v.shape, v.ndim - 1)


def rows_of(v):
    return lax.broadcasted_iota(jnp.int32, v.shape, len(v.shape) - 2)


def y_up(v):
    n = v.shape[-1]
    return jnp.where(lanes(v) == n - 1, 0.0, pltpu.roll(v, n - 1, v.ndim - 1))


def y_down(v):
    return jnp.where(lanes(v) == 0, 0.0, pltpu.roll(v, 1, v.ndim - 1))


def x_up(v, after):
    return pltpu.roll(jnp.where(rows_of(v) == 0, after, v), 7, v.ndim - 2)


def x_down(v, before):
    return pltpu.roll(jnp.where(rows_of(v) == 7, before, v), 1, v.ndim - 2)


def inverse(v):
    guess = pl.reciprocal(v, approx=True)
    return guess * (2.0 - v * guess)


def weigh(dz, dx, dy, c2, s2):
    q0, a, b = dz * dz, dx * dx, dy * dy
    r = a + b
    uv = s2 * (b - a) + c2 * (dx * dy)
    num = q0 * q0 + r * r - 2.0 * (uv * uv)
    over = inverse(q0 + r + 4.0)
    return 0.55 + 0.6 * (num * (over * over))


def flag(cond):
    return jnp.where(cond, 1.0, 0.0).astype(F32)


def spread(v):
    lane = lax.shift_right_logical(lanes(v), 2)
    return jnp.concatenate(
        [jnp.take_along_axis(v, lane + 32 * j, axis=1) for j in range(NY // CY)], 1
    )


def halves(v):
    high = v.astype(jnp.bfloat16)
    return high, (v - high.astype(F32)).astype(jnp.bfloat16)


def dot(a, b):
    (a1, a2), (b1, b2) = halves(a), halves(b)
    mul = functools.partial(jnp.dot, preferred_element_type=F32)
    return mul(a1, b1) + (mul(a1, b2) + mul(a2, b1))


def stage_kernel(
    state_in, ids_in, frozen_in, temp_in, angles_in,
    face_b, face_a, x_chip, x_core, state, coarse,
    ids, frozen, temp, angles, sems,
):
    copies = [
        pltpu.make_async_copy(src, dst, sems.at[i])
        for i, (src, dst) in enumerate(
            [
                (state_in.at[0], state.at[0]),
                (state_in.at[1], state.at[1]),
                (ids_in, ids),
                (frozen_in, frozen),
                (temp_in, temp),
                (angles_in, angles),
            ]
        )
    ]
    for copy in copies:
        copy.start()
    for copy in copies[2:]:
        copy.wait()
    table = jnp.concatenate([angles[...], angles[...]], 1)
    c = jnp.take_along_axis(jnp.broadcast_to(jnp.cos(table), (CX, CY)), ids[0], axis=1)
    s = jnp.take_along_axis(jnp.broadcast_to(jnp.sin(table), (CX, CY)), ids[0], axis=1)
    coarse[0] = c * c - s * s
    coarse[1] = c * s
    coarse[2] = temp[0]
    coarse[3] = -0.5 * frozen[0].astype(F32)
    for copy in copies[:2]:
        copy.wait()
    even = lax.rem(lax.axis_index("narrow"), 2) == 0
    for ref, top in ((face_b, jnp.logical_not(even)), (face_a, even)):
        first = jnp.where(top, 2, 0)
        ref[0:BX] = state[0, first]
        ref[BX : 2 * BX] = state[0, first + 1]
        for k in range(4):
            ref[ROUGH:FACE, k * CY : (k + 1) * CY] = coarse[k]
    core0 = lax.rem(lax.axis_index("wide"), 2) == 0
    for ref, low in ((x_chip, core0), (x_core, jnp.logical_not(core0))):
        for z in range(NPL):
            for at, ch, first, last in ((0, 0, 0, BX - 1), (4, 0, 1, BX - 2), (8, 1, 0, BX - 1)):
                ref[at + z : at + z + 1] = jnp.where(
                    low, state[ch, z, first : first + 1], state[ch, z, last : last + 1]
                )
        for k in range(4):
            ref[12:13, k * CY : (k + 1) * CY] = jnp.where(
                low, coarse[k, 0:1], coarse[k, CX - 1 : CX]
            )
        ref[13:16] = jnp.zeros((3, NY), F32)


def x_sides(x_chip, x_core, rows):
    w = lax.axis_index("wide")
    core0 = lax.rem(w, 2) == 0
    left = jnp.where(core0, x_chip[rows], x_core[rows]) * flag(w > 0)
    right = jnp.where(core0, x_core[rows], x_chip[rows]) * flag(w < NWIDE - 1)
    return left, right


def late_kernel(state, x_chip, x_core, own, late_b, late_a):
    even = lax.rem(lax.axis_index("narrow"), 2) == 0
    left, right = x_sides(x_chip, x_core, slice(0, 8))
    for ref, top in ((late_b, jnp.logical_not(even)), (late_a, even)):
        ref[0:BX] = state[1, jnp.where(top, 3, 0)]
        ref[CORNERS : CORNERS + 1] = jnp.where(top, left[3:4], left[0:1])
        ref[CORNERS + 1 : CORNERS + 2] = jnp.where(top, right[3:4], right[0:1])
        ref[CORNERS + 2 : LATE] = jnp.zeros((LATE - CORNERS - 2, NY), F32)


def widen(ref, at, rough):
    for k in range(CX):
        ref[at, 4 * k : 4 * k + 4] = jnp.broadcast_to(rough[k : k + 1], (4, NY))


def spread_kernel(coarse, fine):
    for k in range(3):
        widen(fine, k, spread(coarse[k]))


def local_terms(c, state, own, fine, fx, fz, known, scale, dxy):
    r0 = pl.multiple_of(c * 8, 8)
    here, at, after = pl.ds(r0, 8), pl.ds(r0 + 8, 8), pl.ds(r0 + 16, 8)
    for z in range(NPL):
        v = own[z, at]
        dx = x_up(v, own[z, after]) - x_down(v, own[z, here])
        dy = y_up(v) - y_down(v)
        m = 1.0 - v * v
        drive = m * (v - 1.5 * (state[1, z, here] + fine[2, here]) * m)
        if z in (0, NPL - 1):
            known[z, here] = drive
            dxy[z // 2, 0, here] = dx
            dxy[z // 2, 1, here] = dy
            continue
        dz = own[z + 1, at] - own[z - 1, at]
        an = weigh(dz, dx, dy, fine[0, here], fine[1, here])
        wt = an * an
        quarter = 0.25 * wt
        fz[z - 1, here] = quarter * dz
        fx[z - 1, here] = quarter * dx
        fy = quarter * dy
        known[z, here] = (y_up(fy) - y_down(fy)) + drive
        scale[z - 1, here] = DT * inverse(wt)


def inside_kernel(state, fine, own, fx, fz, known, scale, dxy):
    for z in range(NPL):
        own[z, 8 : 8 + BX] = state[0, z]

    def chunk(c, carry):
        local_terms(c, state, own, fine, fx, fz, known, scale, dxy)
        return carry

    lax.fori_loop(1, BX // 8 - 1, chunk, 0)


def edge_kernel(
    state, coarse, fine, x_chip, x_core, consts_in, own_in, fx_in, fz_in, known_in, scale_in, dxy_in,
    own, fx, fz, known, scale, dxy, rims, base, consts,
    sem,
):
    fetch = pltpu.make_async_copy(consts_in, consts, sem)
    fetch.start()
    left, right = x_sides(x_chip, x_core, slice(0, 4))
    for z in range(NPL):
        own[z, 7:8] = left[z : z + 1]
        own[z, 8 + BX : 9 + BX] = right[z : z + 1]
    left, right = x_sides(x_chip, x_core, slice(12, 13))
    rows = [side[:, k * CY : (k + 1) * CY] for side in (left, right) for k in (0, 1)]
    rims[...] = spread(jnp.concatenate(rows + rows, 0))
    for c in (0, BX // 8 - 1):
        local_terms(c, state, own, fine, fx, fz, known, scale, dxy)
    t, e = coarse[2], coarse[3]
    row = rows_of(t)
    down, up = [], []
    for k, v in ((2, t), (3, e)):
        before, after = left[:, k * CY : (k + 1) * CY], right[:, k * CY : (k + 1) * CY]
        down.append(jnp.where(row == 0, before, pltpu.roll(v, 1, 0)))
        up.append(jnp.where(row == CX - 1, after, pltpu.roll(v, CX - 1, 0)))
    near = [tuple(down), tuple(up), (y_up(t), y_up(e)), (y_down(t), y_down(e))]
    total = jnp.zeros_like(t)
    for tn, en in near:
        total = total + (1.0 + 0.5 * (e + en)) * (tn - t)
    base[...] = total
    fetch.wait()


def phase_kernel(
    coarse, own, fine, fx12, fz12, known, scale12, dxy, zb, za, base, consts,
    out, edges, spectral, lines,
    sides, halo, fx, fz03, fzout, bent, scale03, change, fresh, sems,
):
    n = lax.axis_index("narrow")
    even = lax.rem(n, 2) == 0
    has_low, has_high = flag(n > 0), flag(n < NNAR - 1)
    for face, at, there in (
        (zb, jnp.where(even, 0, 2), jnp.where(even, has_low, has_high)),
        (za, jnp.where(even, 2, 0), jnp.where(even, has_high, has_low)),
    ):
        for k in range(2):
            halo[at + k, 8 : 8 + BX] = face[k * BX : (k + 1) * BX] * there
    low = jnp.where(even, zb[ROUGH:FACE], za[ROUGH:FACE])
    high = jnp.where(even, za[ROUGH:FACE], zb[ROUGH:FACE])
    for k, v in enumerate((low, low, high, high)):
        wide = spread(v[:, (k % 2) * CY : (k % 2 + 1) * CY])
        widen(sides, k, wide)
        lines[8 + 4 * (k % 2) + 2 * (k // 2) : 9 + 4 * (k % 2) + 2 * (k // 2)] = wide[0:1]
        lines[9 + 4 * (k % 2) + 2 * (k // 2) : 10 + 4 * (k % 2) + 2 * (k // 2)] = wide[CX - 1 : CX]
    t, e = coarse[2], coarse[3]
    still = base[...]
    for v, there in ((low, has_low), (high, has_high)):
        tn, en = v[:, 2 * CY : 3 * CY] * there, v[:, 3 * CY :] * there
        still = still + (1.0 + 0.5 * (e + en)) * (tn - t)
    for z in range(NPL):
        fx[z, 7:8] = jnp.zeros((1, NY), F32)
        fx[z, 8 + BX : 9 + BX] = jnp.zeros((1, NY), F32)
    for z in (1, 2):
        fx[z, 8 : 8 + BX] = fx12[z - 1]
    planes = [(halo, 0), (halo, 1), (own, 0), (own, 1), (own, 2), (own, 3), (halo, 2), (halo, 3)]

    def get(k, rows):
        ref, z = planes[k]
        return ref[z, rows]

    def fluxes(c, carry):
        r0 = pl.multiple_of(c * 8, 8)
        here, at, after = pl.ds(r0, 8), pl.ds(r0 + 8, 8), pl.ds(r0 + 16, 8)
        for side, (zz, there) in enumerate(((0, has_low), (5, has_high))):
            v = get(zz + 1, at)
            dz = get(zz + 2, at) - get(zz, at)
            dx = x_up(v, get(zz + 1, after)) - x_down(v, get(zz + 1, here))
            dy = y_up(v) - y_down(v)
            an = weigh(dz, dx, dy, sides[2 * side, here], sides[2 * side + 1, here])
            fzout[side, here] = (0.25 * there) * (an * an * dz)
        for side, z in enumerate((0, NPL - 1)):
            dz = get(z + 3, at) - get(z + 1, at)
            dx, dy = dxy[side, 0, here], dxy[side, 1, here]
            an = weigh(dz, dx, dy, fine[0, here], fine[1, here])
            wt = an * an
            quarter = 0.25 * wt
            fz03[side, here] = quarter * dz
            fx[z, at] = quarter * dx
            fy = quarter * dy
            bent[side, here] = known[z, here] + (y_up(fy) - y_down(fy))
            scale03[side, here] = DT * inverse(wt)
        return carry

    lax.fori_loop(0, BX // 8, fluxes, 0)

    for side in range(2):
        for row in (0, BX - 1):
            fzout[side, row : row + 1] = jnp.zeros((1, NY), F32)
    flux_z = [(fzout, 0), (fz03, 0), (fz12, 0), (fz12, 1), (fz03, 1), (fzout, 1)]
    rest = [(bent, 0), (known, 1), (known, 2), (bent, 1)]
    scales = [(scale03, 0), (scale12, 0), (scale12, 1), (scale03, 1)]

    def store(c):
        rows = pl.ds(8 * c, 8)
        return pltpu.make_async_copy(fresh.at[:, rows], out.at[0, :, rows], sems.at[c])

    for c in range(BX // 8):
        here, at, after = pl.ds(8 * c, 8), pl.ds(8 * c + 8, 8), pl.ds(8 * c + 16, 8)
        total = jnp.zeros((8, NY), F32)
        for z in range(NPL):
            p, f = own[z, at], fx[z, at]
            spread_z = flux_z[z + 2][0][flux_z[z + 2][1], here] - flux_z[z][0][flux_z[z][1], here]
            spread_x = x_up(f, fx[z, after]) - x_down(f, fx[z, here])
            factor = scales[z][0][scales[z][1], here]
            rise = factor * (rest[z][0][rest[z][1], here] + spread_z + spread_x)
            total = total + rise
            if c in (0, BX // 8 - 1):
                edges[z, 0 if c == 0 else 1] = p + rise
                row, line = (0, z) if c == 0 else (7, NPL + z)
                lines[line : line + 1] = factor[row : row + 1]
            else:
                fresh[z, here] = p + rise
        total = total + pltpu.roll(total, 1, 0)
        total = total + pltpu.roll(total, 2, 0)
        change[2 * c : 2 * c + 1] = total[3:4]
        change[2 * c + 1 : 2 * c + 2] = total[7:8]
        if 0 < c < BX // 8 - 1:
            store(c).start()
    spectral[...] = dot(still, consts[SY_AT]) + dot(change[...], consts[MEAN_AT])
    for c in range(1, BX // 8 - 1):
        store(c).wait()


def rim_kernel(
    own, rims, x_chip, x_core, zb, za, lb, la, edges, spectral_in, lines, consts,
    tiles, spectral, far,
):
    n, w = lax.axis_index("narrow"), lax.axis_index("wide")
    even = lax.rem(n, 2) == 0
    has_left, has_right = flag(w > 0), flag(w < NWIDE - 1)
    has_low, has_high = flag(n > 0), flag(n < NNAR - 1)
    inner = x_sides(x_chip, x_core, slice(4, 8))

    def beyond(b, a, rows, high):
        if high:
            return jnp.where(even, a[rows], b[rows]) * has_high
        return jnp.where(even, b[rows], a[rows]) * has_low

    def corner(high, s):
        return beyond(lb, la, slice(CORNERS + s, CORNERS + s + 1), high)

    def outer(high, plane, x):
        return beyond(zb, za, slice(plane * BX + x, plane * BX + x + 1), high)

    rim = (7, 8 + BX)
    values = [[], [], [], [], []]
    for s in range(2):
        for z in range(NPL):
            at = slice(rim[s], rim[s] + 1)
            here = own[z, at]
            below = own[z - 1, at] if z > 0 else corner(False, s)
            above = own[z + 1, at] if z < NPL - 1 else corner(True, s)
            side = inner[s][z : z + 1]
            x_lo, x_hi = (own[z, 7 + BX : 8 + BX], side) if s else (side, own[z, 8:9])
            for rows, v in zip(values, (here, below, above, x_lo, x_hi)):
                rows.append(v)
    for high in (False, True):
        for s in range(2):
            x, near = (BX - 1, BX - 2) if s else (0, 1)
            mine = own[NPL - 1 if high else 0, 8 + x : 9 + x]
            here, behind = outer(high, 0 if high else 1, x), outer(high, 1 if high else 0, x)
            beside, past = outer(high, 0 if high else 1, near), corner(high, s)
            below, above = (mine, behind) if high else (behind, mine)
            x_lo, x_hi = (beside, past) if s else (past, beside)
            for rows, v in zip(values, (here, below, above, x_lo, x_hi)):
                rows.append(v)
    here, below, above, x_lo, x_hi = (
        jnp.concatenate(rows + [jnp.zeros((4, NY), F32)], 0) for rows in values
    )
    c2, s2 = (
        jnp.concatenate(
            [jnp.broadcast_to(rims[k : k + 1], (NPL, NY)), jnp.broadcast_to(rims[k + 2 : k + 3], (NPL, NY)),
             lines[8 + 4 * k : 12 + 4 * k], jnp.zeros((4, NY), F32)], 0,
        )
        for k in (0, 1)
    )
    dz, dx, dy = above - below, x_hi - x_lo, y_up(here) - y_down(here)
    an = weigh(dz, dx, dy, c2, s2)
    quarter = 0.25 * (an * an)
    row = rows_of(here[0:8])
    x_part = quarter[0:8] * dx[0:8] * jnp.where(row < NPL, -has_left, has_right)
    z_flux = quarter[8:16] * dz[8:16]
    z_part = jnp.zeros((8, NY), F32)
    for high in (False, True):
        for s in range(2):
            line = z_flux[2 * high + s : 2 * high + s + 1]
            line = line * has_high if high else -has_low * line
            z_part = jnp.where(row == NPL * s + (NPL - 1 if high else 0), line, z_part)
    rise = lines[0:8] * (x_part + z_part)
    for c in range(2):
        for z in range(NPL):
            add = rise[NPL * c + z : NPL * c + z + 1]
            tiles[z, c] = edges[z, c] + jnp.where(row == 7 * c, add, 0.0)
    sums = [jnp.sum(rise[NPL * c : NPL * (c + 1)], axis=0, keepdims=True) for c in range(2)]
    more = dot(jnp.concatenate(sums + [jnp.zeros((14, NY), F32)], 0), consts[MEAN_AT])
    first = rows_of(spectral_in)
    moved = spectral_in[...] + jnp.where(
        first == 0, more[0:1], jnp.where(first == CX - 1, more[1:2], 0.0)
    )
    spectral[...] = moved
    core0 = lax.rem(w, 2) == 0
    far[...] = jnp.where(core0, moved[0:8], pltpu.roll(moved[8:16], 4, 0))


def solute_kernel(state, own, x_chip, x_core, zb, za, lb, la, tiles, done, out, sown, fresh, grown, sems):
    within = pl.ds(8, BX - 16)
    fetch = pltpu.make_async_copy(done.at[0, :, within], fresh.at[:, within], sems.at[0])
    fetch.start()
    ends = [
        pltpu.make_async_copy(tiles.at[:, c], out.at[0, :, pl.ds((BX - 8) * c, 8)], sems.at[9 + c])
        for c in range(2)
    ]
    for copy in ends:
        copy.start()
    for c in range(2):
        fresh[:, (BX - 8) * c : (BX - 8) * c + 8] = tiles[:, c]
    n = lax.axis_index("narrow")
    even = lax.rem(n, 2) == 0
    left, right = x_sides(x_chip, x_core, slice(8, 12))
    has_low, has_high = flag(n > 0), flag(n < NNAR - 1)
    for z in range(NPL):
        sown[z, 8 : 8 + BX] = state[1, z]
        sown[z, 7:8] = left[z : z + 1]
        sown[z, 8 + BX : 9 + BX] = right[z : z + 1]
    fetch.wait()

    def step(c, carry):
        r0 = pl.multiple_of(c * 8, 8)
        here, at, after = pl.ds(r0, 8), pl.ds(r0 + 8, 8), pl.ds(r0 + 16, 8)

        beyond = pl.ds(pl.multiple_of(r0 + BX, 8), 8)
        ps = (
            [has_low * jnp.where(even, zb[beyond], za[beyond])]
            + [own[z, at] for z in range(NPL)]
            + [has_high * jnp.where(even, za[here], zb[here])]
        )
        ss = (
            [has_low * jnp.where(even, lb[here], la[here])]
            + [sown[z, at] for z in range(NPL)]
            + [has_high * jnp.where(even, la[here], lb[here])]
        )
        for z in range(NPL):
            p, s = ps[z + 1], ss[z + 1]
            q = 0.55 - 0.25 * p
            near = [
                (ps[z], ss[z]),
                (ps[z + 2], ss[z + 2]),
                (x_up(p, own[z, after]), x_up(s, sown[z, after])),
                (x_down(p, own[z, here]), x_down(s, sown[z, here])),
                (y_up(p), y_up(s)),
                (y_down(p), y_down(s)),
            ]
            total = jnp.zeros_like(p)
            for pn, sn in near:
                total = total + (q - 0.25 * pn) * (sn - s)
            grown[z, here] = s + DT * total + (0.5 + 0.425 * s) * (fresh[z, here] - p)
        store(c).start()
        return carry

    def store(c):
        rows = pl.ds(pl.multiple_of(c * 8, 8), 8)
        return pltpu.make_async_copy(grown.at[:, rows], out.at[1, :, rows], sems.at[1 + c])

    lax.fori_loop(0, BX // 8, step, 0)
    for c in range(BX // 8):
        store(c).wait()
    for copy in ends:
        copy.wait()


def chip_kernel(mine, partner, here, message):
    core = lax.rem(lax.axis_index("wide"), 2)
    first, second = pl.ds(pl.multiple_of(core * CX, 8), CX), pl.ds(pl.multiple_of((1 - core) * CX, 8), CX)
    here[first] = mine[...]
    here[second] = partner[...]
    message[0:CX] = mine[...]
    near = jnp.where(core == 0, partner[0:8], pltpu.roll(partner[8:16], 4, 0))
    message[CX : CX + 8] = near
def window_kernel(here, across, shared, view):
    w = lax.axis_index("wide")
    core, chip = lax.rem(w, 2), lax.div(w, 2)
    has_before, has_after = flag(chip > 0), flag(chip < NWIDE // 2 - 1)

    @pl.when(core == 0)
    def _():
        view[0:4] = across[CX : CX + 4] * has_before
        view[4:20] = across[0:CX] * has_before
        view[20:52] = here[...]
        view[52:56] = shared[0:4] * has_after

    @pl.when(core == 1)
    def _():
        view[0:4] = shared[0:4] * has_before
        view[4:36] = here[...]
        view[36:56] = across[0:20] * has_after


def solve_kernel(planes, coarse, consts, out, modes, rows):
    n, w = lax.axis_index("narrow"), lax.axis_index("wide")
    has_left, has_right = flag(w > 0), flag(w < NWIDE - 1)
    half = NNAR // 2
    folded = [
        [planes[m] + planes[NNAR - 1 - m] for m in range(half)],
        [planes[m] - planes[NNAR - 1 - m] for m in range(half)],
    ]
    for k in range(NNAR):
        total = float(SZ[k, 0]) * folded[k % 2][0]
        for m in range(1, half):
            total = total + float(SZ[k, m]) * folded[k % 2][m]
        modes[k * 56 : (k + 1) * 56] = total
    f = [modes[pl.ds(j, 8, stride=56), :] for j in range(56)]
    inv_of = [consts[INV_AT + 8 * i : INV_AT + 8 * i + 8] for i in range(SUBX)]
    link = [KBAR * v for v in inv_of]

    def solve(order, keep):
        h = [inv_of[0] * f[order[0]]]
        for i in range(1, SUBX):
            h.append(inv_of[i] * f[order[i]] + link[i] * h[-1])
        x = h[-1]
        found = {order[-1]: x}
        for i in range(SUBX - 2, -1, -1):
            if order[i] not in keep:
                break
            x = h[i] + link[i] * x
            found[order[i]] = x
        return found

    mine = solve(list(range(16, 40)), set(range(20, 40)))
    lower = solve(list(range(0, 24)), set(range(20, 24)))
    upper = solve(list(range(55, 31, -1)), set(range(32, 36)))
    weight = consts[pl.ds(pl.multiple_of(SZ_AT + 8 * n, 8), 8)]
    for j in range(CX):
        x = mine[20 + j]
        if 20 + j in lower:
            x = x + has_left * lower[20 + j]
        if 20 + j in upper:
            x = x + has_right * upper[20 + j]
        rows[j : j + 1] = jnp.sum(x * weight, axis=0, keepdims=True)
    out[0] = coarse[2] + dot(rows[...], consts[SY_AT])


def kernel(body, outs, scratch=(), far=(), far_outs=(), aliases=None, mib=16):
    many = isinstance(outs, (list, tuple))

    def call(*args):
        return pl.pallas_call(
            body,
            out_shape=outs,
            in_specs=[HBM if i in far else VMEM for i in range(len(args))],
            out_specs=[HBM if i in far_outs else VMEM for i in range(len(outs))] if many else (HBM if far_outs else VMEM),
            input_output_aliases=aliases or {},
            scratch_shapes=list(scratch),
            compiler_params=params(mib),
            name=body.__name__,
        )(*args)

    return call


def afar(v):
    return pltpu.with_memory_space_constraint(v, pltpu.HBM)


def on_device(state_in, ids, frozen, temp, angles):
    inputs = [afar(v) for v in (state_in, ids, frozen, temp, angles.reshape(1, -1))]
    face_b, face_a, to_chip, to_core, state, coarse = kernel(
        stage_kernel,
        [sds(FACE, NY)] * 2 + [sds(16, NY)] * 2 + [sds(2, NPL, BX, NY), sds(4, CX, CY)],
        [
            pltpu.VMEM((1, CX, CY), jnp.int32),
            pltpu.VMEM((1, CX, CY), jnp.int32),
            pltpu.VMEM((1, CX, CY), F32),
            pltpu.VMEM((1, 64), F32),
            pltpu.SemaphoreType.DMA((6,)),
        ],
        far=range(5),
    )(*inputs)
    zb = lax.ppermute(face_b, "narrow", PAIR_B)
    za = lax.ppermute(face_a, "narrow", PAIR_A)
    x_chip = lax.ppermute(to_chip, "wide", CHIPS)
    x_core = lax.ppermute(to_core, "wide", CORES)
    fine = kernel(spread_kernel, sds(3, BX, NY))(coarse)
    shapes = [
        sds(NPL, BX + 16, NY), sds(2, BX, NY), sds(2, BX, NY), sds(NPL, BX, NY), sds(2, BX, NY),
        sds(2, 2, BX, NY),
    ]
    inside = kernel(inside_kernel, shapes)(state, fine)
    late_b, late_a = kernel(late_kernel, [sds(LATE, NY)] * 2)(state, x_chip, x_core, inside[0])
    lb = lax.ppermute(late_b, "narrow", PAIR_B)
    la = lax.ppermute(late_a, "narrow", PAIR_A)
    own, fx12, fz12, known, scale12, dxy, rims, base, consts = kernel(
        edge_kernel,
        shapes + [sds(8, NY), sds(CX, CY), sds(*CONSTS.shape)],
        [pltpu.SemaphoreType.DMA],
        far=(5,),
        aliases={6 + i: i for i in range(6)},
    )(state, coarse, fine, x_chip, x_core, afar(jnp.asarray(CONSTS)), *inside)
    result, edges, spectral, lines = kernel(
        phase_kernel,
        [sds(2, NPL, BX, NY), sds(NPL, 2, 8, NY), sds(CX, CY), sds(16, NY)],
        [
            pltpu.VMEM((4, BX, NY), F32),
            pltpu.VMEM((4, BX + 16, NY), F32),
            pltpu.VMEM((NPL, BX + 16, NY), F32),
            pltpu.VMEM((2, BX, NY), F32),
            pltpu.VMEM((2, BX, NY), F32),
            pltpu.VMEM((2, BX, NY), F32),
            pltpu.VMEM((2, BX, NY), F32),
            pltpu.VMEM((CX, NY), F32),
            pltpu.VMEM((NPL, BX, NY), F32),
            pltpu.SemaphoreType.DMA((BX // 8,)),
        ],
        far_outs=(0,),
    )(coarse, own, fine, fx12, fz12, known, scale12, dxy, zb, za, base, consts)
    tiles, spectral, far = kernel(
        rim_kernel, [sds(NPL, 2, 8, NY), sds(CX, CY), sds(8, CY)]
    )(own, rims, x_chip, x_core, zb, za, lb, la, edges, spectral, lines, consts)
    partner = lax.ppermute(spectral, "wide", CORES)
    shared = lax.ppermute(far, "wide", NEXT_CHIPS)
    here, message = kernel(chip_kernel, [sds(2 * CX, CY), sds(CX + 8, CY)])(spectral, partner)
    across = lax.ppermute(message, "wide", CHIPS)
    view = kernel(window_kernel, sds(56, CY))(here, across, shared)
    planes = lax.all_to_all(jnp.broadcast_to(view[None], (NNAR, 56, CY)), "narrow", 0, 0)
    state_new = kernel(
        solute_kernel,
        sds(2, NPL, BX, NY),
        [
            pltpu.VMEM((NPL, BX + 16, NY), F32),
            pltpu.VMEM((NPL, BX, NY), F32),
            pltpu.VMEM((NPL, BX, NY), F32),
            pltpu.SemaphoreType.DMA((3 + BX // 8,)),
        ],
        far=(9,),
        far_outs=(0,),
        aliases={9: 0},
    )(state, own, x_chip, x_core, zb, za, lb, la, tiles, result)
    adjusted = kernel(
        solve_kernel,
        sds(1, CX, CY),
        [pltpu.VMEM((NNAR * 56, CY), F32), pltpu.VMEM((CX, CY), F32)],
    )(planes, coarse, consts)
    return state_new, adjusted


def solution(mesh):
    return jax.shard_map(
        on_device,
        mesh=mesh,
        in_specs=(
            P(None, "narrow", "wide", None),
            P("narrow", "wide", None),
            P("narrow", "wide", None),
            P("narrow", "wide", None),
            P(),
        ),
        out_specs=(P(None, "narrow", "wide", None), P("narrow", "wide", None)),
        check_vma=False,
    )
```

time: 50.8 us -> 45.9 us (0.904)
  the two profiles are of different devices: /device:TPU:2 before, /device:TPU:8 now
where the time goes in v3:
time: 45.9 us; the launch traced here: 45.3 us
  starting transfers between devices  18.3 us (40%)
  waiting for transfers between devices  15.2 us (33%)
  Pallas kernels  10.3 us (22%)
  between operations  0.73 us (2%)
  local copies, waits for them, and re-layouts  0.71 us (2%)
    pallas_call x11, Pallas kernels, call(): pl.pallas_call(body, out_shape=outs, in_specs=[HBM if i in far else VMEM...  10.3 us
    ppermute x1, starting transfers between devices, on_device(): x_chip = lax.ppermute(to_chip, 'wide', CHIPS)  5.8 us
    all_to_all x1, waiting for transfers between devices, on_device(): lax.all_to_all(jnp.broadcast_to(view[None], (NNAR, 56, CY)), 'narrow', 0, 0)  5.6 us
    ppermute x1, starting transfers between devices, on_device(): zb = lax.ppermute(face_b, 'narrow', PAIR_B)  4.58 us
    ppermute x1, waiting for transfers between devices, on_device(): lb = lax.ppermute(late_b, 'narrow', PAIR_B)  4.47 us
    all_to_all x1, starting transfers between devices, on_device(): lax.all_to_all(jnp.broadcast_to(view[None], (NNAR, 56, CY)), 'narrow', 0, 0)  3.4 us
    ppermute x1, waiting for transfers between devices, on_device(): shared = lax.ppermute(far, 'wide', NEXT_CHIPS)  3.37 us
    ppermute x1, starting transfers between devices, on_device(): across = lax.ppermute(message, 'wide', CHIPS)  2.65 us
  transfers between devices with their start and end apart: 10, of which 5 were waited for; matrix products, arithmetic and copies ran while one was open for 0% of the time, Pallas kernels for 17%

profile of v3, /device:TPU:8, one launch (start us, length us, event | category | flops | bytes accessed | tf_op | source)
XLA Modules:
  0.0 45.3 jit_solution(7956879661968285257)
XLA Ops:
  0.6 1.4 %stage_kernel.1 = (f32[144,512]{1,0:T(8,128)S(1)}, f32[144,512]{1,0:T(8,128)S(1)}, f32[16,512]{1,0:T(8,128)S(1)}, f32[16,512]{1,0:T(8,128)S(1)}, f32[2,4,64,512]...) custom-call(f32[2,4,64,512]{3,2,1,0:T(8,128)} %state_in.1, s32[1,16,128]{2,1,0:T(8,128)} %ids_in.1, s32[1,16,128]{2,1,0:T(8,128)} %frozen_in.1, ...), custom_call_target="tpu_custom_call" | custom-call | tf_op jit(solution)/shard_map/stage_kernel/pallas_call | solution.py:601
  2.0 4.6 %collective-permute-start.2 = (f32[144,512]{1,0:T(8,128)S(1)}, f32[144,512]{1,0:T(8,128)S(1)}, u32[]{:S(2)}, u32[]{:S(2)}) collective-permute-start(f32[144,512]{1,0:T(8,128)S(1)} %get-tuple-element.45), channel_id=1, source_target_pairs={{0,224},{32,64},{64,32},{96,128},{128,96},{160,192},{192,160},{224... | collective-permute-start | bytes 884744 | tf_op jit(solution)/shard_map/ppermute | solution.py:633
  6.6 0.0 collective-permute-start.3
  6.6 5.8 %collective-permute-start = (f32[16,512]{1,0:T(8,128)S(1)}, f32[16,512]{1,0:T(8,128)S(1)}, u32[]{:S(2)}, u32[]{:S(2)}) collective-permute-start(f32[16,512]{1,0:T(8,128)S(1)} %get-tuple-element.36), channel_id=1, source_target_pairs={{0,31},{1,2},{2,1},{3,4},{4,3},{5,6},{6,5},{7,8},{8,7},{9,10},{10,... | collective-permute-start | bytes 98312 | tf_op jit(solution)/shard_map/ppermute | solution.py:635
  12.4 0.0 collective-permute-start.1
  12.4 0.1 spread_kernel.1.fine
  12.6 1.2 %inside_kernel.1 = (f32[4,80,512]{2,1,0:T(8,128)S(1)}, f32[2,64,512]{2,1,0:T(8,128)S(1)}, f32[2,64,512]{2,1,0:T(8,128)S(1)}, f32[4,64,512]{2,1,0:T(8,128)S(1)}, ...) custom-call(f32[2,4,64,512]{3,2,1,0:T(8,128)S(1)} %get-tuple-element.34.state, f32[3,64,512]{2,1,0:T(8,128)S(1)} %spread_kernel.1.fine), custom_call_target="tpu_custom_call" | custom-call | tf_op jit(solution)/shard_map/inside_kernel/pallas_call | solution.py:601
  13.8 0.6 %collective-permute-done.x_chip = f32[16,512]{1,0:T(8,128)S(1)} collective-permute-done((f32[16,512]{1,0:T(8,128)S(1)}, f32[16,512]{1,0:T(8,128)S(1)}, u32[]{:S(2)}, u32[]{:S(2)}) %collective-permute-start) | collective-permute-done | bytes 32800 | tf_op jit(solution)/shard_map/ppermute | solution.py:635
  14.4 0.0 collective-permute-done.1.x_core
  14.4 0.6 %collective-permute-start.4 = (f32[72,512]{1,0:T(8,128)S(1)}, f32[72,512]{1,0:T(8,128)S(1)}, u32[]{:S(2)}, u32[]{:S(2)}) collective-permute-start(f32[72,512]{1,0:T(8,128)S(1)} %get-tuple-element.47), channel_id=1, source_target_pairs={{0,224},{32,64},{64,32},{96,128},{128,96},{160,192},{192,160},{224... | collective-permute-start | bytes 442376 | tf_op jit(solution)/shard_map/ppermute | solution.py:644
  15.0 1.0 %collective-permute-start.5 = (f32[72,512]{1,0:T(8,128)S(1)}, f32[72,512]{1,0:T(8,128)S(1)}, u32[]{:S(2)}, u32[]{:S(2)}) collective-permute-start(f32[72,512]{1,0:T(8,128)S(1)} %get-tuple-element.48), channel_id=1, source_target_pairs={{0,32},{32,0},{64,96},{96,64},{128,160},{160,128},{192,224},{224,1... | collective-permute-start | bytes 442376 | tf_op jit(solution)/shard_map/ppermute | solution.py:645
  16.0 1.0 %edge_kernel.1 = (f32[4,80,512]{2,1,0:T(8,128)S(1)}, f32[2,64,512]{2,1,0:T(8,128)S(1)}, f32[2,64,512]{2,1,0:T(8,128)S(1)}, f32[4,64,512]{2,1,0:T(8,128)S(1)}, f3...) custom-call(f32[2,4,64,512]{3,2,1,0:T(8,128)S(1)} %get-tuple-element, ...), custom_call_target="tpu_custom_call", output_to_operand_aliasing={{0}: (6, {}), {1}: (7, {}), {2}: (8, {}), {3}: (9, {}), {4}... | custom-call | tf_op jit(solution)/shard_map/edge_kernel/pallas_call | solution.py:601
  17.0 0.0 collective-permute-done.2.zb
  17.0 0.0 collective-permute-done.3.za
  17.1 2.3 %phase_kernel.1 = (f32[2,4,64,512]{3,2,1,0:T(8,128)}, f32[4,2,8,512]{3,2,1,0:T(8,128)S(1)}, f32[16,128]{1,0:T(8,128)S(1)}, f32[16,512]{1,0:T(8,128)S(1)}) custom-call(f32[4,16,128]{2,1,0:T(8,128)S(1)} %get-tuple-element.35.coarse, f32[4,80,512]{2,1,0:T(8,128)S(1)} %get-tuple-element.44.own, f32[3,64,512]{2,1,0:T(8,128)S(1)} %spread_kernel.1.fine, ...), custom_call_target="tpu_custom_call" | custom-call | tf_op jit(solution)/shard_map/phase_kernel/pallas_call | solution.py:601
  19.4 4.5 %collective-permute-done.4.lb = f32[72,512]{1,0:T(8,128)S(1)} collective-permute-done((f32[72,512]{1,0:T(8,128)S(1)}, f32[72,512]{1,0:T(8,128)S(1)}, u32[]{:S(2)}, u32[]{:S(2)}) %collective-permute-start.4) | collective-permute-done | bytes 147488 | tf_op jit(solution)/shard_map/ppermute | solution.py:644
  23.8 0.0 collective-permute-done.5.la
  23.8 0.3 rim_kernel.1
  24.2 0.1 collective-permute-start.6
  24.3 1.2 %collective-permute-done.6.partner = f32[16,128]{1,0:T(8,128)S(1)} collective-permute-done((f32[16,128]{1,0:T(8,128)S(1)}, f32[16,128]{1,0:T(8,128)S(1)}, u32[]{:S(2)}, u32[]{:S(2)}) %collective-permute-start.6) | collective-permute-done | bytes 8224 | tf_op jit(solution)/shard_map/ppermute | solution.py:673
  25.4 2.6 %collective-permute-start.7 = (f32[24,128]{1,0:T(8,128)S(1)}, f32[24,128]{1,0:T(8,128)S(1)}, u32[]{:S(2)}, u32[]{:S(2)}) collective-permute-start(f32[24,128]{1,0:T(8,128)S(1)} %get-tuple-element.64), channel_id=1, source_target_pairs={{0,31},{1,2},{2,1},{3,4},{4,3},{5,6},{6,5},{7,8},{8,7},{9,10},{10,... | collective-permute-start | bytes 36872 | tf_op jit(solution)/shard_map/ppermute | solution.py:676
  28.1 0.2 collective-permute-start.8
  28.3 3.4 %collective-permute-done.8.shared = f32[8,128]{1,0:T(8,128)S(1)} collective-permute-done((f32[8,128]{1,0:T(8,128)S(1)}, f32[8,128]{1,0:T(8,128)S(1)}, u32[]{:S(2)}, u32[]{:S(2)}) %collective-permute-start.8) | collective-permute-done | bytes 4128 | tf_op jit(solution)/shard_map/ppermute | solution.py:674
  31.7 0.0 collective-permute-done.7.across
  31.7 0.7 %broadcast_in_dim.2 = f32[8,56,128]{2,1,0:T(8,128)} broadcast(f32[56,128]{1,0:T(8,128)S(1)} %window_kernel.1), dimensions={1,2} | broadcast | bytes 258048 | tf_op jit(solution)/shard_map/broadcast_in_dim | solution.py:678
  32.4 3.4 %all-to-all-start = ((f32[8,56,128]{2,1,0:T(8,128)}), f32[8,56,128]{2,1,0:T(8,128)S(1)}, u32[]{:S(2)}, u32[]{:S(2)}) async-start(f32[8,56,128]{2,1,0:T(8,128)} %broadcast_in_dim.2), calls=%async_computation | async-start | bytes 458752 | tf_op jit(solution)/shard_map/all_to_all | solution.py:678
  35.8 2.9 %solute_kernel.1 = f32[2,4,64,512]{3,2,1,0:T(8,128)} custom-call(f32[2,4,64,512]{3,2,1,0:T(8,128)S(1)} %get-tuple-element.34.state, f32[4,80,512]{2,1,0:T(8,128)S(1)} %get-tuple-element.44.own, f32[16,512]{1,0:T(8,128)S(1)} %collective-permute-done.x_chip, f32[16,512]{1,0:T(8,128)S(1)} %collective-permute-done.1.x_core, ...), custom_call_target="tpu_custom_call", output_to_operand_aliasing={{}: (9, {})} | custom-call | tf_op jit(solution)/shard_map/solute_kernel/pallas_call | solution.py:601
  38.8 5.6 %all-to-all-done.planes = f32[8,56,128]{2,1,0:T(8,128)S(1)} async-done(((f32[8,56,128]{2,1,0:T(8,128)}), f32[8,56,128]{2,1,0:T(8,128)S(1)}, u32[]{:S(2)}, u32[]{:S(2)}) %all-to-all-start) | async-done | bytes 229408 | tf_op jit(solution)/shard_map/all_to_all | solution.py:678
  44.4 0.9 %solve_kernel.1 = f32[1,16,128]{2,1,0:T(8,128)} custom-call(f32[8,56,128]{2,1,0:T(8,128)S(1)} %all-to-all-done.planes, f32[4,16,128]{2,1,0:T(8,128)S(1)} %get-tuple-element.35.coarse, f32[896,128]{1,0:T(8,128)S(1)} %get-tuple-element.56.consts), custom_call_target="tpu_custom_call" | custom-call | tf_op jit(solution)/shard_map/solve_kernel/pallas_call | solution.py:601
  (3 shorter events, 0.0 us)
Async XLA Ops:
  2.0 15.0 %collective-permute-start.2 = (f32[144,512]{1,0:T(8,128)S(1)}, f32[144,512]{1,0:T(8,128)S(1)}, u32[]{:S(2)}, u32[]{:S(2)}) collective-permute-start(f32[144,512]{1,0:T(8,128)S(1)} %get-tuple-element.45), channel_id=1, source_target_pairs={{0,224},{32,64},{64,32},{96,128},{128,96},{160,192},{192,160},{224... | collective-permute-start | bytes 884744 | tf_op jit(solution)/shard_map/ppermute | solution.py:633
  6.6 10.4 %collective-permute-start.3 = (f32[144,512]{1,0:T(8,128)S(1)}, f32[144,512]{1,0:T(8,128)S(1)}, u32[]{:S(2)}, u32[]{:S(2)}) collective-permute-start(f32[144,512]{1,0:T(8,128)S(1)} %get-tuple-element.46), channel_id=1, source_target_pairs={{0,32},{32,0},{64,96},{96,64},{128,160},{160,128},{192,224},{224,1... | collective-permute-start | bytes 884744 | tf_op jit(solution)/shard_map/ppermute | solution.py:634
  6.6 7.7 %collective-permute-start = (f32[16,512]{1,0:T(8,128)S(1)}, f32[16,512]{1,0:T(8,128)S(1)}, u32[]{:S(2)}, u32[]{:S(2)}) collective-permute-start(f32[16,512]{1,0:T(8,128)S(1)} %get-tuple-element.36), channel_id=1, source_target_pairs={{0,31},{1,2},{2,1},{3,4},{4,3},{5,6},{6,5},{7,8},{8,7},{9,10},{10,... | collective-permute-start | bytes 98312 | tf_op jit(solution)/shard_map/ppermute | solution.py:635
  12.4 1.9 %collective-permute-start.1 = (f32[16,512]{1,0:T(8,128)S(1)}, f32[16,512]{1,0:T(8,128)S(1)}, u32[]{:S(2)}, u32[]{:S(2)}) collective-permute-start(f32[16,512]{1,0:T(8,128)S(1)} %get-tuple-element.37), channel_id=1, source_target_pairs={{0,1},{1,0},{2,3},{3,2},{4,5},{5,4},{6,7},{7,6},{8,9},{9,8},{10,11... | collective-permute-start | bytes 98312 | tf_op jit(solution)/shard_map/ppermute | solution.py:636
  14.4 9.4 %collective-permute-start.4 = (f32[72,512]{1,0:T(8,128)S(1)}, f32[72,512]{1,0:T(8,128)S(1)}, u32[]{:S(2)}, u32[]{:S(2)}) collective-permute-start(f32[72,512]{1,0:T(8,128)S(1)} %get-tuple-element.47), channel_id=1, source_target_pairs={{0,224},{32,64},{64,32},{96,128},{128,96},{160,192},{192,160},{224... | collective-permute-start | bytes 442376 | tf_op jit(solution)/shard_map/ppermute | solution.py:644
  15.0 8.9 %collective-permute-start.5 = (f32[72,512]{1,0:T(8,128)S(1)}, f32[72,512]{1,0:T(8,128)S(1)}, u32[]{:S(2)}, u32[]{:S(2)}) collective-permute-start(f32[72,512]{1,0:T(8,128)S(1)} %get-tuple-element.48), channel_id=1, source_target_pairs={{0,32},{32,0},{64,96},{96,64},{128,160},{160,128},{192,224},{224,1... | collective-permute-start | bytes 442376 | tf_op jit(solution)/shard_map/ppermute | solution.py:645
  24.2 1.3 %collective-permute-start.6 = (f32[16,128]{1,0:T(8,128)S(1)}, f32[16,128]{1,0:T(8,128)S(1)}, u32[]{:S(2)}, u32[]{:S(2)}) collective-permute-start(f32[16,128]{1,0:T(8,128)S(1)} %get-tuple-element.62.mine), channel_id=1, source_target_pairs={{0,1},{1,0},{2,3},{3,2},{4,5},{5,4},{6,7},{7,6},{8,9},{9,8},{10,11... | collective-permute-start | bytes 24584 | tf_op jit(solution)/shard_map/ppermute | solution.py:673
  25.4 6.3 %collective-permute-start.7 = (f32[24,128]{1,0:T(8,128)S(1)}, f32[24,128]{1,0:T(8,128)S(1)}, u32[]{:S(2)}, u32[]{:S(2)}) collective-permute-start(f32[24,128]{1,0:T(8,128)S(1)} %get-tuple-element.64), channel_id=1, source_target_pairs={{0,31},{1,2},{2,1},{3,4},{4,3},{5,6},{6,5},{7,8},{8,7},{9,10},{10,... | collective-permute-start | bytes 36872 | tf_op jit(solution)/shard_map/ppermute | solution.py:676
  28.1 3.6 %collective-permute-start.8 = (f32[8,128]{1,0:T(8,128)S(1)}, f32[8,128]{1,0:T(8,128)S(1)}, u32[]{:S(2)}, u32[]{:S(2)}) collective-permute-start(f32[8,128]{1,0:T(8,128)S(1)} %get-tuple-element.65), channel_id=1, source_target_pairs={{0,30},{1,3},{2,0},{3,5},{4,2},{5,7},{6,4},{7,9},{8,6},{9,11},{10,... | collective-permute-start | bytes 12296 | tf_op jit(solution)/shard_map/ppermute | solution.py:674
  32.4 12.0 %all-to-all-start = ((f32[8,56,128]{2,1,0:T(8,128)}), f32[8,56,128]{2,1,0:T(8,128)S(1)}, u32[]{:S(2)}, u32[]{:S(2)}) async-start(f32[8,56,128]{2,1,0:T(8,128)} %broadcast_in_dim.2), calls=%async_computation | async-start | bytes 458752 | tf_op jit(solution)/shard_map/all_to_all | solution.py:678

commit v4 on v3

--- a/solution.py
+++ b/solution.py
@@ -53,19 +53,44 @@
 INVERSE = elimination()
 
 
-CONSTS = np.concatenate([SY, MEAN_Y, INVERSE.reshape(-1, CY), SZ_ROWS.reshape(-1, CY)]).astype(np.float32)
+LINK = KBAR * INVERSE
+PASS = np.prod(LINK[4:20], axis=0)
+MEET = 1.0 / (1.0 - LINK[11] ** 2)
+
+CONSTS = np.concatenate(
+    [SY, MEAN_Y, INVERSE.reshape(-1, CY), SZ_ROWS.reshape(-1, CY), PASS, MEET]
+).astype(np.float32)
 SY_AT, MEAN_AT, INV_AT, SZ_AT = slice(0, 128), slice(128, 640), 640, 640 + 8 * SUBX
-
-
-def wide_ring(k):
-    return [(i, (i + k) % NWIDE) for i in range(NWIDE)]
-
-
+PASS_AT = slice(SZ_AT + 64, SZ_AT + 72)
+MEET_AT = slice(SZ_AT + 72, SZ_AT + 80)
+
+
+def flat(n, w):
+    return n * NWIDE + w
+
+
+def everywhere(step):
+    return [(flat(n, w), flat(*step(n, w))) for n in range(NNAR) for w in range(NWIDE)]
+
+
+def swap_b(n, w):
+    return (n, w ^ 1) if n in (0, NNAR - 1) else (((n + 1) ^ 1) - 1, w)
+
+
+def swap_chips(n, w):
+    return (n ^ 1, w) if w in (0, NWIDE - 1) else (n, ((w + 1) ^ 1) - 1)
+
+
+def inward(n, w):
+    to = w + 2 if w % 2 else w - 2
+    return n, to if 0 <= to < NWIDE else w ^ 1
+
+
+BOTH = ("narrow", "wide")
 PAIR_A = [(i, i ^ 1) for i in range(NNAR)]
-PAIR_B = [(i, (((i + 1) ^ 1) - 1) % NNAR) for i in range(NNAR)]
 CORES = [(i, i ^ 1) for i in range(NWIDE)]
-CHIPS = [(i, (((i + 1) ^ 1) - 1) % NWIDE) for i in range(NWIDE)]
-NEXT_CHIPS = [(i, (i + (2 if i % 2 else -2)) % NWIDE) for i in range(NWIDE)]
+PAIR_B, CHIPS = everywhere(swap_b), everywhere(swap_chips)
+INWARD = everywhere(inward)
 
 
 def lanes(v):
@@ -210,7 +235,7 @@
 
 
 def local_terms(c, state, own, fine, fx, fz, known, scale, dxy):
-    r0 = pl.multiple_of(c * 8, 8)
+    r0 = 8 * c
     here, at, after = pl.ds(r0, 8), pl.ds(r0 + 8, 8), pl.ds(r0 + 16, 8)
     for z in range(NPL):
         v = own[z, at]
@@ -234,7 +259,9 @@
         scale[z - 1, here] = DT * inverse(wt)
 
 
-def inside_kernel(state, fine, own, fx, fz, known, scale, dxy):
+def inside_kernel(state, fine, consts_in, own, fx, fz, known, scale, dxy, consts, sem):
+    fetch = pltpu.make_async_copy(consts_in, consts, sem)
+    fetch.start()
     for z in range(NPL):
         own[z, 8 : 8 + BX] = state[0, z]
 
@@ -242,16 +269,15 @@
         local_terms(c, state, own, fine, fx, fz, known, scale, dxy)
         return carry
 
-    lax.fori_loop(1, BX // 8 - 1, chunk, 0)
+    for c in range(1, BX // 8 - 1):
+        chunk(c, 0)
+    fetch.wait()
 
 
 def edge_kernel(
-    state, coarse, fine, x_chip, x_core, consts_in, own_in, fx_in, fz_in, known_in, scale_in, dxy_in,
-    own, fx, fz, known, scale, dxy, rims, base, consts,
-    sem,
+    state, coarse, fine, x_chip, x_core, own_in, fx_in, fz_in, known_in, scale_in, dxy_in,
+    own, fx, fz, known, scale, dxy, rims, base,
 ):
-    fetch = pltpu.make_async_copy(consts_in, consts, sem)
-    fetch.start()
     left, right = x_sides(x_chip, x_core, slice(0, 4))
     for z in range(NPL):
         own[z, 7:8] = left[z : z + 1]
@@ -273,7 +299,6 @@
     for tn, en in near:
         total = total + (1.0 + 0.5 * (e + en)) * (tn - t)
     base[...] = total
-    fetch.wait()
 
 
 def phase_kernel(
@@ -314,7 +339,7 @@
         return ref[z, rows]
 
     def fluxes(c, carry):
-        r0 = pl.multiple_of(c * 8, 8)
+        r0 = 8 * c
         here, at, after = pl.ds(r0, 8), pl.ds(r0 + 8, 8), pl.ds(r0 + 16, 8)
         for side, (zz, there) in enumerate(((0, has_low), (5, has_high))):
             v = get(zz + 1, at)
@@ -336,7 +361,8 @@
             scale03[side, here] = DT * inverse(wt)
         return carry
 
-    lax.fori_loop(0, BX // 8, fluxes, 0)
+    for c in range(BX // 8):
+        fluxes(c, 0)
 
     for side in range(2):
         for row in (0, BX - 1):
@@ -378,7 +404,7 @@
 
 def rim_kernel(
     own, rims, x_chip, x_core, zb, za, lb, la, edges, spectral_in, lines, consts,
-    tiles, spectral, far,
+    tiles, spectral,
 ):
     n, w = lax.axis_index("narrow"), lax.axis_index("wide")
     even = lax.rem(n, 2) == 0
@@ -453,8 +479,6 @@
         first == 0, more[0:1], jnp.where(first == CX - 1, more[1:2], 0.0)
     )
     spectral[...] = moved
-    core0 = lax.rem(w, 2) == 0
-    far[...] = jnp.where(core0, moved[0:8], pltpu.roll(moved[8:16], 4, 0))
 
 
 def solute_kernel(state, own, x_chip, x_core, zb, za, lb, la, tiles, done, out, sown, fresh, grown, sems):
@@ -479,11 +503,11 @@
         sown[z, 8 + BX : 9 + BX] = right[z : z + 1]
     fetch.wait()
 
-    def step(c, carry):
-        r0 = pl.multiple_of(c * 8, 8)
+    def step(c):
+        r0 = 8 * c
         here, at, after = pl.ds(r0, 8), pl.ds(r0 + 8, 8), pl.ds(r0 + 16, 8)
 
-        beyond = pl.ds(pl.multiple_of(r0 + BX, 8), 8)
+        beyond = pl.ds(r0 + BX, 8)
         ps = (
             [has_low * jnp.where(even, zb[beyond], za[beyond])]
             + [own[z, at] for z in range(NPL)]
@@ -510,49 +534,38 @@
                 total = total + (q - 0.25 * pn) * (sn - s)
             grown[z, here] = s + DT * total + (0.5 + 0.425 * s) * (fresh[z, here] - p)
         store(c).start()
-        return carry
 
     def store(c):
-        rows = pl.ds(pl.multiple_of(c * 8, 8), 8)
+        rows = pl.ds(8 * c, 8)
         return pltpu.make_async_copy(grown.at[:, rows], out.at[1, :, rows], sems.at[1 + c])
 
-    lax.fori_loop(0, BX // 8, step, 0)
+    for c in range(BX // 8):
+        step(c)
     for c in range(BX // 8):
         store(c).wait()
     for copy in ends:
         copy.wait()
 
 
-def chip_kernel(mine, partner, here, message):
-    core = lax.rem(lax.axis_index("wide"), 2)
-    first, second = pl.ds(pl.multiple_of(core * CX, 8), CX), pl.ds(pl.multiple_of((1 - core) * CX, 8), CX)
-    here[first] = mine[...]
-    here[second] = partner[...]
-    message[0:CX] = mine[...]
-    near = jnp.where(core == 0, partner[0:8], pltpu.roll(partner[8:16], 4, 0))
-    message[CX : CX + 8] = near
-def window_kernel(here, across, shared, view):
-    w = lax.axis_index("wide")
-    core, chip = lax.rem(w, 2), lax.div(w, 2)
-    has_before, has_after = flag(chip > 0), flag(chip < NWIDE // 2 - 1)
-
-    @pl.when(core == 0)
-    def _():
-        view[0:4] = across[CX : CX + 4] * has_before
-        view[4:20] = across[0:CX] * has_before
-        view[20:52] = here[...]
-        view[52:56] = shared[0:4] * has_after
-
-    @pl.when(core == 1)
-    def _():
-        view[0:4] = shared[0:4] * has_before
-        view[4:36] = here[...]
-        view[36:56] = across[0:20] * has_after
-
-
-def solve_kernel(planes, coarse, consts, out, modes, rows):
-    n, w = lax.axis_index("narrow"), lax.axis_index("wide")
-    has_left, has_right = flag(w > 0), flag(w < NWIDE - 1)
+def eliminate(state, f, consts, first):
+    states = []
+    for i, v in enumerate(f):
+        inv = consts[INV_AT + 8 * (first + i) : INV_AT + 8 * (first + i) + 8]
+        state = inv * v if state is None else inv * v + (KBAR * inv) * state
+        states.append(state)
+    return states
+
+
+def back(x, states, consts, first):
+    values = []
+    for i in range(len(states) - 1, -1, -1):
+        inv = consts[INV_AT + 8 * (first + i) : INV_AT + 8 * (first + i) + 8]
+        x = states[i] + (KBAR * inv) * x
+        values.append(x)
+    return values[::-1]
+
+
+def mode_kernel(planes, consts, f, to_chip, to_core, to_next, modes):
     half = NNAR // 2
     folded = [
         [planes[m] + planes[NNAR - 1 - m] for m in range(half)],
@@ -562,35 +575,60 @@
         total = float(SZ[k, 0]) * folded[k % 2][0]
         for m in range(1, half):
             total = total + float(SZ[k, m]) * folded[k % 2][m]
-        modes[k * 56 : (k + 1) * 56] = total
-    f = [modes[pl.ds(j, 8, stride=56), :] for j in range(56)]
-    inv_of = [consts[INV_AT + 8 * i : INV_AT + 8 * i + 8] for i in range(SUBX)]
-    link = [KBAR * v for v in inv_of]
-
-    def solve(order, keep):
-        h = [inv_of[0] * f[order[0]]]
-        for i in range(1, SUBX):
-            h.append(inv_of[i] * f[order[i]] + link[i] * h[-1])
-        x = h[-1]
-        found = {order[-1]: x}
-        for i in range(SUBX - 2, -1, -1):
-            if order[i] not in keep:
-                break
-            x = h[i] + link[i] * x
-            found[order[i]] = x
-        return found
-
-    mine = solve(list(range(16, 40)), set(range(20, 40)))
-    lower = solve(list(range(0, 24)), set(range(20, 24)))
-    upper = solve(list(range(55, 31, -1)), set(range(32, 36)))
+        modes[k * CX : (k + 1) * CX] = total
+    values = [modes[pl.ds(j, 8, stride=CX), :] for j in range(CX)]
+    for j in range(CX):
+        f[j] = values[j]
+    mirrored = values[::-1]
+    right_margin = eliminate(None, values[12:], consts, 0)[-1]
+    left_margin = eliminate(None, mirrored[12:], consts, 0)[-1]
+    right_core = eliminate(None, values, consts, 4)[-1]
+    left_core = eliminate(None, mirrored, consts, 4)[-1]
+    core0 = lax.rem(lax.axis_index("wide"), 2) == 0
+    to_core[0:8] = jnp.where(core0, right_margin, left_margin)
+    to_core[8:16] = jnp.where(core0, right_core, left_core)
+    to_chip[0:8] = jnp.where(core0, left_margin, right_margin)
+    to_chip[8:16] = jnp.where(core0, left_core, right_core)
+    to_next[...] = to_chip[0:8]
+
+
+def pass_kernel(to_chip, by_core, consts, message):
+    message[0:8] = to_chip[0:8]
+    message[8:16] = to_chip[8:16] + consts[PASS_AT] * by_core[0:8]
+
+
+def solve_kernel(f, by_chip, by_core, by_next, coarse, consts, out, rows):
+    n, w = lax.axis_index("narrow"), lax.axis_index("wide")
+    core0 = lax.rem(w, 2) == 0
+    has_left, has_right = flag(w > 0), flag(w < NWIDE - 1)
+    beyond = consts[PASS_AT] * by_next[...] * jnp.where(core0, flag(w < NWIDE - 2), flag(w > 1))
+    other = jnp.concatenate([by_core[0:8], by_core[8:16] + beyond], 0)
+    left = jnp.where(core0, by_chip[...], other) * has_left
+    right = jnp.where(core0, other, by_chip[...]) * has_right
+    values = [f[j] for j in range(CX)]
+    mirrored = values[::-1]
+    half = CX // 2
+
+    low = eliminate(left[0:8], values[:half], consts, 4)
+    high = eliminate(right[0:8], mirrored[:half], consts, 4)
+    link = KBAR * consts[INV_AT + 8 * 11 : INV_AT + 8 * 12]
+    x_low = consts[MEET_AT] * (low[-1] + link * high[-1])
+    x_high = consts[MEET_AT] * (high[-1] + link * low[-1])
+    x = back(x_low, low[:-1], consts, 4) + [x_low]
+    x += (back(x_high, high[:-1], consts, 4) + [x_high])[::-1]
+
+    for here, near, there in (
+        (range(4), left, has_left),
+        (range(CX - 1, CX - 5, -1), right, has_right),
+    ):
+        states = eliminate(near[8:16], [values[j] for j in here], consts, 20)
+        found = back(states[-1], states[:-1], consts, 20) + [states[-1]]
+        for j, v in zip(here, found):
+            x[j] = x[j] + there * v
+
     weight = consts[pl.ds(pl.multiple_of(SZ_AT + 8 * n, 8), 8)]
     for j in range(CX):
-        x = mine[20 + j]
-        if 20 + j in lower:
-            x = x + has_left * lower[20 + j]
-        if 20 + j in upper:
-            x = x + has_right * upper[20 + j]
-        rows[j : j + 1] = jnp.sum(x * weight, axis=0, keepdims=True)
+        rows[j : j + 1] = jnp.sum(x[j] * weight, axis=0, keepdims=True)
     out[0] = coarse[2] + dot(rows[...], consts[SY_AT])
 
 
@@ -630,26 +668,26 @@
         ],
         far=range(5),
     )(*inputs)
-    zb = lax.ppermute(face_b, "narrow", PAIR_B)
+    zb = lax.ppermute(face_b, BOTH, PAIR_B)
     za = lax.ppermute(face_a, "narrow", PAIR_A)
-    x_chip = lax.ppermute(to_chip, "wide", CHIPS)
+    x_chip = lax.ppermute(to_chip, BOTH, CHIPS)
     x_core = lax.ppermute(to_core, "wide", CORES)
     fine = kernel(spread_kernel, sds(3, BX, NY))(coarse)
     shapes = [
         sds(NPL, BX + 16, NY), sds(2, BX, NY), sds(2, BX, NY), sds(NPL, BX, NY), sds(2, BX, NY),
         sds(2, 2, BX, NY),
     ]
-    inside = kernel(inside_kernel, shapes)(state, fine)
+    *inside, consts = kernel(
+        inside_kernel, shapes + [sds(*CONSTS.shape)], [pltpu.SemaphoreType.DMA], far=(2,)
+    )(state, fine, afar(jnp.asarray(CONSTS)))
     late_b, late_a = kernel(late_kernel, [sds(LATE, NY)] * 2)(state, x_chip, x_core, inside[0])
-    lb = lax.ppermute(late_b, "narrow", PAIR_B)
+    lb = lax.ppermute(late_b, BOTH, PAIR_B)
     la = lax.ppermute(late_a, "narrow", PAIR_A)
-    own, fx12, fz12, known, scale12, dxy, rims, base, consts = kernel(
+    own, fx12, fz12, known, scale12, dxy, rims, base = kernel(
         edge_kernel,
-        shapes + [sds(8, NY), sds(CX, CY), sds(*CONSTS.shape)],
-        [pltpu.SemaphoreType.DMA],
-        far=(5,),
-        aliases={6 + i: i for i in range(6)},
-    )(state, coarse, fine, x_chip, x_core, afar(jnp.asarray(CONSTS)), *inside)
+        shapes + [sds(8, NY), sds(CX, CY)],
+        aliases={5 + i: i for i in range(6)},
+    )(state, coarse, fine, x_chip, x_core, *inside)
     result, edges, spectral, lines = kernel(
         phase_kernel,
         [sds(2, NPL, BX, NY), sds(NPL, 2, 8, NY), sds(CX, CY), sds(16, NY)],
@@ -667,15 +705,10 @@
         ],
         far_outs=(0,),
     )(coarse, own, fine, fx12, fz12, known, scale12, dxy, zb, za, base, consts)
-    tiles, spectral, far = kernel(
-        rim_kernel, [sds(NPL, 2, 8, NY), sds(CX, CY), sds(8, CY)]
-    )(own, rims, x_chip, x_core, zb, za, lb, la, edges, spectral, lines, consts)
-    partner = lax.ppermute(spectral, "wide", CORES)
-    shared = lax.ppermute(far, "wide", NEXT_CHIPS)
-    here, message = kernel(chip_kernel, [sds(2 * CX, CY), sds(CX + 8, CY)])(spectral, partner)
-    across = lax.ppermute(message, "wide", CHIPS)
-    view = kernel(window_kernel, sds(56, CY))(here, across, shared)
-    planes = lax.all_to_all(jnp.broadcast_to(view[None], (NNAR, 56, CY)), "narrow", 0, 0)
+    tiles, spectral = kernel(rim_kernel, [sds(NPL, 2, 8, NY), sds(CX, CY)])(
+        own, rims, x_chip, x_core, zb, za, lb, la, edges, spectral, lines, consts
+    )
+    planes = lax.all_to_all(jnp.broadcast_to(spectral[None], (NNAR, CX, CY)), "narrow", 0, 0)
     state_new = kernel(
         solute_kernel,
         sds(2, NPL, BX, NY),
@@ -689,11 +722,17 @@
         far_outs=(0,),
         aliases={9: 0},
     )(state, own, x_chip, x_core, zb, za, lb, la, tiles, result)
-    adjusted = kernel(
-        solve_kernel,
-        sds(1, CX, CY),
-        [pltpu.VMEM((NNAR * 56, CY), F32), pltpu.VMEM((CX, CY), F32)],
-    )(planes, coarse, consts)
+    f, to_chip, to_core, to_next = kernel(
+        mode_kernel,
+        [sds(CX, 8, CY), sds(16, CY), sds(16, CY), sds(8, CY)],
+        [pltpu.VMEM((NNAR * CX, CY), F32)],
+    )(planes, consts)
+    by_core = lax.ppermute(to_core, "wide", CORES)
+    by_next = lax.ppermute(to_next, BOTH, INWARD)
+    by_chip = lax.ppermute(kernel(pass_kernel, sds(16, CY))(to_chip, by_core, consts), BOTH, CHIPS)
+    adjusted = kernel(solve_kernel, sds(1, CX, CY), [pltpu.VMEM((CX, CY), F32)])(
+        f, by_chip, by_core, by_next, coarse, consts
+    )
     return state_new, adjusted
 
 

time: 45.9 us -> 42.2 us (0.919)
  blocking collectives: 0 us -> 13.4 us
  waiting for transfers between devices: 15.2 us -> 3.96 us
  starting transfers between devices: 18.3 us -> 15.1 us
  Pallas kernels: 10.3 us -> 8.77 us
  local copies, waits for them, and re-layouts: 0.71 us -> 0.01 us
    all_to_all x0 -> x1, blocking collectives: none -> 13.4 us  [on_device(): lax.all_to_all(jnp.broadcast_to(spectral[None], (NNAR, CX, CY)), 'narrow'...]
    ppermute x6, waiting for transfers between devices: 9.56 us -> 2.28 us  [the longest x1 1.16 us: on_device(): by_core = lax.ppermute(to_core, 'wide', CORES)]
    ppermute x6, starting transfers between devices: 13.9 us -> 8.15 us  [the longest x1 4.62 us: on_device(): x_chip = lax.ppermute(to_chip, BOTH, CHIPS)]
    all_to_all x1 -> x0, waiting for transfers between devices: 5.6 us -> none  [on_device(): lax.all_to_all(jnp.broadcast_to(view[None], (NNAR, 56, CY)), 'narrow', 0, 0)]
    all_to_all x1 -> x0, starting transfers between devices: 3.4 us -> none  [on_device(): lax.all_to_all(jnp.broadcast_to(view[None], (NNAR, 56, CY)), 'narrow', 0, 0)]
    ppermute x1, starting transfers between devices: 0.01 us -> 2.97 us  [on_device(): za = lax.ppermute(face_a, 'narrow', PAIR_A)]
    ppermute x1, starting transfers between devices: 1.02 us -> 3.94 us  [on_device(): la = lax.ppermute(late_a, 'narrow', PAIR_A)]
    ppermute x1, waiting for transfers between devices: 0.01 us -> 1.67 us  [on_device(): la = lax.ppermute(late_a, 'narrow', PAIR_A)]
  transfers between devices with their start and end apart: 10 -> 9, of which waited for: 5 -> 4; matrix products, arithmetic and copies ran while one was open for 0% -> 0% of each run, Pallas kernels for 17% -> 15%
where the time goes in v4:
time: 42.2 us; the launch traced here: 42 us
  starting transfers between devices  15.1 us (36%)
  blocking collectives  13.4 us (32%)
  Pallas kernels  8.77 us (21%)
  waiting for transfers between devices  3.96 us (9%)
  between operations  0.75 us (2%)
    all_to_all x1, blocking collectives, on_device(): lax.all_to_all(jnp.broadcast_to(spectral[None], (NNAR, CX, CY)), 'narrow'...  13.4 us
    pallas_call x11, Pallas kernels, call(): pl.pallas_call(body, out_shape=outs, in_specs=[HBM if i in far else VMEM...  8.77 us
    ppermute x1, starting transfers between devices, on_device(): x_chip = lax.ppermute(to_chip, BOTH, CHIPS)  4.62 us
    ppermute x1, starting transfers between devices, on_device(): la = lax.ppermute(late_a, 'narrow', PAIR_A)  3.94 us
    ppermute x1, starting transfers between devices, on_device(): za = lax.ppermute(face_a, 'narrow', PAIR_A)  2.97 us
    ppermute x1, starting transfers between devices, on_device(): lax.ppermute(kernel(pass_kernel, sds(16, CY))(to_chip, by_core, consts),...  2.83 us
    ppermute x1, waiting for transfers between devices, on_device(): la = lax.ppermute(late_a, 'narrow', PAIR_A)  1.67 us
    ppermute x1, waiting for transfers between devices, on_device(): by_core = lax.ppermute(to_core, 'wide', CORES)  1.16 us
  transfers between devices with their start and end apart: 9, of which 4 were waited for; matrix products, arithmetic and copies ran while one was open for 0% of the time, Pallas kernels for 15%

profile of v4, /device:TPU:8, one launch (start us, length us, event | category | flops | bytes accessed | tf_op | source)
XLA Modules:
  0.0 42.0 jit_solution(11159083734116069159)
XLA Ops:
  0.6 1.4 %stage_kernel.1 = (f32[144,512]{1,0:T(8,128)S(1)}, f32[144,512]{1,0:T(8,128)S(1)}, f32[16,512]{1,0:T(8,128)S(1)}, f32[16,512]{1,0:T(8,128)S(1)}, f32[2,4,64,512]...) custom-call(f32[2,4,64,512]{3,2,1,0:T(8,128)} %state_in.1, s32[1,16,128]{2,1,0:T(8,128)} %ids_in.1, s32[1,16,128]{2,1,0:T(8,128)} %frozen_in.1, ...), custom_call_target="tpu_custom_call" | custom-call | tf_op jit(solution)/shard_map/stage_kernel/pallas_call | solution.py:639
  2.0 0.1 collective-permute-start.2
  2.1 3.0 %collective-permute-start.3 = (f32[144,512]{1,0:T(8,128)S(1)}, f32[144,512]{1,0:T(8,128)S(1)}, u32[]{:S(2)}, u32[]{:S(2)}) collective-permute-start(f32[144,512]{1,0:T(8,128)S(1)} %get-tuple-element.47), channel_id=1, source_target_pairs={{0,32},{32,0},{64,96},{96,64},{128,160},{160,128},{192,224},{224,1... | collective-permute-start | bytes 884744 | tf_op jit(solution)/shard_map/ppermute | solution.py:672
  5.1 4.6 %collective-permute-start = (f32[16,512]{1,0:T(8,128)S(1)}, f32[16,512]{1,0:T(8,128)S(1)}, u32[]{:S(2)}, u32[]{:S(2)}) collective-permute-start(f32[16,512]{1,0:T(8,128)S(1)} %get-tuple-element.37), channel_id=1, source_target_pairs={{0,32},{1,2},{2,1},{3,4},{4,3},{5,6},{6,5},{7,8},{8,7},{9,10},{10,... | collective-permute-start | bytes 98312 | tf_op jit(solution)/shard_map/ppermute | solution.py:673
  9.7 0.0 collective-permute-start.1
  9.7 0.1 spread_kernel.1.fine
  9.9 1.0 %inside_kernel.1 = (f32[4,80,512]{2,1,0:T(8,128)S(1)}, f32[2,64,512]{2,1,0:T(8,128)S(1)}, f32[2,64,512]{2,1,0:T(8,128)S(1)}, f32[4,64,512]{2,1,0:T(8,128)S(1)}, ...) custom-call(f32[2,4,64,512]{3,2,1,0:T(8,128)S(1)} %get-tuple-element.35.state, ...), custom_call_target="tpu_custom_call" | custom-call | tf_op jit(solution)/shard_map/inside_kernel/pallas_call | solution.py:639
  10.9 0.8 %collective-permute-done.x_chip = f32[16,512]{1,0:T(8,128)S(1)} collective-permute-done((f32[16,512]{1,0:T(8,128)S(1)}, f32[16,512]{1,0:T(8,128)S(1)}, u32[]{:S(2)}, u32[]{:S(2)}) %collective-permute-start) | collective-permute-done | bytes 32800 | tf_op jit(solution)/shard_map/ppermute | solution.py:673
  11.7 0.0 collective-permute-done.1.x_core
  11.7 0.1 collective-permute-start.4
  11.8 3.9 %collective-permute-start.5 = (f32[72,512]{1,0:T(8,128)S(1)}, f32[72,512]{1,0:T(8,128)S(1)}, u32[]{:S(2)}, u32[]{:S(2)}) collective-permute-start(f32[72,512]{1,0:T(8,128)S(1)} %get-tuple-element.49), channel_id=1, source_target_pairs={{0,32},{32,0},{64,96},{96,64},{128,160},{160,128},{192,224},{224,1... | collective-permute-start | bytes 442376 | tf_op jit(solution)/shard_map/ppermute | solution.py:685
  15.8 0.3 edge_kernel.1
  16.0 0.0 collective-permute-done.2.zb
  16.0 0.0 collective-permute-done.3.za
  16.1 1.9 %phase_kernel.1 = (f32[2,4,64,512]{3,2,1,0:T(8,128)}, f32[4,2,8,512]{3,2,1,0:T(8,128)S(1)}, f32[16,128]{1,0:T(8,128)S(1)}, f32[16,512]{1,0:T(8,128)S(1)}) custom-call(f32[4,16,128]{2,1,0:T(8,128)S(1)} %get-tuple-element.36.coarse, f32[4,80,512]{2,1,0:T(8,128)S(1)} %get-tuple-element.45.own, f32[3,64,512]{2,1,0:T(8,128)S(1)} %spread_kernel.1.fine, ...), custom_call_target="tpu_custom_call" | custom-call | tf_op jit(solution)/shard_map/phase_kernel/pallas_call | solution.py:639
  17.9 0.0 collective-permute-done.4.lb
  17.9 1.7 %collective-permute-done.5.la = f32[72,512]{1,0:T(8,128)S(1)} collective-permute-done((f32[72,512]{1,0:T(8,128)S(1)}, f32[72,512]{1,0:T(8,128)S(1)}, u32[]{:S(2)}, u32[]{:S(2)}) %collective-permute-start.5) | collective-permute-done | bytes 147488 | tf_op jit(solution)/shard_map/ppermute | solution.py:685
  19.6 0.3 rim_kernel.1
  20.0 13.4 %all_to_all.5.planes = f32[8,16,128]{2,1,0:T(8,128)S(1)} all-to-all(f32[8,16,128]{2,1,0:T(8,128)S(1)} %broadcast_in_dim.2), channel_id=1, replica_groups=mesh['narrow'=8,'wide'=32] {'narrow'}, dimensions={0} | all-to-all | bytes 131072 | tf_op jit(solution)/shard_map/all_to_all | solution.py:711
  33.4 0.1 mode_kernel.1
  33.5 0.1 collective-permute-start.6
  33.6 1.2 %collective-permute-done.6.by_core = f32[16,128]{1,0:T(8,128)S(1)} collective-permute-done((f32[16,128]{1,0:T(8,128)S(1)}, f32[16,128]{1,0:T(8,128)S(1)}, u32[]{:S(2)}, u32[]{:S(2)}) %collective-permute-start.6) | collective-permute-done | bytes 8224 | tf_op jit(solution)/shard_map/ppermute | solution.py:730
  34.7 2.8 %collective-permute-start.7 = (f32[16,128]{1,0:T(8,128)S(1)}, f32[16,128]{1,0:T(8,128)S(1)}, u32[]{:S(2)}, u32[]{:S(2)}) collective-permute-start(f32[16,128]{1,0:T(8,128)S(1)} %pass_kernel.1), channel_id=1, source_target_pairs={{0,32},{1,2},{2,1},{3,4},{4,3},{5,6},{6,5},{7,8},{8,7},{9,10},{10,... | collective-permute-start | bytes 24584 | tf_op jit(solution)/shard_map/ppermute | solution.py:732
  37.6 0.4 collective-permute-start.8
  38.0 2.8 %solute_kernel.1 = f32[2,4,64,512]{3,2,1,0:T(8,128)} custom-call(f32[2,4,64,512]{3,2,1,0:T(8,128)S(1)} %get-tuple-element.35.state, f32[4,80,512]{2,1,0:T(8,128)S(1)} %get-tuple-element.45.own, f32[16,512]{1,0:T(8,128)S(1)} %collective-permute-done.x_chip, f32[16,512]{1,0:T(8,128)S(1)} %collective-permute-done.1.x_core, ...), custom_call_target="tpu_custom_call", output_to_operand_aliasing={{}: (9, {})} | custom-call | tf_op jit(solution)/shard_map/solute_kernel/pallas_call | solution.py:639
  40.8 0.4 collective-permute-done.8.by_next
  41.2 0.0 collective-permute-done.7.by_chip
  41.2 0.8 %solve_kernel.1 = f32[1,16,128]{2,1,0:T(8,128)} custom-call(f32[16,8,128]{2,1,0:T(8,128)S(1)} %get-tuple-element.64.f, f32[16,128]{1,0:T(8,128)S(1)} %collective-permute-done.7.by_chip, f32[16,128]{1,0:T(8,128)S(1)} %collective-permute-done.6.by_core, f32[8,128]{1,0:T(8,128)S(1)} %collective-permute-done.8.by_next, ...), custom_call_target="tpu_custom_call" | custom-call | tf_op jit(solution)/shard_map/solve_kernel/pallas_call | solution.py:639
  (3 shorter events, 0.0 us)
Async XLA Ops:
  2.0 14.0 %collective-permute-start.2 = (f32[144,512]{1,0:T(8,128)S(1)}, f32[144,512]{1,0:T(8,128)S(1)}, u32[]{:S(2)}, u32[]{:S(2)}) collective-permute-start(f32[144,512]{1,0:T(8,128)S(1)} %get-tuple-element.46), channel_id=1, source_target_pairs={{0,1},{1,0},{2,3},{3,2},{4,5},{5,4},{6,7},{7,6},{8,9},{9,8},{10,11... | collective-permute-start | bytes 884744 | tf_op jit(solution)/shard_map/ppermute | solution.py:671
  2.1 13.9 %collective-permute-start.3 = (f32[144,512]{1,0:T(8,128)S(1)}, f32[144,512]{1,0:T(8,128)S(1)}, u32[]{:S(2)}, u32[]{:S(2)}) collective-permute-start(f32[144,512]{1,0:T(8,128)S(1)} %get-tuple-element.47), channel_id=1, source_target_pairs={{0,32},{32,0},{64,96},{96,64},{128,160},{160,128},{192,224},{224,1... | collective-permute-start | bytes 884744 | tf_op jit(solution)/shard_map/ppermute | solution.py:672
  5.1 6.6 %collective-permute-start = (f32[16,512]{1,0:T(8,128)S(1)}, f32[16,512]{1,0:T(8,128)S(1)}, u32[]{:S(2)}, u32[]{:S(2)}) collective-permute-start(f32[16,512]{1,0:T(8,128)S(1)} %get-tuple-element.37), channel_id=1, source_target_pairs={{0,32},{1,2},{2,1},{3,4},{4,3},{5,6},{6,5},{7,8},{8,7},{9,10},{10,... | collective-permute-start | bytes 98312 | tf_op jit(solution)/shard_map/ppermute | solution.py:673
  9.7 2.0 %collective-permute-start.1 = (f32[16,512]{1,0:T(8,128)S(1)}, f32[16,512]{1,0:T(8,128)S(1)}, u32[]{:S(2)}, u32[]{:S(2)}) collective-permute-start(f32[16,512]{1,0:T(8,128)S(1)} %get-tuple-element.38), channel_id=1, source_target_pairs={{0,1},{1,0},{2,3},{3,2},{4,5},{5,4},{6,7},{7,6},{8,9},{9,8},{10,11... | collective-permute-start | bytes 98312 | tf_op jit(solution)/shard_map/ppermute | solution.py:674
  11.7 6.2 %collective-permute-start.4 = (f32[72,512]{1,0:T(8,128)S(1)}, f32[72,512]{1,0:T(8,128)S(1)}, u32[]{:S(2)}, u32[]{:S(2)}) collective-permute-start(f32[72,512]{1,0:T(8,128)S(1)} %get-tuple-element.48), channel_id=1, source_target_pairs={{0,1},{1,0},{2,3},{3,2},{4,5},{5,4},{6,7},{7,6},{8,9},{9,8},{10,11... | collective-permute-start | bytes 442376 | tf_op jit(solution)/shard_map/ppermute | solution.py:684
  11.8 7.8 %collective-permute-start.5 = (f32[72,512]{1,0:T(8,128)S(1)}, f32[72,512]{1,0:T(8,128)S(1)}, u32[]{:S(2)}, u32[]{:S(2)}) collective-permute-start(f32[72,512]{1,0:T(8,128)S(1)} %get-tuple-element.49), channel_id=1, source_target_pairs={{0,32},{32,0},{64,96},{96,64},{128,160},{160,128},{192,224},{224,1... | collective-permute-start | bytes 442376 | tf_op jit(solution)/shard_map/ppermute | solution.py:685
  33.5 1.3 %collective-permute-start.6 = (f32[16,128]{1,0:T(8,128)S(1)}, f32[16,128]{1,0:T(8,128)S(1)}, u32[]{:S(2)}, u32[]{:S(2)}) collective-permute-start(f32[16,128]{1,0:T(8,128)S(1)} %get-tuple-element.66), channel_id=1, source_target_pairs={{0,1},{1,0},{2,3},{3,2},{4,5},{5,4},{6,7},{7,6},{8,9},{9,8},{10,11... | collective-permute-start | bytes 24584 | tf_op jit(solution)/shard_map/ppermute | solution.py:730
  34.7 6.4 %collective-permute-start.7 = (f32[16,128]{1,0:T(8,128)S(1)}, f32[16,128]{1,0:T(8,128)S(1)}, u32[]{:S(2)}, u32[]{:S(2)}) collective-permute-start(f32[16,128]{1,0:T(8,128)S(1)} %pass_kernel.1), channel_id=1, source_target_pairs={{0,32},{1,2},{2,1},{3,4},{4,3},{5,6},{6,5},{7,8},{8,7},{9,10},{10,... | collective-permute-start | bytes 24584 | tf_op jit(solution)/shard_map/ppermute | solution.py:732
  37.6 3.6 %collective-permute-start.8 = (f32[8,128]{1,0:T(8,128)S(1)}, f32[8,128]{1,0:T(8,128)S(1)}, u32[]{:S(2)}, u32[]{:S(2)}) collective-permute-start(f32[8,128]{1,0:T(8,128)S(1)} %get-tuple-element.67), channel_id=1, source_target_pairs={{0,1},{1,3},{2,0},{3,5},{4,2},{5,7},{6,4},{7,9},{8,6},{9,11},{10,8... | collective-permute-start | bytes 12296 | tf_op jit(solution)/shard_map/ppermute | solution.py:731

commit v5 on v4

--- a/solution.py
+++ b/solution.py
@@ -11,7 +11,9 @@
 F32 = jnp.float32
 NNAR, NWIDE = 8, 32
 NPL, BX, NY = 4, 64, 512
-ROUGH, FACE, CORNERS, LATE = 128, 144, 64, 72
+SPLIT = 24
+ROUGH, EARLY, FACE = 128, 144, 144 + SPLIT
+CORNERS, LATE = 64 - SPLIT, 72 - SPLIT
 CX, CY = 16, 128
 SUBX = 24
 SIGMA, KBAR = 0.05, 0.75
@@ -78,7 +80,9 @@
 
 
 def swap_chips(n, w):
-    return (n ^ 1, w) if w in (0, NWIDE - 1) else (n, ((w + 1) ^ 1) - 1)
+    if w in (0, NWIDE - 1):
+        return (n ^ 4, w) if n % 4 in (1, 2) else (n, NWIDE - 1 - w)
+    return n, ((w + 1) ^ 1) - 1
 
 
 def inward(n, w):
@@ -183,15 +187,18 @@
     coarse[1] = c * s
     coarse[2] = temp[0]
     coarse[3] = -0.5 * frozen[0].astype(F32)
-    for copy in copies[:2]:
-        copy.wait()
     even = lax.rem(lax.axis_index("narrow"), 2) == 0
+    for ref in (face_b, face_a):
+        for k in range(4):
+            ref[ROUGH:EARLY, k * CY : (k + 1) * CY] = coarse[k]
+    copies[0].wait()
     for ref, top in ((face_b, jnp.logical_not(even)), (face_a, even)):
         first = jnp.where(top, 2, 0)
         ref[0:BX] = state[0, first]
         ref[BX : 2 * BX] = state[0, first + 1]
-        for k in range(4):
-            ref[ROUGH:FACE, k * CY : (k + 1) * CY] = coarse[k]
+    copies[1].wait()
+    for ref, top in ((face_b, jnp.logical_not(even)), (face_a, even)):
+        ref[EARLY:FACE] = state[1, jnp.where(top, 3, 0), 0:SPLIT]
     core0 = lax.rem(lax.axis_index("wide"), 2) == 0
     for ref, low in ((x_chip, core0), (x_core, jnp.logical_not(core0))):
         for z in range(NPL):
@@ -218,7 +225,7 @@
     even = lax.rem(lax.axis_index("narrow"), 2) == 0
     left, right = x_sides(x_chip, x_core, slice(0, 8))
     for ref, top in ((late_b, jnp.logical_not(even)), (late_a, even)):
-        ref[0:BX] = state[1, jnp.where(top, 3, 0)]
+        ref[0:CORNERS] = state[1, jnp.where(top, 3, 0), SPLIT:BX]
         ref[CORNERS : CORNERS + 1] = jnp.where(top, left[3:4], left[0:1])
         ref[CORNERS + 1 : CORNERS + 2] = jnp.where(top, right[3:4], right[0:1])
         ref[CORNERS + 2 : LATE] = jnp.zeros((LATE - CORNERS - 2, NY), F32)
@@ -303,8 +310,8 @@
 
 def phase_kernel(
     coarse, own, fine, fx12, fz12, known, scale12, dxy, zb, za, base, consts,
-    out, edges, spectral, lines,
-    sides, halo, fx, fz03, fzout, bent, scale03, change, fresh, sems,
+    fresh, spectral, lines,
+    sides, halo, fx, fz03, fzout, bent, scale03, change,
 ):
     n = lax.axis_index("narrow")
     even = lax.rem(n, 2) == 0
@@ -315,8 +322,8 @@
     ):
         for k in range(2):
             halo[at + k, 8 : 8 + BX] = face[k * BX : (k + 1) * BX] * there
-    low = jnp.where(even, zb[ROUGH:FACE], za[ROUGH:FACE])
-    high = jnp.where(even, za[ROUGH:FACE], zb[ROUGH:FACE])
+    low = jnp.where(even, zb[ROUGH:EARLY], za[ROUGH:EARLY])
+    high = jnp.where(even, za[ROUGH:EARLY], zb[ROUGH:EARLY])
     for k, v in enumerate((low, low, high, high)):
         wide = spread(v[:, (k % 2) * CY : (k % 2 + 1) * CY])
         widen(sides, k, wide)
@@ -371,10 +378,6 @@
     rest = [(bent, 0), (known, 1), (known, 2), (bent, 1)]
     scales = [(scale03, 0), (scale12, 0), (scale12, 1), (scale03, 1)]
 
-    def store(c):
-        rows = pl.ds(8 * c, 8)
-        return pltpu.make_async_copy(fresh.at[:, rows], out.at[0, :, rows], sems.at[c])
-
     for c in range(BX // 8):
         here, at, after = pl.ds(8 * c, 8), pl.ds(8 * c + 8, 8), pl.ds(8 * c + 16, 8)
         total = jnp.zeros((8, NY), F32)
@@ -386,25 +389,19 @@
             rise = factor * (rest[z][0][rest[z][1], here] + spread_z + spread_x)
             total = total + rise
             if c in (0, BX // 8 - 1):
-                edges[z, 0 if c == 0 else 1] = p + rise
                 row, line = (0, z) if c == 0 else (7, NPL + z)
                 lines[line : line + 1] = factor[row : row + 1]
-            else:
-                fresh[z, here] = p + rise
+            fresh[z, here] = p + rise
         total = total + pltpu.roll(total, 1, 0)
         total = total + pltpu.roll(total, 2, 0)
         change[2 * c : 2 * c + 1] = total[3:4]
         change[2 * c + 1 : 2 * c + 2] = total[7:8]
-        if 0 < c < BX // 8 - 1:
-            store(c).start()
     spectral[...] = dot(still, consts[SY_AT]) + dot(change[...], consts[MEAN_AT])
-    for c in range(1, BX // 8 - 1):
-        store(c).wait()
 
 
 def rim_kernel(
-    own, rims, x_chip, x_core, zb, za, lb, la, edges, spectral_in, lines, consts,
-    tiles, spectral,
+    own, rims, x_chip, x_core, zb, za, lb, la, spectral_in, lines, consts, fresh_in,
+    fresh, spectral,
 ):
     n, w = lax.axis_index("narrow"), lax.axis_index("wide")
     even = lax.rem(n, 2) == 0
@@ -471,7 +468,8 @@
     for c in range(2):
         for z in range(NPL):
             add = rise[NPL * c + z : NPL * c + z + 1]
-            tiles[z, c] = edges[z, c] + jnp.where(row == 7 * c, add, 0.0)
+            at = (BX - 1) * c
+            fresh[z, at : at + 1] = fresh_in[z, at : at + 1] + add
     sums = [jnp.sum(rise[NPL * c : NPL * (c + 1)], axis=0, keepdims=True) for c in range(2)]
     more = dot(jnp.concatenate(sums + [jnp.zeros((14, NY), F32)], 0), consts[MEAN_AT])
     first = rows_of(spectral_in)
@@ -481,18 +479,12 @@
     spectral[...] = moved
 
 
-def solute_kernel(state, own, x_chip, x_core, zb, za, lb, la, tiles, done, out, sown, fresh, grown, sems):
-    within = pl.ds(8, BX - 16)
-    fetch = pltpu.make_async_copy(done.at[0, :, within], fresh.at[:, within], sems.at[0])
-    fetch.start()
-    ends = [
-        pltpu.make_async_copy(tiles.at[:, c], out.at[0, :, pl.ds((BX - 8) * c, 8)], sems.at[9 + c])
-        for c in range(2)
+def solute_kernel(state, own, x_chip, x_core, zb, za, lb, la, fresh, out, sown, grown, sems):
+    phase_out = [
+        pltpu.make_async_copy(fresh.at[z], out.at[0, z], sems.at[8 + z]) for z in range(NPL)
     ]
-    for copy in ends:
+    for copy in phase_out:
         copy.start()
-    for c in range(2):
-        fresh[:, (BX - 8) * c : (BX - 8) * c + 8] = tiles[:, c]
     n = lax.axis_index("narrow")
     even = lax.rem(n, 2) == 0
     left, right = x_sides(x_chip, x_core, slice(8, 12))
@@ -501,7 +493,6 @@
         sown[z, 8 : 8 + BX] = state[1, z]
         sown[z, 7:8] = left[z : z + 1]
         sown[z, 8 + BX : 9 + BX] = right[z : z + 1]
-    fetch.wait()
 
     def step(c):
         r0 = 8 * c
@@ -513,10 +504,14 @@
             + [own[z, at] for z in range(NPL)]
             + [has_high * jnp.where(even, za[here], zb[here])]
         )
+        if r0 < SPLIT:
+            (b, a), there = (zb, za), pl.ds(EARLY + r0, 8)
+        else:
+            (b, a), there = (lb, la), pl.ds(r0 - SPLIT, 8)
         ss = (
-            [has_low * jnp.where(even, lb[here], la[here])]
+            [has_low * jnp.where(even, b[there], a[there])]
             + [sown[z, at] for z in range(NPL)]
-            + [has_high * jnp.where(even, la[here], lb[here])]
+            + [has_high * jnp.where(even, a[there], b[there])]
         )
         for z in range(NPL):
             p, s = ps[z + 1], ss[z + 1]
@@ -537,13 +532,13 @@
 
     def store(c):
         rows = pl.ds(8 * c, 8)
-        return pltpu.make_async_copy(grown.at[:, rows], out.at[1, :, rows], sems.at[1 + c])
+        return pltpu.make_async_copy(grown.at[:, rows], out.at[1, :, rows], sems.at[c])
 
     for c in range(BX // 8):
         step(c)
     for c in range(BX // 8):
         store(c).wait()
-    for copy in ends:
+    for copy in phase_out:
         copy.wait()
 
 
@@ -589,7 +584,8 @@
     to_core[8:16] = jnp.where(core0, right_core, left_core)
     to_chip[0:8] = jnp.where(core0, left_margin, right_margin)
     to_chip[8:16] = jnp.where(core0, left_core, right_core)
-    to_next[...] = to_chip[0:8]
+    to_next[0:8] = to_chip[0:8]
+    to_next[8:24] = jnp.zeros((16, CY), F32)
 
 
 def pass_kernel(to_chip, by_core, consts, message):
@@ -601,7 +597,7 @@
     n, w = lax.axis_index("narrow"), lax.axis_index("wide")
     core0 = lax.rem(w, 2) == 0
     has_left, has_right = flag(w > 0), flag(w < NWIDE - 1)
-    beyond = consts[PASS_AT] * by_next[...] * jnp.where(core0, flag(w < NWIDE - 2), flag(w > 1))
+    beyond = consts[PASS_AT] * by_next[0:8] * jnp.where(core0, flag(w < NWIDE - 2), flag(w > 1))
     other = jnp.concatenate([by_core[0:8], by_core[8:16] + beyond], 0)
     left = jnp.where(core0, by_chip[...], other) * has_left
     right = jnp.where(core0, other, by_chip[...]) * has_right
@@ -688,9 +684,9 @@
         shapes + [sds(8, NY), sds(CX, CY)],
         aliases={5 + i: i for i in range(6)},
     )(state, coarse, fine, x_chip, x_core, *inside)
-    result, edges, spectral, lines = kernel(
+    fresh, spectral, lines = kernel(
         phase_kernel,
-        [sds(2, NPL, BX, NY), sds(NPL, 2, 8, NY), sds(CX, CY), sds(16, NY)],
+        [sds(NPL, BX, NY), sds(CX, CY), sds(16, NY)],
         [
             pltpu.VMEM((4, BX, NY), F32),
             pltpu.VMEM((4, BX + 16, NY), F32),
@@ -700,14 +696,11 @@
             pltpu.VMEM((2, BX, NY), F32),
             pltpu.VMEM((2, BX, NY), F32),
             pltpu.VMEM((CX, NY), F32),
-            pltpu.VMEM((NPL, BX, NY), F32),
-            pltpu.SemaphoreType.DMA((BX // 8,)),
         ],
-        far_outs=(0,),
     )(coarse, own, fine, fx12, fz12, known, scale12, dxy, zb, za, base, consts)
-    tiles, spectral = kernel(rim_kernel, [sds(NPL, 2, 8, NY), sds(CX, CY)])(
-        own, rims, x_chip, x_core, zb, za, lb, la, edges, spectral, lines, consts
-    )
+    fresh, spectral = kernel(
+        rim_kernel, [sds(NPL, BX, NY), sds(CX, CY)], aliases={11: 0}
+    )(own, rims, x_chip, x_core, zb, za, lb, la, spectral, lines, consts, fresh)
     planes = lax.all_to_all(jnp.broadcast_to(spectral[None], (NNAR, CX, CY)), "narrow", 0, 0)
     state_new = kernel(
         solute_kernel,
@@ -715,16 +708,13 @@
         [
             pltpu.VMEM((NPL, BX + 16, NY), F32),
             pltpu.VMEM((NPL, BX, NY), F32),
-            pltpu.VMEM((NPL, BX, NY), F32),
-            pltpu.SemaphoreType.DMA((3 + BX // 8,)),
+            pltpu.SemaphoreType.DMA((BX // 8 + NPL,)),
         ],
-        far=(9,),
         far_outs=(0,),
-        aliases={9: 0},
-    )(state, own, x_chip, x_core, zb, za, lb, la, tiles, result)
+    )(state, own, x_chip, x_core, zb, za, lb, la, fresh)
     f, to_chip, to_core, to_next = kernel(
         mode_kernel,
-        [sds(CX, 8, CY), sds(16, CY), sds(16, CY), sds(8, CY)],
+        [sds(CX, 8, CY), sds(16, CY), sds(16, CY), sds(24, CY)],
         [pltpu.VMEM((NNAR * CX, CY), F32)],
     )(planes, consts)
     by_core = lax.ppermute(to_core, "wide", CORES)

time: 42.2 us -> 42 us (level)
  Pallas kernels: 8.77 us -> 7.16 us
  starting transfers between devices: 15.1 us -> 15.9 us
  waiting for transfers between devices: 3.96 us -> 4.51 us
    ppermute x1, starting transfers between devices: 0.42 us -> 3.27 us  [on_device(): by_next = lax.ppermute(to_next, BOTH, INWARD)]
    ppermute x1, waiting for transfers between devices: 0.01 us -> 2.58 us  [on_device(): lax.ppermute(kernel(pass_kernel, sds(16, CY))(to_chip, by_core, consts),...]
    ppermute x1, starting transfers between devices: 2.83 us -> 0.84 us  [on_device(): lax.ppermute(kernel(pass_kernel, sds(16, CY))(to_chip, by_core, consts),...]
    pallas_call x11, Pallas kernels: 8.77 us -> 7.16 us  [call(): pl.pallas_call(body, out_shape=outs, in_specs=[HBM if i in far else VMEM...]
    ppermute x1, waiting for transfers between devices: 1.16 us -> 0.01 us  [on_device(): by_core = lax.ppermute(to_core, 'wide', CORES)]
    ppermute x1, waiting for transfers between devices: 1.67 us -> 1.15 us  [on_device(): la = lax.ppermute(late_a, 'narrow', PAIR_A)]
  transfers between devices with their start and end apart: 9 -> 9, of which waited for: 4 -> 3; matrix products, arithmetic and copies ran while one was open for 0% -> 0% of each run, Pallas kernels for 15% -> 11%
where the time goes in v5:
time: 42 us; the launch traced here: 41.8 us
  starting transfers between devices  15.9 us (38%)
  blocking collectives  13.4 us (32%)
  Pallas kernels  7.16 us (17%)
  waiting for transfers between devices  4.51 us (11%)
  between operations  0.74 us (2%)
    all_to_all x1, blocking collectives, on_device(): lax.all_to_all(jnp.broadcast_to(spectral[None], (NNAR, CX, CY)), 'narrow'...  13.4 us
    pallas_call x11, Pallas kernels, call(): pl.pallas_call(body, out_shape=outs, in_specs=[HBM if i in far else VMEM...  7.16 us
    ppermute x1, starting transfers between devices, on_device(): x_chip = lax.ppermute(to_chip, BOTH, CHIPS)  4.62 us
    ppermute x1, starting transfers between devices, on_device(): la = lax.ppermute(late_a, 'narrow', PAIR_A)  3.94 us
    ppermute x1, starting transfers between devices, on_device(): by_next = lax.ppermute(to_next, BOTH, INWARD)  3.27 us
    ppermute x1, starting transfers between devices, on_device(): za = lax.ppermute(face_a, 'narrow', PAIR_A)  2.97 us
    ppermute x1, waiting for transfers between devices, on_device(): lax.ppermute(kernel(pass_kernel, sds(16, CY))(to_chip, by_core, consts),...  2.58 us
    ppermute x1, waiting for transfers between devices, on_device(): la = lax.ppermute(late_a, 'narrow', PAIR_A)  1.15 us
  transfers between devices with their start and end apart: 9, of which 3 were waited for; matrix products, arithmetic and copies ran while one was open for 0% of the time, Pallas kernels for 11%

profile of v5, /device:TPU:8, one launch (start us, length us, event | category | flops | bytes accessed | tf_op | source)
XLA Modules:
  0.0 41.8 jit_solution(4661842680279561002)
XLA Ops:
  0.6 1.4 %stage_kernel.1 = (f32[168,512]{1,0:T(8,128)S(1)}, f32[168,512]{1,0:T(8,128)S(1)}, f32[16,512]{1,0:T(8,128)S(1)}, f32[16,512]{1,0:T(8,128)S(1)}, f32[2,4,64,512]...) custom-call(f32[2,4,64,512]{3,2,1,0:T(8,128)} %state_in.1, s32[1,16,128]{2,1,0:T(8,128)} %ids_in.1, s32[1,16,128]{2,1,0:T(8,128)} %frozen_in.1, ...), custom_call_target="tpu_custom_call" | custom-call | tf_op jit(solution)/shard_map/stage_kernel/pallas_call | solution.py:635
  2.0 0.1 collective-permute-start.2
  2.1 3.0 %collective-permute-start.3 = (f32[168,512]{1,0:T(8,128)S(1)}, f32[168,512]{1,0:T(8,128)S(1)}, u32[]{:S(2)}, u32[]{:S(2)}) collective-permute-start(f32[168,512]{1,0:T(8,128)S(1)} %get-tuple-element.46), channel_id=1, source_target_pairs={{0,32},{32,0},{64,96},{96,64},{128,160},{160,128},{192,224},{224,1... | collective-permute-start | bytes 1032200 | tf_op jit(solution)/shard_map/ppermute | solution.py:668
  5.1 4.6 %collective-permute-start = (f32[16,512]{1,0:T(8,128)S(1)}, f32[16,512]{1,0:T(8,128)S(1)}, u32[]{:S(2)}, u32[]{:S(2)}) collective-permute-start(f32[16,512]{1,0:T(8,128)S(1)} %get-tuple-element.36), channel_id=1, source_target_pairs={{0,31},{1,2},{2,1},{3,4},{4,3},{5,6},{6,5},{7,8},{8,7},{9,10},{10,... | collective-permute-start | bytes 98312 | tf_op jit(solution)/shard_map/ppermute | solution.py:669
  9.7 0.0 collective-permute-start.1
  9.7 0.1 spread_kernel.1.fine
  9.9 1.0 %inside_kernel.1 = (f32[4,80,512]{2,1,0:T(8,128)S(1)}, f32[2,64,512]{2,1,0:T(8,128)S(1)}, f32[2,64,512]{2,1,0:T(8,128)S(1)}, f32[4,64,512]{2,1,0:T(8,128)S(1)}, ...) custom-call(f32[2,4,64,512]{3,2,1,0:T(8,128)S(1)} %get-tuple-element.34.state, ...), custom_call_target="tpu_custom_call" | custom-call | tf_op jit(solution)/shard_map/inside_kernel/pallas_call | solution.py:635
  10.9 0.8 %collective-permute-done.x_chip = f32[16,512]{1,0:T(8,128)S(1)} collective-permute-done((f32[16,512]{1,0:T(8,128)S(1)}, f32[16,512]{1,0:T(8,128)S(1)}, u32[]{:S(2)}, u32[]{:S(2)}) %collective-permute-start) | collective-permute-done | bytes 32800 | tf_op jit(solution)/shard_map/ppermute | solution.py:669
  11.7 0.0 collective-permute-done.1.x_core
  11.7 0.1 collective-permute-start.4
  11.8 3.9 %collective-permute-start.5 = (f32[48,512]{1,0:T(8,128)S(1)}, f32[48,512]{1,0:T(8,128)S(1)}, u32[]{:S(2)}, u32[]{:S(2)}) collective-permute-start(f32[48,512]{1,0:T(8,128)S(1)} %get-tuple-element.48), channel_id=1, source_target_pairs={{0,32},{32,0},{64,96},{96,64},{128,160},{160,128},{192,224},{224,1... | collective-permute-start | bytes 294920 | tf_op jit(solution)/shard_map/ppermute | solution.py:681
  15.8 0.3 edge_kernel.1
  16.0 0.0 collective-permute-done.2.zb
  16.0 0.0 collective-permute-done.3.za
  16.1 1.4 %phase_kernel.1 = (f32[4,64,512]{2,1,0:T(8,128)S(1)}, f32[16,128]{1,0:T(8,128)S(1)}, f32[16,512]{1,0:T(8,128)S(1)}) custom-call(f32[4,16,128]{2,1,0:T(8,128)S(1)} %get-tuple-element.35.coarse, f32[4,80,512]{2,1,0:T(8,128)S(1)} %get-tuple-element.44.own, f32[3,64,512]{2,1,0:T(8,128)S(1)} %spread_kernel.1.fine, f32[2,64,512]{2,1,0:T(8,128)S(1)} %get-tuple-element.50.fx12, ...), custom_call_target="tpu_custom_call" | custom-call | tf_op jit(solution)/shard_map/phase_kernel/pallas_call | solution.py:635
  17.4 0.0 collective-permute-done.4.lb
  17.4 1.2 %collective-permute-done.5.la = f32[48,512]{1,0:T(8,128)S(1)} collective-permute-done((f32[48,512]{1,0:T(8,128)S(1)}, f32[48,512]{1,0:T(8,128)S(1)}, u32[]{:S(2)}, u32[]{:S(2)}) %collective-permute-start.5) | collective-permute-done | bytes 98336 | tf_op jit(solution)/shard_map/ppermute | solution.py:681
  18.6 0.3 rim_kernel.1
  18.9 13.4 %all_to_all.5.planes = f32[8,16,128]{2,1,0:T(8,128)S(1)} all-to-all(f32[8,16,128]{2,1,0:T(8,128)S(1)} %broadcast_in_dim.2), channel_id=1, replica_groups=mesh['narrow'=8,'wide'=32] {'narrow'}, dimensions={0} | all-to-all | bytes 131072 | tf_op jit(solution)/shard_map/all_to_all | solution.py:704
  32.3 0.1 mode_kernel.1
  32.4 0.1 collective-permute-start.6
  32.5 3.3 %collective-permute-start.8 = (f32[24,128]{1,0:T(8,128)S(1)}, f32[24,128]{1,0:T(8,128)S(1)}, u32[]{:S(2)}, u32[]{:S(2)}) collective-permute-start(f32[24,128]{1,0:T(8,128)S(1)} %get-tuple-element.65), channel_id=1, source_target_pairs={{0,1},{1,3},{2,0},{3,5},{4,2},{5,7},{6,4},{7,9},{8,6},{9,11},{10,8... | collective-permute-start | bytes 36872 | tf_op jit(solution)/shard_map/ppermute | solution.py:721
  35.8 0.0 collective-permute-done.6.by_core
  35.8 0.8 %collective-permute-start.7 = (f32[16,128]{1,0:T(8,128)S(1)}, f32[16,128]{1,0:T(8,128)S(1)}, u32[]{:S(2)}, u32[]{:S(2)}) collective-permute-start(f32[16,128]{1,0:T(8,128)S(1)} %pass_kernel.1), channel_id=1, source_target_pairs={{0,31},{1,2},{2,1},{3,4},{4,3},{5,6},{6,5},{7,8},{8,7},{9,10},{10,... | collective-permute-start | bytes 24584 | tf_op jit(solution)/shard_map/ppermute | solution.py:722
  36.6 1.7 %solute_kernel.1 = f32[2,4,64,512]{3,2,1,0:T(8,128)} custom-call(f32[2,4,64,512]{3,2,1,0:T(8,128)S(1)} %get-tuple-element.34.state, f32[4,80,512]{2,1,0:T(8,128)S(1)} %get-tuple-element.44.own, f32[16,512]{1,0:T(8,128)S(1)} %collective-permute-done.x_chip, f32[16,512]{1,0:T(8,128)S(1)} %collective-permute-done.1.x_core, ...), custom_call_target="tpu_custom_call" | custom-call | tf_op jit(solution)/shard_map/solute_kernel/pallas_call | solution.py:635
  38.4 0.0 collective-permute-done.8.by_next
  38.4 2.6 %collective-permute-done.7.by_chip = f32[16,128]{1,0:T(8,128)S(1)} collective-permute-done((f32[16,128]{1,0:T(8,128)S(1)}, f32[16,128]{1,0:T(8,128)S(1)}, u32[]{:S(2)}, u32[]{:S(2)}) %collective-permute-start.7) | collective-permute-done | bytes 8224 | tf_op jit(solution)/shard_map/ppermute | solution.py:722
  41.0 0.8 %solve_kernel.1 = f32[1,16,128]{2,1,0:T(8,128)} custom-call(f32[16,8,128]{2,1,0:T(8,128)S(1)} %get-tuple-element.62.f, f32[16,128]{1,0:T(8,128)S(1)} %collective-permute-done.7.by_chip, f32[16,128]{1,0:T(8,128)S(1)} %collective-permute-done.6.by_core, f32[24,128]{1,0:T(8,128)S(1)} %collective-permute-done.8.by_next, ...), custom_call_target="tpu_custom_call" | custom-call | tf_op jit(solution)/shard_map/solve_kernel/pallas_call | solution.py:635
  (3 shorter events, 0.0 us)
Async XLA Ops:
  2.0 14.0 %collective-permute-start.2 = (f32[168,512]{1,0:T(8,128)S(1)}, f32[168,512]{1,0:T(8,128)S(1)}, u32[]{:S(2)}, u32[]{:S(2)}) collective-permute-start(f32[168,512]{1,0:T(8,128)S(1)} %get-tuple-element.45), channel_id=1, source_target_pairs={{0,1},{1,0},{2,3},{3,2},{4,5},{5,4},{6,7},{7,6},{8,9},{9,8},{10,11... | collective-permute-start | bytes 1032200 | tf_op jit(solution)/shard_map/ppermute | solution.py:667
  2.1 13.9 %collective-permute-start.3 = (f32[168,512]{1,0:T(8,128)S(1)}, f32[168,512]{1,0:T(8,128)S(1)}, u32[]{:S(2)}, u32[]{:S(2)}) collective-permute-start(f32[168,512]{1,0:T(8,128)S(1)} %get-tuple-element.46), channel_id=1, source_target_pairs={{0,32},{32,0},{64,96},{96,64},{128,160},{160,128},{192,224},{224,1... | collective-permute-start | bytes 1032200 | tf_op jit(solution)/shard_map/ppermute | solution.py:668
  5.1 6.6 %collective-permute-start = (f32[16,512]{1,0:T(8,128)S(1)}, f32[16,512]{1,0:T(8,128)S(1)}, u32[]{:S(2)}, u32[]{:S(2)}) collective-permute-start(f32[16,512]{1,0:T(8,128)S(1)} %get-tuple-element.36), channel_id=1, source_target_pairs={{0,31},{1,2},{2,1},{3,4},{4,3},{5,6},{6,5},{7,8},{8,7},{9,10},{10,... | collective-permute-start | bytes 98312 | tf_op jit(solution)/shard_map/ppermute | solution.py:669
  9.7 2.0 %collective-permute-start.1 = (f32[16,512]{1,0:T(8,128)S(1)}, f32[16,512]{1,0:T(8,128)S(1)}, u32[]{:S(2)}, u32[]{:S(2)}) collective-permute-start(f32[16,512]{1,0:T(8,128)S(1)} %get-tuple-element.37), channel_id=1, source_target_pairs={{0,1},{1,0},{2,3},{3,2},{4,5},{5,4},{6,7},{7,6},{8,9},{9,8},{10,11... | collective-permute-start | bytes 98312 | tf_op jit(solution)/shard_map/ppermute | solution.py:670
  11.7 5.7 %collective-permute-start.4 = (f32[48,512]{1,0:T(8,128)S(1)}, f32[48,512]{1,0:T(8,128)S(1)}, u32[]{:S(2)}, u32[]{:S(2)}) collective-permute-start(f32[48,512]{1,0:T(8,128)S(1)} %get-tuple-element.47), channel_id=1, source_target_pairs={{0,1},{1,0},{2,3},{3,2},{4,5},{5,4},{6,7},{7,6},{8,9},{9,8},{10,11... | collective-permute-start | bytes 294920 | tf_op jit(solution)/shard_map/ppermute | solution.py:680
  11.8 6.8 %collective-permute-start.5 = (f32[48,512]{1,0:T(8,128)S(1)}, f32[48,512]{1,0:T(8,128)S(1)}, u32[]{:S(2)}, u32[]{:S(2)}) collective-permute-start(f32[48,512]{1,0:T(8,128)S(1)} %get-tuple-element.48), channel_id=1, source_target_pairs={{0,32},{32,0},{64,96},{96,64},{128,160},{160,128},{192,224},{224,1... | collective-permute-start | bytes 294920 | tf_op jit(solution)/shard_map/ppermute | solution.py:681
  32.4 3.4 %collective-permute-start.6 = (f32[16,128]{1,0:T(8,128)S(1)}, f32[16,128]{1,0:T(8,128)S(1)}, u32[]{:S(2)}, u32[]{:S(2)}) collective-permute-start(f32[16,128]{1,0:T(8,128)S(1)} %get-tuple-element.64), channel_id=1, source_target_pairs={{0,1},{1,0},{2,3},{3,2},{4,5},{5,4},{6,7},{7,6},{8,9},{9,8},{10,11... | collective-permute-start | bytes 24584 | tf_op jit(solution)/shard_map/ppermute | solution.py:720
  32.5 5.9 %collective-permute-start.8 = (f32[24,128]{1,0:T(8,128)S(1)}, f32[24,128]{1,0:T(8,128)S(1)}, u32[]{:S(2)}, u32[]{:S(2)}) collective-permute-start(f32[24,128]{1,0:T(8,128)S(1)} %get-tuple-element.65), channel_id=1, source_target_pairs={{0,1},{1,3},{2,0},{3,5},{4,2},{5,7},{6,4},{7,9},{8,6},{9,11},{10,8... | collective-permute-start | bytes 36872 | tf_op jit(solution)/shard_map/ppermute | solution.py:721
  35.8 5.2 %collective-permute-start.7 = (f32[16,128]{1,0:T(8,128)S(1)}, f32[16,128]{1,0:T(8,128)S(1)}, u32[]{:S(2)}, u32[]{:S(2)}) collective-permute-start(f32[16,128]{1,0:T(8,128)S(1)} %pass_kernel.1), channel_id=1, source_target_pairs={{0,31},{1,2},{2,1},{3,4},{4,3},{5,6},{6,5},{7,8},{8,7},{9,10},{10,... | collective-permute-start | bytes 24584 | tf_op jit(solution)/shard_map/ppermute | solution.py:722

commit v6 on v5

--- a/solution.py
+++ b/solution.py
@@ -85,6 +85,10 @@
     return n, ((w + 1) ^ 1) - 1
 
 
+def swap_chips_last(n, w):
+    return (n ^ 1, w) if w in (0, NWIDE - 1) else (n, ((w + 1) ^ 1) - 1)
+
+
 def inward(n, w):
     to = w + 2 if w % 2 else w - 2
     return n, to if 0 <= to < NWIDE else w ^ 1
@@ -94,7 +98,7 @@
 PAIR_A = [(i, i ^ 1) for i in range(NNAR)]
 CORES = [(i, i ^ 1) for i in range(NWIDE)]
 PAIR_B, CHIPS = everywhere(swap_b), everywhere(swap_chips)
-INWARD = everywhere(inward)
+INWARD, CHIPS_LAST = everywhere(inward), everywhere(swap_chips_last)
 
 
 def lanes(v):
@@ -584,8 +588,7 @@
     to_core[8:16] = jnp.where(core0, right_core, left_core)
     to_chip[0:8] = jnp.where(core0, left_margin, right_margin)
     to_chip[8:16] = jnp.where(core0, left_core, right_core)
-    to_next[0:8] = to_chip[0:8]
-    to_next[8:24] = jnp.zeros((16, CY), F32)
+    to_next[...] = to_chip[0:8]
 
 
 def pass_kernel(to_chip, by_core, consts, message):
@@ -597,7 +600,7 @@
     n, w = lax.axis_index("narrow"), lax.axis_index("wide")
     core0 = lax.rem(w, 2) == 0
     has_left, has_right = flag(w > 0), flag(w < NWIDE - 1)
-    beyond = consts[PASS_AT] * by_next[0:8] * jnp.where(core0, flag(w < NWIDE - 2), flag(w > 1))
+    beyond = consts[PASS_AT] * by_next[...] * jnp.where(core0, flag(w < NWIDE - 2), flag(w > 1))
     other = jnp.concatenate([by_core[0:8], by_core[8:16] + beyond], 0)
     left = jnp.where(core0, by_chip[...], other) * has_left
     right = jnp.where(core0, other, by_chip[...]) * has_right
@@ -714,12 +717,12 @@
     )(state, own, x_chip, x_core, zb, za, lb, la, fresh)
     f, to_chip, to_core, to_next = kernel(
         mode_kernel,
-        [sds(CX, 8, CY), sds(16, CY), sds(16, CY), sds(24, CY)],
+        [sds(CX, 8, CY), sds(16, CY), sds(16, CY), sds(8, CY)],
         [pltpu.VMEM((NNAR * CX, CY), F32)],
     )(planes, consts)
     by_core = lax.ppermute(to_core, "wide", CORES)
     by_next = lax.ppermute(to_next, BOTH, INWARD)
-    by_chip = lax.ppermute(kernel(pass_kernel, sds(16, CY))(to_chip, by_core, consts), BOTH, CHIPS)
+    by_chip = lax.ppermute(kernel(pass_kernel, sds(16, CY))(to_chip, by_core, consts), BOTH, CHIPS_LAST)
     adjusted = kernel(solve_kernel, sds(1, CX, CY), [pltpu.VMEM((CX, CY), F32)])(
         f, by_chip, by_core, by_next, coarse, consts
     )

time: 42 us -> 41.2 us (0.981)
  waiting for transfers between devices: 4.51 us -> 3.28 us
  starting transfers between devices: 15.9 us -> 16.4 us
    ppermute x1, waiting for transfers between devices: 2.58 us -> 0.01 us  [on_device(): lax.ppermute(kernel(pass_kernel, sds(16, CY))(to_chip, by_core, consts),...]
    ppermute x1, starting transfers between devices: 0.84 us -> 2.96 us  [on_device(): lax.ppermute(kernel(pass_kernel, sds(16, CY))(to_chip, by_core, consts),...]
    ppermute x1, starting transfers between devices: 3.27 us -> 1.66 us  [on_device(): by_next = lax.ppermute(to_next, BOTH, INWARD)]
    ppermute x1, waiting for transfers between devices: 0.01 us -> 1.16 us  [on_device(): by_core = lax.ppermute(to_core, 'wide', CORES)]
  transfers between devices with their start and end apart: 9 -> 9, of which waited for: 3 -> 4; matrix products, arithmetic and copies ran while one was open for 0% -> 0% of each run, Pallas kernels for 11% -> 11%
where the time goes in v6:
time: 41.2 us; the launch traced here: 41 us
  starting transfers between devices  16.4 us (40%)
  blocking collectives  13.4 us (33%)
  Pallas kernels  7.16 us (17%)
  waiting for transfers between devices  3.28 us (8%)
  between operations  0.74 us (2%)
    all_to_all x1, blocking collectives, on_device(): lax.all_to_all(jnp.broadcast_to(spectral[None], (NNAR, CX, CY)), 'narrow'...  13.4 us
    pallas_call x11, Pallas kernels, call(): pl.pallas_call(body, out_shape=outs, in_specs=[HBM if i in far else VMEM...  7.16 us
    ppermute x1, starting transfers between devices, on_device(): x_chip = lax.ppermute(to_chip, BOTH, CHIPS)  4.62 us
    ppermute x1, starting transfers between devices, on_device(): la = lax.ppermute(late_a, 'narrow', PAIR_A)  3.94 us
    ppermute x1, starting transfers between devices, on_device(): za = lax.ppermute(face_a, 'narrow', PAIR_A)  2.97 us
    ppermute x1, starting transfers between devices, on_device(): lax.ppermute(kernel(pass_kernel, sds(16, CY))(to_chip, by_core, consts),...  2.96 us
    ppermute x1, starting transfers between devices, on_device(): by_next = lax.ppermute(to_next, BOTH, INWARD)  1.66 us
    ppermute x1, waiting for transfers between devices, on_device(): by_core = lax.ppermute(to_core, 'wide', CORES)  1.16 us
  transfers between devices with their start and end apart: 9, of which 4 were waited for; matrix products, arithmetic and copies ran while one was open for 0% of the time, Pallas kernels for 11%

profile of v6, /device:TPU:8, one launch (start us, length us, event | category | flops | bytes accessed | tf_op | source)
XLA Modules:
  0.0 41.0 jit_solution(2127154014903344422)
XLA Ops:
  0.6 1.4 %stage_kernel.1 = (f32[168,512]{1,0:T(8,128)S(1)}, f32[168,512]{1,0:T(8,128)S(1)}, f32[16,512]{1,0:T(8,128)S(1)}, f32[16,512]{1,0:T(8,128)S(1)}, f32[2,4,64,512]...) custom-call(f32[2,4,64,512]{3,2,1,0:T(8,128)} %state_in.1, s32[1,16,128]{2,1,0:T(8,128)} %ids_in.1, s32[1,16,128]{2,1,0:T(8,128)} %frozen_in.1, ...), custom_call_target="tpu_custom_call" | custom-call | tf_op jit(solution)/shard_map/stage_kernel/pallas_call | solution.py:638
  2.0 0.1 collective-permute-start.2
  2.1 3.0 %collective-permute-start.3 = (f32[168,512]{1,0:T(8,128)S(1)}, f32[168,512]{1,0:T(8,128)S(1)}, u32[]{:S(2)}, u32[]{:S(2)}) collective-permute-start(f32[168,512]{1,0:T(8,128)S(1)} %get-tuple-element.46), channel_id=1, source_target_pairs={{0,32},{32,0},{64,96},{96,64},{128,160},{160,128},{192,224},{224,1... | collective-permute-start | bytes 1032200 | tf_op jit(solution)/shard_map/ppermute | solution.py:671
  5.1 4.6 %collective-permute-start = (f32[16,512]{1,0:T(8,128)S(1)}, f32[16,512]{1,0:T(8,128)S(1)}, u32[]{:S(2)}, u32[]{:S(2)}) collective-permute-start(f32[16,512]{1,0:T(8,128)S(1)} %get-tuple-element.36), channel_id=1, source_target_pairs={{0,31},{1,2},{2,1},{3,4},{4,3},{5,6},{6,5},{7,8},{8,7},{9,10},{10,... | collective-permute-start | bytes 98312 | tf_op jit(solution)/shard_map/ppermute | solution.py:672
  9.7 0.0 collective-permute-start.1
  9.7 0.1 spread_kernel.1.fine
  9.9 1.0 %inside_kernel.1 = (f32[4,80,512]{2,1,0:T(8,128)S(1)}, f32[2,64,512]{2,1,0:T(8,128)S(1)}, f32[2,64,512]{2,1,0:T(8,128)S(1)}, f32[4,64,512]{2,1,0:T(8,128)S(1)}, ...) custom-call(f32[2,4,64,512]{3,2,1,0:T(8,128)S(1)} %get-tuple-element.34.state, ...), custom_call_target="tpu_custom_call" | custom-call | tf_op jit(solution)/shard_map/inside_kernel/pallas_call | solution.py:638
  10.9 0.8 %collective-permute-done.x_chip = f32[16,512]{1,0:T(8,128)S(1)} collective-permute-done((f32[16,512]{1,0:T(8,128)S(1)}, f32[16,512]{1,0:T(8,128)S(1)}, u32[]{:S(2)}, u32[]{:S(2)}) %collective-permute-start) | collective-permute-done | bytes 32800 | tf_op jit(solution)/shard_map/ppermute | solution.py:672
  11.7 0.0 collective-permute-done.1.x_core
  11.7 0.1 collective-permute-start.4
  11.8 3.9 %collective-permute-start.5 = (f32[48,512]{1,0:T(8,128)S(1)}, f32[48,512]{1,0:T(8,128)S(1)}, u32[]{:S(2)}, u32[]{:S(2)}) collective-permute-start(f32[48,512]{1,0:T(8,128)S(1)} %get-tuple-element.48), channel_id=1, source_target_pairs={{0,32},{32,0},{64,96},{96,64},{128,160},{160,128},{192,224},{224,1... | collective-permute-start | bytes 294920 | tf_op jit(solution)/shard_map/ppermute | solution.py:684
  15.8 0.3 edge_kernel.1
  16.0 0.0 collective-permute-done.2.zb
  16.0 0.0 collective-permute-done.3.za
  16.1 1.4 %phase_kernel.1 = (f32[4,64,512]{2,1,0:T(8,128)S(1)}, f32[16,128]{1,0:T(8,128)S(1)}, f32[16,512]{1,0:T(8,128)S(1)}) custom-call(f32[4,16,128]{2,1,0:T(8,128)S(1)} %get-tuple-element.35.coarse, f32[4,80,512]{2,1,0:T(8,128)S(1)} %get-tuple-element.44.own, f32[3,64,512]{2,1,0:T(8,128)S(1)} %spread_kernel.1.fine, f32[2,64,512]{2,1,0:T(8,128)S(1)} %get-tuple-element.50.fx12, ...), custom_call_target="tpu_custom_call" | custom-call | tf_op jit(solution)/shard_map/phase_kernel/pallas_call | solution.py:638
  17.4 0.0 collective-permute-done.4.lb
  17.4 1.2 %collective-permute-done.5.la = f32[48,512]{1,0:T(8,128)S(1)} collective-permute-done((f32[48,512]{1,0:T(8,128)S(1)}, f32[48,512]{1,0:T(8,128)S(1)}, u32[]{:S(2)}, u32[]{:S(2)}) %collective-permute-start.5) | collective-permute-done | bytes 98336 | tf_op jit(solution)/shard_map/ppermute | solution.py:684
  18.6 0.3 rim_kernel.1
  18.9 13.4 %all_to_all.5.planes = f32[8,16,128]{2,1,0:T(8,128)S(1)} all-to-all(f32[8,16,128]{2,1,0:T(8,128)S(1)} %broadcast_in_dim.2), channel_id=1, replica_groups=mesh['narrow'=8,'wide'=32] {'narrow'}, dimensions={0} | all-to-all | bytes 131072 | tf_op jit(solution)/shard_map/all_to_all | solution.py:707
  32.3 0.1 mode_kernel.1
  32.4 0.1 collective-permute-start.6
  32.5 1.2 %collective-permute-done.6.by_core = f32[16,128]{1,0:T(8,128)S(1)} collective-permute-done((f32[16,128]{1,0:T(8,128)S(1)}, f32[16,128]{1,0:T(8,128)S(1)}, u32[]{:S(2)}, u32[]{:S(2)}) %collective-permute-start.6) | collective-permute-done | bytes 8224 | tf_op jit(solution)/shard_map/ppermute | solution.py:723
  33.7 3.0 %collective-permute-start.7 = (f32[16,128]{1,0:T(8,128)S(1)}, f32[16,128]{1,0:T(8,128)S(1)}, u32[]{:S(2)}, u32[]{:S(2)}) collective-permute-start(f32[16,128]{1,0:T(8,128)S(1)} %pass_kernel.1), channel_id=1, source_target_pairs={{0,32},{1,2},{2,1},{3,4},{4,3},{5,6},{6,5},{7,8},{8,7},{9,10},{10,... | collective-permute-start | bytes 24584 | tf_op jit(solution)/shard_map/ppermute | solution.py:725
  36.6 1.7 %collective-permute-start.8 = (f32[8,128]{1,0:T(8,128)S(1)}, f32[8,128]{1,0:T(8,128)S(1)}, u32[]{:S(2)}, u32[]{:S(2)}) collective-permute-start(f32[8,128]{1,0:T(8,128)S(1)} %get-tuple-element.65), channel_id=1, source_target_pairs={{0,1},{1,3},{2,0},{3,5},{4,2},{5,7},{6,4},{7,9},{8,6},{9,11},{10,8... | collective-permute-start | bytes 12296 | tf_op jit(solution)/shard_map/ppermute | solution.py:724
  38.3 1.7 %solute_kernel.1 = f32[2,4,64,512]{3,2,1,0:T(8,128)} custom-call(f32[2,4,64,512]{3,2,1,0:T(8,128)S(1)} %get-tuple-element.34.state, f32[4,80,512]{2,1,0:T(8,128)S(1)} %get-tuple-element.44.own, f32[16,512]{1,0:T(8,128)S(1)} %collective-permute-done.x_chip, f32[16,512]{1,0:T(8,128)S(1)} %collective-permute-done.1.x_core, ...), custom_call_target="tpu_custom_call" | custom-call | tf_op jit(solution)/shard_map/solute_kernel/pallas_call | solution.py:638
  40.0 0.2 collective-permute-done.8.by_next
  40.2 0.0 collective-permute-done.7.by_chip
  40.2 0.8 %solve_kernel.1 = f32[1,16,128]{2,1,0:T(8,128)} custom-call(f32[16,8,128]{2,1,0:T(8,128)S(1)} %get-tuple-element.62.f, f32[16,128]{1,0:T(8,128)S(1)} %collective-permute-done.7.by_chip, f32[16,128]{1,0:T(8,128)S(1)} %collective-permute-done.6.by_core, f32[8,128]{1,0:T(8,128)S(1)} %collective-permute-done.8.by_next, ...), custom_call_target="tpu_custom_call" | custom-call | tf_op jit(solution)/shard_map/solve_kernel/pallas_call | solution.py:638
  (3 shorter events, 0.0 us)
Async XLA Ops:
  2.0 14.0 %collective-permute-start.2 = (f32[168,512]{1,0:T(8,128)S(1)}, f32[168,512]{1,0:T(8,128)S(1)}, u32[]{:S(2)}, u32[]{:S(2)}) collective-permute-start(f32[168,512]{1,0:T(8,128)S(1)} %get-tuple-element.45), channel_id=1, source_target_pairs={{0,1},{1,0},{2,3},{3,2},{4,5},{5,4},{6,7},{7,6},{8,9},{9,8},{10,11... | collective-permute-start | bytes 1032200 | tf_op jit(solution)/shard_map/ppermute | solution.py:670
  2.1 13.9 %collective-permute-start.3 = (f32[168,512]{1,0:T(8,128)S(1)}, f32[168,512]{1,0:T(8,128)S(1)}, u32[]{:S(2)}, u32[]{:S(2)}) collective-permute-start(f32[168,512]{1,0:T(8,128)S(1)} %get-tuple-element.46), channel_id=1, source_target_pairs={{0,32},{32,0},{64,96},{96,64},{128,160},{160,128},{192,224},{224,1... | collective-permute-start | bytes 1032200 | tf_op jit(solution)/shard_map/ppermute | solution.py:671
  5.1 6.6 %collective-permute-start = (f32[16,512]{1,0:T(8,128)S(1)}, f32[16,512]{1,0:T(8,128)S(1)}, u32[]{:S(2)}, u32[]{:S(2)}) collective-permute-start(f32[16,512]{1,0:T(8,128)S(1)} %get-tuple-element.36), channel_id=1, source_target_pairs={{0,31},{1,2},{2,1},{3,4},{4,3},{5,6},{6,5},{7,8},{8,7},{9,10},{10,... | collective-permute-start | bytes 98312 | tf_op jit(solution)/shard_map/ppermute | solution.py:672
  9.7 2.0 %collective-permute-start.1 = (f32[16,512]{1,0:T(8,128)S(1)}, f32[16,512]{1,0:T(8,128)S(1)}, u32[]{:S(2)}, u32[]{:S(2)}) collective-permute-start(f32[16,512]{1,0:T(8,128)S(1)} %get-tuple-element.37), channel_id=1, source_target_pairs={{0,1},{1,0},{2,3},{3,2},{4,5},{5,4},{6,7},{7,6},{8,9},{9,8},{10,11... | collective-permute-start | bytes 98312 | tf_op jit(solution)/shard_map/ppermute | solution.py:673
  11.7 5.7 %collective-permute-start.4 = (f32[48,512]{1,0:T(8,128)S(1)}, f32[48,512]{1,0:T(8,128)S(1)}, u32[]{:S(2)}, u32[]{:S(2)}) collective-permute-start(f32[48,512]{1,0:T(8,128)S(1)} %get-tuple-element.47), channel_id=1, source_target_pairs={{0,1},{1,0},{2,3},{3,2},{4,5},{5,4},{6,7},{7,6},{8,9},{9,8},{10,11... | collective-permute-start | bytes 294920 | tf_op jit(solution)/shard_map/ppermute | solution.py:683
  11.8 6.8 %collective-permute-start.5 = (f32[48,512]{1,0:T(8,128)S(1)}, f32[48,512]{1,0:T(8,128)S(1)}, u32[]{:S(2)}, u32[]{:S(2)}) collective-permute-start(f32[48,512]{1,0:T(8,128)S(1)} %get-tuple-element.48), channel_id=1, source_target_pairs={{0,32},{32,0},{64,96},{96,64},{128,160},{160,128},{192,224},{224,1... | collective-permute-start | bytes 294920 | tf_op jit(solution)/shard_map/ppermute | solution.py:684
  32.4 1.3 %collective-permute-start.6 = (f32[16,128]{1,0:T(8,128)S(1)}, f32[16,128]{1,0:T(8,128)S(1)}, u32[]{:S(2)}, u32[]{:S(2)}) collective-permute-start(f32[16,128]{1,0:T(8,128)S(1)} %get-tuple-element.64), channel_id=1, source_target_pairs={{0,1},{1,0},{2,3},{3,2},{4,5},{5,4},{6,7},{7,6},{8,9},{9,8},{10,11... | collective-permute-start | bytes 24584 | tf_op jit(solution)/shard_map/ppermute | solution.py:723
  33.7 6.6 %collective-permute-start.7 = (f32[16,128]{1,0:T(8,128)S(1)}, f32[16,128]{1,0:T(8,128)S(1)}, u32[]{:S(2)}, u32[]{:S(2)}) collective-permute-start(f32[16,128]{1,0:T(8,128)S(1)} %pass_kernel.1), channel_id=1, source_target_pairs={{0,32},{1,2},{2,1},{3,4},{4,3},{5,6},{6,5},{7,8},{8,7},{9,10},{10,... | collective-permute-start | bytes 24584 | tf_op jit(solution)/shard_map/ppermute | solution.py:725
  36.6 3.6 %collective-permute-start.8 = (f32[8,128]{1,0:T(8,128)S(1)}, f32[8,128]{1,0:T(8,128)S(1)}, u32[]{:S(2)}, u32[]{:S(2)}) collective-permute-start(f32[8,128]{1,0:T(8,128)S(1)} %get-tuple-element.65), channel_id=1, source_target_pairs={{0,1},{1,3},{2,0},{3,5},{4,2},{5,7},{6,4},{7,9},{8,6},{9,11},{10,8... | collective-permute-start | bytes 12296 | tf_op jit(solution)/shard_map/ppermute | solution.py:724

commit v7 on v6

--- a/solution.py
+++ b/solution.py
@@ -164,7 +164,7 @@
 
 def stage_kernel(
     state_in, ids_in, frozen_in, temp_in, angles_in,
-    face_b, face_a, x_chip, x_core, state, coarse,
+    face_b, face_a, state, coarse,
     ids, frozen, temp, angles, sems,
 ):
     copies = [
@@ -180,7 +180,7 @@
             ]
         )
     ]
-    for copy in copies:
+    for copy in copies[2:] + copies[:2]:
         copy.start()
     for copy in copies[2:]:
         copy.wait()
@@ -203,6 +203,9 @@
     copies[1].wait()
     for ref, top in ((face_b, jnp.logical_not(even)), (face_a, even)):
         ref[EARLY:FACE] = state[1, jnp.where(top, 3, 0), 0:SPLIT]
+
+
+def column_kernel(state, coarse, x_chip, x_core):
     core0 = lax.rem(lax.axis_index("wide"), 2) == 0
     for ref, low in ((x_chip, core0), (x_core, jnp.logical_not(core0))):
         for z in range(NPL):
@@ -330,7 +333,7 @@
     high = jnp.where(even, za[ROUGH:EARLY], zb[ROUGH:EARLY])
     for k, v in enumerate((low, low, high, high)):
         wide = spread(v[:, (k % 2) * CY : (k % 2 + 1) * CY])
-        widen(sides, k, wide)
+        sides[k] = wide
         lines[8 + 4 * (k % 2) + 2 * (k // 2) : 9 + 4 * (k % 2) + 2 * (k // 2)] = wide[0:1]
         lines[9 + 4 * (k % 2) + 2 * (k // 2) : 10 + 4 * (k % 2) + 2 * (k // 2)] = wide[CX - 1 : CX]
     t, e = coarse[2], coarse[3]
@@ -357,7 +360,13 @@
             dz = get(zz + 2, at) - get(zz, at)
             dx = x_up(v, get(zz + 1, after)) - x_down(v, get(zz + 1, here))
             dy = y_up(v) - y_down(v)
-            an = weigh(dz, dx, dy, sides[2 * side, here], sides[2 * side + 1, here])
+            c2, s2 = (
+                jnp.where(
+                    rows_of(v) < 4, sides[k, 2 * c : 2 * c + 1], sides[k, 2 * c + 1 : 2 * c + 2]
+                )
+                for k in (2 * side, 2 * side + 1)
+            )
+            an = weigh(dz, dx, dy, c2, s2)
             fzout[side, here] = (0.25 * there) * (an * an * dz)
         for side, z in enumerate((0, NPL - 1)):
             dz = get(z + 3, at) - get(z + 1, at)
@@ -655,9 +664,9 @@
 
 def on_device(state_in, ids, frozen, temp, angles):
     inputs = [afar(v) for v in (state_in, ids, frozen, temp, angles.reshape(1, -1))]
-    face_b, face_a, to_chip, to_core, state, coarse = kernel(
+    face_b, face_a, state, coarse = kernel(
         stage_kernel,
-        [sds(FACE, NY)] * 2 + [sds(16, NY)] * 2 + [sds(2, NPL, BX, NY), sds(4, CX, CY)],
+        [sds(FACE, NY)] * 2 + [sds(2, NPL, BX, NY), sds(4, CX, CY)],
         [
             pltpu.VMEM((1, CX, CY), jnp.int32),
             pltpu.VMEM((1, CX, CY), jnp.int32),
@@ -669,6 +678,7 @@
     )(*inputs)
     zb = lax.ppermute(face_b, BOTH, PAIR_B)
     za = lax.ppermute(face_a, "narrow", PAIR_A)
+    to_chip, to_core = kernel(column_kernel, [sds(16, NY)] * 2)(state, coarse)
     x_chip = lax.ppermute(to_chip, BOTH, CHIPS)
     x_core = lax.ppermute(to_core, "wide", CORES)
     fine = kernel(spread_kernel, sds(3, BX, NY))(coarse)
@@ -691,7 +701,7 @@
         phase_kernel,
         [sds(NPL, BX, NY), sds(CX, CY), sds(16, NY)],
         [
-            pltpu.VMEM((4, BX, NY), F32),
+            pltpu.VMEM((4, CX, NY), F32),
             pltpu.VMEM((4, BX + 16, NY), F32),
             pltpu.VMEM((NPL, BX + 16, NY), F32),
             pltpu.VMEM((2, BX, NY), F32),

time: 41.2 us -> 41.2 us (level)
    pallas_call x11 -> x12, Pallas kernels: 7.16 us -> 7.05 us  [call(): pl.pallas_call(body, out_shape=outs, in_specs=[HBM if i in far else VMEM...]
where the time goes in v7:
time: 41.2 us; the launch traced here: 41 us
  starting transfers between devices  16.4 us (40%)
  blocking collectives  13.4 us (33%)
  Pallas kernels  7.05 us (17%)
  waiting for transfers between devices  3.39 us (8%)
  between operations  0.74 us (2%)
    all_to_all x1, blocking collectives, on_device(): lax.all_to_all(jnp.broadcast_to(spectral[None], (NNAR, CX, CY)), 'narrow'...  13.4 us
    pallas_call x12, Pallas kernels, call(): pl.pallas_call(body, out_shape=outs, in_specs=[HBM if i in far else VMEM...  7.05 us
    ppermute x1, starting transfers between devices, on_device(): x_chip = lax.ppermute(to_chip, BOTH, CHIPS)  4.71 us
    ppermute x1, starting transfers between devices, on_device(): la = lax.ppermute(late_a, 'narrow', PAIR_A)  3.95 us
    ppermute x1, starting transfers between devices, on_device(): za = lax.ppermute(face_a, 'narrow', PAIR_A)  2.97 us
    ppermute x1, starting transfers between devices, on_device(): lax.ppermute(kernel(pass_kernel, sds(16, CY))(to_chip, by_core, consts),...  2.86 us
    ppermute x1, starting transfers between devices, on_device(): by_next = lax.ppermute(to_next, BOTH, INWARD)  1.59 us
    ppermute x1, waiting for transfers between devices, on_device(): la = lax.ppermute(late_a, 'narrow', PAIR_A)  1.2 us
  transfers between devices with their start and end apart: 9, of which 4 were waited for; matrix products, arithmetic and copies ran while one was open for 0% of the time, Pallas kernels for 11%

profile of v7, /device:TPU:8, one launch (start us, length us, event | category | flops | bytes accessed | tf_op | source)
XLA Modules:
  0.0 41.0 jit_solution(7905048787110715899)
XLA Ops:
  0.6 1.3 %stage_kernel.1 = (f32[168,512]{1,0:T(8,128)S(1)}, f32[168,512]{1,0:T(8,128)S(1)}, f32[2,4,64,512]{3,2,1,0:T(8,128)S(1)}, f32[4,16,128]{2,1,0:T(8,128)S(1)}) custom-call(f32[2,4,64,512]{3,2,1,0:T(8,128)} %state_in.1, s32[1,16,128]{2,1,0:T(8,128)} %ids_in.1, s32[1,16,128]{2,1,0:T(8,128)} %frozen_in.1, f32[1,16,128]{2,1,0:T(8,128)} %temp_in.1, f32[1,64]{1,0:T(1,128)} %bitcast.1), custom_call_target="tpu_custom_call" | custom-call | tf_op jit(solution)/shard_map/stage_kernel/pallas_call | solution.py:647
  2.0 0.1 collective-permute-start.2
  2.1 3.0 %collective-permute-start.3 = (f32[168,512]{1,0:T(8,128)S(1)}, f32[168,512]{1,0:T(8,128)S(1)}, u32[]{:S(2)}, u32[]{:S(2)}) collective-permute-start(f32[168,512]{1,0:T(8,128)S(1)} %get-tuple-element.46), channel_id=1, source_target_pairs={{0,32},{32,0},{64,96},{96,64},{128,160},{160,128},{192,224},{224,1... | collective-permute-start | bytes 1032200 | tf_op jit(solution)/shard_map/ppermute | solution.py:680
  5.1 4.7 %collective-permute-start = (f32[16,512]{1,0:T(8,128)S(1)}, f32[16,512]{1,0:T(8,128)S(1)}, u32[]{:S(2)}, u32[]{:S(2)}) collective-permute-start(f32[16,512]{1,0:T(8,128)S(1)} %get-tuple-element.36), channel_id=1, source_target_pairs={{0,31},{1,2},{2,1},{3,4},{4,3},{5,6},{6,5},{7,8},{8,7},{9,10},{10,... | collective-permute-start | bytes 98312 | tf_op jit(solution)/shard_map/ppermute | solution.py:682
  9.8 0.0 collective-permute-start.1
  9.8 0.1 spread_kernel.1.fine
  9.9 1.0 %inside_kernel.1 = (f32[4,80,512]{2,1,0:T(8,128)S(1)}, f32[2,64,512]{2,1,0:T(8,128)S(1)}, f32[2,64,512]{2,1,0:T(8,128)S(1)}, f32[4,64,512]{2,1,0:T(8,128)S(1)}, ...) custom-call(f32[2,4,64,512]{3,2,1,0:T(8,128)S(1)} %get-tuple-element.34.state, ...), custom_call_target="tpu_custom_call" | custom-call | tf_op jit(solution)/shard_map/inside_kernel/pallas_call | solution.py:647
  11.0 0.8 %collective-permute-done.x_chip = f32[16,512]{1,0:T(8,128)S(1)} collective-permute-done((f32[16,512]{1,0:T(8,128)S(1)}, f32[16,512]{1,0:T(8,128)S(1)}, u32[]{:S(2)}, u32[]{:S(2)}) %collective-permute-start) | collective-permute-done | bytes 32800 | tf_op jit(solution)/shard_map/ppermute | solution.py:682
  11.7 0.0 collective-permute-done.1.x_core
  11.7 0.1 collective-permute-start.4
  11.8 3.9 %collective-permute-start.5 = (f32[48,512]{1,0:T(8,128)S(1)}, f32[48,512]{1,0:T(8,128)S(1)}, u32[]{:S(2)}, u32[]{:S(2)}) collective-permute-start(f32[48,512]{1,0:T(8,128)S(1)} %get-tuple-element.48), channel_id=1, source_target_pairs={{0,32},{32,0},{64,96},{96,64},{128,160},{160,128},{192,224},{224,1... | collective-permute-start | bytes 294920 | tf_op jit(solution)/shard_map/ppermute | solution.py:694
  15.8 0.3 edge_kernel.1
  16.1 0.0 collective-permute-done.2.zb
  16.1 0.0 collective-permute-done.3.za
  16.1 1.3 %phase_kernel.1 = (f32[4,64,512]{2,1,0:T(8,128)S(1)}, f32[16,128]{1,0:T(8,128)S(1)}, f32[16,512]{1,0:T(8,128)S(1)}) custom-call(f32[4,16,128]{2,1,0:T(8,128)S(1)} %get-tuple-element.35.coarse, f32[4,80,512]{2,1,0:T(8,128)S(1)} %get-tuple-element.44.own, f32[3,64,512]{2,1,0:T(8,128)S(1)} %spread_kernel.1.fine, f32[2,64,512]{2,1,0:T(8,128)S(1)} %get-tuple-element.50.fx12, ...), custom_call_target="tpu_custom_call" | custom-call | tf_op jit(solution)/shard_map/phase_kernel/pallas_call | solution.py:647
  17.4 0.0 collective-permute-done.4.lb
  17.4 1.2 %collective-permute-done.5.la = f32[48,512]{1,0:T(8,128)S(1)} collective-permute-done((f32[48,512]{1,0:T(8,128)S(1)}, f32[48,512]{1,0:T(8,128)S(1)}, u32[]{:S(2)}, u32[]{:S(2)}) %collective-permute-start.5) | collective-permute-done | bytes 98336 | tf_op jit(solution)/shard_map/ppermute | solution.py:694
  18.6 0.3 rim_kernel.1
  18.9 13.4 %all_to_all.5.planes = f32[8,16,128]{2,1,0:T(8,128)S(1)} all-to-all(f32[8,16,128]{2,1,0:T(8,128)S(1)} %broadcast_in_dim.2), channel_id=1, replica_groups=mesh['narrow'=8,'wide'=32] {'narrow'}, dimensions={0} | all-to-all | bytes 131072 | tf_op jit(solution)/shard_map/all_to_all | solution.py:717
  32.4 0.1 mode_kernel.1
  32.4 0.1 collective-permute-start.6
  32.5 1.2 %collective-permute-done.6.by_core = f32[16,128]{1,0:T(8,128)S(1)} collective-permute-done((f32[16,128]{1,0:T(8,128)S(1)}, f32[16,128]{1,0:T(8,128)S(1)}, u32[]{:S(2)}, u32[]{:S(2)}) %collective-permute-start.6) | collective-permute-done | bytes 8224 | tf_op jit(solution)/shard_map/ppermute | solution.py:733
  33.7 2.9 %collective-permute-start.7 = (f32[16,128]{1,0:T(8,128)S(1)}, f32[16,128]{1,0:T(8,128)S(1)}, u32[]{:S(2)}, u32[]{:S(2)}) collective-permute-start(f32[16,128]{1,0:T(8,128)S(1)} %pass_kernel.1), channel_id=1, source_target_pairs={{0,32},{1,2},{2,1},{3,4},{4,3},{5,6},{6,5},{7,8},{8,7},{9,10},{10,... | collective-permute-start | bytes 24584 | tf_op jit(solution)/shard_map/ppermute | solution.py:735
  36.6 1.6 %collective-permute-start.8 = (f32[8,128]{1,0:T(8,128)S(1)}, f32[8,128]{1,0:T(8,128)S(1)}, u32[]{:S(2)}, u32[]{:S(2)}) collective-permute-start(f32[8,128]{1,0:T(8,128)S(1)} %get-tuple-element.65), channel_id=1, source_target_pairs={{0,1},{1,3},{2,0},{3,5},{4,2},{5,7},{6,4},{7,9},{8,6},{9,11},{10,8... | collective-permute-start | bytes 12296 | tf_op jit(solution)/shard_map/ppermute | solution.py:734
  38.2 1.7 %solute_kernel.1 = f32[2,4,64,512]{3,2,1,0:T(8,128)} custom-call(f32[2,4,64,512]{3,2,1,0:T(8,128)S(1)} %get-tuple-element.34.state, f32[4,80,512]{2,1,0:T(8,128)S(1)} %get-tuple-element.44.own, f32[16,512]{1,0:T(8,128)S(1)} %collective-permute-done.x_chip, f32[16,512]{1,0:T(8,128)S(1)} %collective-permute-done.1.x_core, ...), custom_call_target="tpu_custom_call" | custom-call | tf_op jit(solution)/shard_map/solute_kernel/pallas_call | solution.py:647
  39.9 0.3 collective-permute-done.8.by_next
  40.2 0.0 collective-permute-done.7.by_chip
  40.2 0.8 %solve_kernel.1 = f32[1,16,128]{2,1,0:T(8,128)} custom-call(f32[16,8,128]{2,1,0:T(8,128)S(1)} %get-tuple-element.62.f, f32[16,128]{1,0:T(8,128)S(1)} %collective-permute-done.7.by_chip, f32[16,128]{1,0:T(8,128)S(1)} %collective-permute-done.6.by_core, f32[8,128]{1,0:T(8,128)S(1)} %collective-permute-done.8.by_next, ...), custom_call_target="tpu_custom_call" | custom-call | tf_op jit(solution)/shard_map/solve_kernel/pallas_call | solution.py:647
  (4 shorter events, 0.1 us)
Async XLA Ops:
  2.0 14.1 %collective-permute-start.2 = (f32[168,512]{1,0:T(8,128)S(1)}, f32[168,512]{1,0:T(8,128)S(1)}, u32[]{:S(2)}, u32[]{:S(2)}) collective-permute-start(f32[168,512]{1,0:T(8,128)S(1)} %get-tuple-element.45), channel_id=1, source_target_pairs={{0,1},{1,0},{2,3},{3,2},{4,5},{5,4},{6,7},{7,6},{8,9},{9,8},{10,11... | collective-permute-start | bytes 1032200 | tf_op jit(solution)/shard_map/ppermute | solution.py:679
  2.1 14.0 %collective-permute-start.3 = (f32[168,512]{1,0:T(8,128)S(1)}, f32[168,512]{1,0:T(8,128)S(1)}, u32[]{:S(2)}, u32[]{:S(2)}) collective-permute-start(f32[168,512]{1,0:T(8,128)S(1)} %get-tuple-element.46), channel_id=1, source_target_pairs={{0,32},{32,0},{64,96},{96,64},{128,160},{160,128},{192,224},{224,1... | collective-permute-start | bytes 1032200 | tf_op jit(solution)/shard_map/ppermute | solution.py:680
  5.1 6.7 %collective-permute-start = (f32[16,512]{1,0:T(8,128)S(1)}, f32[16,512]{1,0:T(8,128)S(1)}, u32[]{:S(2)}, u32[]{:S(2)}) collective-permute-start(f32[16,512]{1,0:T(8,128)S(1)} %get-tuple-element.36), channel_id=1, source_target_pairs={{0,31},{1,2},{2,1},{3,4},{4,3},{5,6},{6,5},{7,8},{8,7},{9,10},{10,... | collective-permute-start | bytes 98312 | tf_op jit(solution)/shard_map/ppermute | solution.py:682
  9.8 1.9 %collective-permute-start.1 = (f32[16,512]{1,0:T(8,128)S(1)}, f32[16,512]{1,0:T(8,128)S(1)}, u32[]{:S(2)}, u32[]{:S(2)}) collective-permute-start(f32[16,512]{1,0:T(8,128)S(1)} %get-tuple-element.37), channel_id=1, source_target_pairs={{0,1},{1,0},{2,3},{3,2},{4,5},{5,4},{6,7},{7,6},{8,9},{9,8},{10,11... | collective-permute-start | bytes 98312 | tf_op jit(solution)/shard_map/ppermute | solution.py:683
  11.7 5.7 %collective-permute-start.4 = (f32[48,512]{1,0:T(8,128)S(1)}, f32[48,512]{1,0:T(8,128)S(1)}, u32[]{:S(2)}, u32[]{:S(2)}) collective-permute-start(f32[48,512]{1,0:T(8,128)S(1)} %get-tuple-element.47), channel_id=1, source_target_pairs={{0,1},{1,0},{2,3},{3,2},{4,5},{5,4},{6,7},{7,6},{8,9},{9,8},{10,11... | collective-permute-start | bytes 294920 | tf_op jit(solution)/shard_map/ppermute | solution.py:693
  11.8 6.8 %collective-permute-start.5 = (f32[48,512]{1,0:T(8,128)S(1)}, f32[48,512]{1,0:T(8,128)S(1)}, u32[]{:S(2)}, u32[]{:S(2)}) collective-permute-start(f32[48,512]{1,0:T(8,128)S(1)} %get-tuple-element.48), channel_id=1, source_target_pairs={{0,32},{32,0},{64,96},{96,64},{128,160},{160,128},{192,224},{224,1... | collective-permute-start | bytes 294920 | tf_op jit(solution)/shard_map/ppermute | solution.py:694
  32.4 1.3 %collective-permute-start.6 = (f32[16,128]{1,0:T(8,128)S(1)}, f32[16,128]{1,0:T(8,128)S(1)}, u32[]{:S(2)}, u32[]{:S(2)}) collective-permute-start(f32[16,128]{1,0:T(8,128)S(1)} %get-tuple-element.64), channel_id=1, source_target_pairs={{0,1},{1,0},{2,3},{3,2},{4,5},{5,4},{6,7},{7,6},{8,9},{9,8},{10,11... | collective-permute-start | bytes 24584 | tf_op jit(solution)/shard_map/ppermute | solution.py:733
  33.7 6.5 %collective-permute-start.7 = (f32[16,128]{1,0:T(8,128)S(1)}, f32[16,128]{1,0:T(8,128)S(1)}, u32[]{:S(2)}, u32[]{:S(2)}) collective-permute-start(f32[16,128]{1,0:T(8,128)S(1)} %pass_kernel.1), channel_id=1, source_target_pairs={{0,32},{1,2},{2,1},{3,4},{4,3},{5,6},{6,5},{7,8},{8,7},{9,10},{10,... | collective-permute-start | bytes 24584 | tf_op jit(solution)/shard_map/ppermute | solution.py:735
  36.6 3.6 %collective-permute-start.8 = (f32[8,128]{1,0:T(8,128)S(1)}, f32[8,128]{1,0:T(8,128)S(1)}, u32[]{:S(2)}, u32[]{:S(2)}) collective-permute-start(f32[8,128]{1,0:T(8,128)S(1)} %get-tuple-element.65), channel_id=1, source_target_pairs={{0,1},{1,3},{2,0},{3,5},{4,2},{5,7},{6,4},{7,9},{8,6},{9,11},{10,8... | collective-permute-start | bytes 12296 | tf_op jit(solution)/shard_map/ppermute | solution.py:734

commit v8 on v7

--- a/solution.py
+++ b/solution.py
@@ -11,7 +11,7 @@
 F32 = jnp.float32
 NNAR, NWIDE = 8, 32
 NPL, BX, NY = 4, 64, 512
-SPLIT = 24
+SPLIT = 16
 ROUGH, EARLY, FACE = 128, 144, 144 + SPLIT
 CORNERS, LATE = 64 - SPLIT, 72 - SPLIT
 CX, CY = 16, 128

time: 41.2 us -> 41.5 us (level)
  waiting for transfers between devices: 3.39 us -> 4.32 us
  starting transfers between devices: 16.4 us -> 15.7 us
    ppermute x1, waiting for transfers between devices: 0.26 us -> 0.84 us  [on_device(): by_next = lax.ppermute(to_next, BOTH, INWARD)]
    ppermute x1, starting transfers between devices: 1.59 us -> 1.01 us  [on_device(): by_next = lax.ppermute(to_next, BOTH, INWARD)]
where the time goes in v8:
time: 41.5 us; the launch traced here: 41.3 us
  starting transfers between devices  15.7 us (38%)
  blocking collectives  13.4 us (32%)
  Pallas kernels  7.05 us (17%)
  waiting for transfers between devices  4.32 us (10%)
  between operations  0.74 us (2%)
    all_to_all x1, blocking collectives, on_device(): lax.all_to_all(jnp.broadcast_to(spectral[None], (NNAR, CX, CY)), 'narrow'...  13.4 us
    pallas_call x12, Pallas kernels, call(): pl.pallas_call(body, out_shape=outs, in_specs=[HBM if i in far else VMEM...  7.05 us
    ppermute x1, starting transfers between devices, on_device(): x_chip = lax.ppermute(to_chip, BOTH, CHIPS)  4.71 us
    ppermute x1, starting transfers between devices, on_device(): la = lax.ppermute(late_a, 'narrow', PAIR_A)  3.95 us
    ppermute x1, starting transfers between devices, on_device(): za = lax.ppermute(face_a, 'narrow', PAIR_A)  2.97 us
    ppermute x1, starting transfers between devices, on_device(): lax.ppermute(kernel(pass_kernel, sds(16, CY))(to_chip, by_core, consts),...  2.83 us
    ppermute x1, waiting for transfers between devices, on_device(): la = lax.ppermute(late_a, 'narrow', PAIR_A)  1.56 us
    ppermute x1, waiting for transfers between devices, on_device(): by_core = lax.ppermute(to_core, 'wide', CORES)  1.16 us
  transfers between devices with their start and end apart: 9, of which 4 were waited for; matrix products, arithmetic and copies ran while one was open for 0% of the time, Pallas kernels for 11%

profile of v8, /device:TPU:8, one launch (start us, length us, event | category | flops | bytes accessed | tf_op | source)
XLA Modules:
  0.0 41.3 jit_solution(17740996814574279002)
XLA Ops:
  0.6 1.3 %stage_kernel.1 = (f32[160,512]{1,0:T(8,128)S(1)}, f32[160,512]{1,0:T(8,128)S(1)}, f32[2,4,64,512]{3,2,1,0:T(8,128)S(1)}, f32[4,16,128]{2,1,0:T(8,128)S(1)}) custom-call(f32[2,4,64,512]{3,2,1,0:T(8,128)} %state_in.1, s32[1,16,128]{2,1,0:T(8,128)} %ids_in.1, s32[1,16,128]{2,1,0:T(8,128)} %frozen_in.1, f32[1,16,128]{2,1,0:T(8,128)} %temp_in.1, f32[1,64]{1,0:T(1,128)} %bitcast.1), custom_call_target="tpu_custom_call" | custom-call | tf_op jit(solution)/shard_map/stage_kernel/pallas_call | solution.py:647
  2.0 0.1 collective-permute-start.2
  2.1 3.0 %collective-permute-start.3 = (f32[160,512]{1,0:T(8,128)S(1)}, f32[160,512]{1,0:T(8,128)S(1)}, u32[]{:S(2)}, u32[]{:S(2)}) collective-permute-start(f32[160,512]{1,0:T(8,128)S(1)} %get-tuple-element.46), channel_id=1, source_target_pairs={{0,32},{32,0},{64,96},{96,64},{128,160},{160,128},{192,224},{224,1... | collective-permute-start | bytes 983048 | tf_op jit(solution)/shard_map/ppermute | solution.py:680
  5.1 4.7 %collective-permute-start = (f32[16,512]{1,0:T(8,128)S(1)}, f32[16,512]{1,0:T(8,128)S(1)}, u32[]{:S(2)}, u32[]{:S(2)}) collective-permute-start(f32[16,512]{1,0:T(8,128)S(1)} %get-tuple-element.36), channel_id=1, source_target_pairs={{0,31},{1,2},{2,1},{3,4},{4,3},{5,6},{6,5},{7,8},{8,7},{9,10},{10,... | collective-permute-start | bytes 98312 | tf_op jit(solution)/shard_map/ppermute | solution.py:682
  9.8 0.0 collective-permute-start.1
  9.8 0.1 spread_kernel.1.fine
  9.9 1.0 %inside_kernel.1 = (f32[4,80,512]{2,1,0:T(8,128)S(1)}, f32[2,64,512]{2,1,0:T(8,128)S(1)}, f32[2,64,512]{2,1,0:T(8,128)S(1)}, f32[4,64,512]{2,1,0:T(8,128)S(1)}, ...) custom-call(f32[2,4,64,512]{3,2,1,0:T(8,128)S(1)} %get-tuple-element.34.state, ...), custom_call_target="tpu_custom_call" | custom-call | tf_op jit(solution)/shard_map/inside_kernel/pallas_call | solution.py:647
  11.0 0.8 %collective-permute-done.x_chip = f32[16,512]{1,0:T(8,128)S(1)} collective-permute-done((f32[16,512]{1,0:T(8,128)S(1)}, f32[16,512]{1,0:T(8,128)S(1)}, u32[]{:S(2)}, u32[]{:S(2)}) %collective-permute-start) | collective-permute-done | bytes 32800 | tf_op jit(solution)/shard_map/ppermute | solution.py:682
  11.7 0.0 collective-permute-done.1.x_core
  11.7 0.1 collective-permute-start.4
  11.8 3.9 %collective-permute-start.5 = (f32[56,512]{1,0:T(8,128)S(1)}, f32[56,512]{1,0:T(8,128)S(1)}, u32[]{:S(2)}, u32[]{:S(2)}) collective-permute-start(f32[56,512]{1,0:T(8,128)S(1)} %get-tuple-element.48), channel_id=1, source_target_pairs={{0,32},{32,0},{64,96},{96,64},{128,160},{160,128},{192,224},{224,1... | collective-permute-start | bytes 344072 | tf_op jit(solution)/shard_map/ppermute | solution.py:694
  15.8 0.3 edge_kernel.1
  16.1 0.0 collective-permute-done.2.zb
  16.1 0.0 collective-permute-done.3.za
  16.1 1.3 %phase_kernel.1 = (f32[4,64,512]{2,1,0:T(8,128)S(1)}, f32[16,128]{1,0:T(8,128)S(1)}, f32[16,512]{1,0:T(8,128)S(1)}) custom-call(f32[4,16,128]{2,1,0:T(8,128)S(1)} %get-tuple-element.35.coarse, f32[4,80,512]{2,1,0:T(8,128)S(1)} %get-tuple-element.44.own, f32[3,64,512]{2,1,0:T(8,128)S(1)} %spread_kernel.1.fine, f32[2,64,512]{2,1,0:T(8,128)S(1)} %get-tuple-element.50.fx12, ...), custom_call_target="tpu_custom_call" | custom-call | tf_op jit(solution)/shard_map/phase_kernel/pallas_call | solution.py:647
  17.4 0.0 collective-permute-done.4.lb
  17.4 1.6 %collective-permute-done.5.la = f32[56,512]{1,0:T(8,128)S(1)} collective-permute-done((f32[56,512]{1,0:T(8,128)S(1)}, f32[56,512]{1,0:T(8,128)S(1)}, u32[]{:S(2)}, u32[]{:S(2)}) %collective-permute-start.5) | collective-permute-done | bytes 114720 | tf_op jit(solution)/shard_map/ppermute | solution.py:694
  18.9 0.3 rim_kernel.1
  19.3 13.4 %all_to_all.5.planes = f32[8,16,128]{2,1,0:T(8,128)S(1)} all-to-all(f32[8,16,128]{2,1,0:T(8,128)S(1)} %broadcast_in_dim.2), channel_id=1, replica_groups=mesh['narrow'=8,'wide'=32] {'narrow'}, dimensions={0} | all-to-all | bytes 131072 | tf_op jit(solution)/shard_map/all_to_all | solution.py:717
  32.7 0.1 mode_kernel.1
  32.8 0.1 collective-permute-start.6
  32.9 1.2 %collective-permute-done.6.by_core = f32[16,128]{1,0:T(8,128)S(1)} collective-permute-done((f32[16,128]{1,0:T(8,128)S(1)}, f32[16,128]{1,0:T(8,128)S(1)}, u32[]{:S(2)}, u32[]{:S(2)}) %collective-permute-start.6) | collective-permute-done | bytes 8224 | tf_op jit(solution)/shard_map/ppermute | solution.py:733
  34.0 2.8 %collective-permute-start.7 = (f32[16,128]{1,0:T(8,128)S(1)}, f32[16,128]{1,0:T(8,128)S(1)}, u32[]{:S(2)}, u32[]{:S(2)}) collective-permute-start(f32[16,128]{1,0:T(8,128)S(1)} %pass_kernel.1), channel_id=1, source_target_pairs={{0,32},{1,2},{2,1},{3,4},{4,3},{5,6},{6,5},{7,8},{8,7},{9,10},{10,... | collective-permute-start | bytes 24584 | tf_op jit(solution)/shard_map/ppermute | solution.py:735
  36.9 1.0 %collective-permute-start.8 = (f32[8,128]{1,0:T(8,128)S(1)}, f32[8,128]{1,0:T(8,128)S(1)}, u32[]{:S(2)}, u32[]{:S(2)}) collective-permute-start(f32[8,128]{1,0:T(8,128)S(1)} %get-tuple-element.65), channel_id=1, source_target_pairs={{0,1},{1,3},{2,0},{3,5},{4,2},{5,7},{6,4},{7,9},{8,6},{9,11},{10,8... | collective-permute-start | bytes 12296 | tf_op jit(solution)/shard_map/ppermute | solution.py:734
  37.9 1.7 %solute_kernel.1 = f32[2,4,64,512]{3,2,1,0:T(8,128)} custom-call(f32[2,4,64,512]{3,2,1,0:T(8,128)S(1)} %get-tuple-element.34.state, f32[4,80,512]{2,1,0:T(8,128)S(1)} %get-tuple-element.44.own, f32[16,512]{1,0:T(8,128)S(1)} %collective-permute-done.x_chip, f32[16,512]{1,0:T(8,128)S(1)} %collective-permute-done.1.x_core, ...), custom_call_target="tpu_custom_call" | custom-call | tf_op jit(solution)/shard_map/solute_kernel/pallas_call | solution.py:647
  39.6 0.8 %collective-permute-done.8.by_next = f32[8,128]{1,0:T(8,128)S(1)} collective-permute-done((f32[8,128]{1,0:T(8,128)S(1)}, f32[8,128]{1,0:T(8,128)S(1)}, u32[]{:S(2)}, u32[]{:S(2)}) %collective-permute-start.8) | collective-permute-done | bytes 4128 | tf_op jit(solution)/shard_map/ppermute | solution.py:734
  40.5 0.0 collective-permute-done.7.by_chip
  40.5 0.8 %solve_kernel.1 = f32[1,16,128]{2,1,0:T(8,128)} custom-call(f32[16,8,128]{2,1,0:T(8,128)S(1)} %get-tuple-element.62.f, f32[16,128]{1,0:T(8,128)S(1)} %collective-permute-done.7.by_chip, f32[16,128]{1,0:T(8,128)S(1)} %collective-permute-done.6.by_core, f32[8,128]{1,0:T(8,128)S(1)} %collective-permute-done.8.by_next, ...), custom_call_target="tpu_custom_call" | custom-call | tf_op jit(solution)/shard_map/solve_kernel/pallas_call | solution.py:647
  (4 shorter events, 0.1 us)
Async XLA Ops:
  2.0 14.1 %collective-permute-start.2 = (f32[160,512]{1,0:T(8,128)S(1)}, f32[160,512]{1,0:T(8,128)S(1)}, u32[]{:S(2)}, u32[]{:S(2)}) collective-permute-start(f32[160,512]{1,0:T(8,128)S(1)} %get-tuple-element.45), channel_id=1, source_target_pairs={{0,1},{1,0},{2,3},{3,2},{4,5},{5,4},{6,7},{7,6},{8,9},{9,8},{10,11... | collective-permute-start | bytes 983048 | tf_op jit(solution)/shard_map/ppermute | solution.py:679
  2.1 14.0 %collective-permute-start.3 = (f32[160,512]{1,0:T(8,128)S(1)}, f32[160,512]{1,0:T(8,128)S(1)}, u32[]{:S(2)}, u32[]{:S(2)}) collective-permute-start(f32[160,512]{1,0:T(8,128)S(1)} %get-tuple-element.46), channel_id=1, source_target_pairs={{0,32},{32,0},{64,96},{96,64},{128,160},{160,128},{192,224},{224,1... | collective-permute-start | bytes 983048 | tf_op jit(solution)/shard_map/ppermute | solution.py:680
  5.1 6.7 %collective-permute-start = (f32[16,512]{1,0:T(8,128)S(1)}, f32[16,512]{1,0:T(8,128)S(1)}, u32[]{:S(2)}, u32[]{:S(2)}) collective-permute-start(f32[16,512]{1,0:T(8,128)S(1)} %get-tuple-element.36), channel_id=1, source_target_pairs={{0,31},{1,2},{2,1},{3,4},{4,3},{5,6},{6,5},{7,8},{8,7},{9,10},{10,... | collective-permute-start | bytes 98312 | tf_op jit(solution)/shard_map/ppermute | solution.py:682
  9.8 1.9 %collective-permute-start.1 = (f32[16,512]{1,0:T(8,128)S(1)}, f32[16,512]{1,0:T(8,128)S(1)}, u32[]{:S(2)}, u32[]{:S(2)}) collective-permute-start(f32[16,512]{1,0:T(8,128)S(1)} %get-tuple-element.37), channel_id=1, source_target_pairs={{0,1},{1,0},{2,3},{3,2},{4,5},{5,4},{6,7},{7,6},{8,9},{9,8},{10,11... | collective-permute-start | bytes 98312 | tf_op jit(solution)/shard_map/ppermute | solution.py:683
  11.7 5.7 %collective-permute-start.4 = (f32[56,512]{1,0:T(8,128)S(1)}, f32[56,512]{1,0:T(8,128)S(1)}, u32[]{:S(2)}, u32[]{:S(2)}) collective-permute-start(f32[56,512]{1,0:T(8,128)S(1)} %get-tuple-element.47), channel_id=1, source_target_pairs={{0,1},{1,0},{2,3},{3,2},{4,5},{5,4},{6,7},{7,6},{8,9},{9,8},{10,11... | collective-permute-start | bytes 344072 | tf_op jit(solution)/shard_map/ppermute | solution.py:693
  11.8 7.1 %collective-permute-start.5 = (f32[56,512]{1,0:T(8,128)S(1)}, f32[56,512]{1,0:T(8,128)S(1)}, u32[]{:S(2)}, u32[]{:S(2)}) collective-permute-start(f32[56,512]{1,0:T(8,128)S(1)} %get-tuple-element.48), channel_id=1, source_target_pairs={{0,32},{32,0},{64,96},{96,64},{128,160},{160,128},{192,224},{224,1... | collective-permute-start | bytes 344072 | tf_op jit(solution)/shard_map/ppermute | solution.py:694
  32.8 1.3 %collective-permute-start.6 = (f32[16,128]{1,0:T(8,128)S(1)}, f32[16,128]{1,0:T(8,128)S(1)}, u32[]{:S(2)}, u32[]{:S(2)}) collective-permute-start(f32[16,128]{1,0:T(8,128)S(1)} %get-tuple-element.64), channel_id=1, source_target_pairs={{0,1},{1,0},{2,3},{3,2},{4,5},{5,4},{6,7},{7,6},{8,9},{9,8},{10,11... | collective-permute-start | bytes 24584 | tf_op jit(solution)/shard_map/ppermute | solution.py:733
  34.0 6.4 %collective-permute-start.7 = (f32[16,128]{1,0:T(8,128)S(1)}, f32[16,128]{1,0:T(8,128)S(1)}, u32[]{:S(2)}, u32[]{:S(2)}) collective-permute-start(f32[16,128]{1,0:T(8,128)S(1)} %pass_kernel.1), channel_id=1, source_target_pairs={{0,32},{1,2},{2,1},{3,4},{4,3},{5,6},{6,5},{7,8},{8,7},{9,10},{10,... | collective-permute-start | bytes 24584 | tf_op jit(solution)/shard_map/ppermute | solution.py:735
  36.9 3.6 %collective-permute-start.8 = (f32[8,128]{1,0:T(8,128)S(1)}, f32[8,128]{1,0:T(8,128)S(1)}, u32[]{:S(2)}, u32[]{:S(2)}) collective-permute-start(f32[8,128]{1,0:T(8,128)S(1)} %get-tuple-element.65), channel_id=1, source_target_pairs={{0,1},{1,3},{2,0},{3,5},{4,2},{5,7},{6,4},{7,9},{8,6},{9,11},{10,8... | collective-permute-start | bytes 12296 | tf_op jit(solution)/shard_map/ppermute | solution.py:734

commit v9 on v7

--- a/solution.py
+++ b/solution.py
@@ -243,11 +243,6 @@
         ref[at, 4 * k : 4 * k + 4] = jnp.broadcast_to(rough[k : k + 1], (4, NY))
 
 
-def spread_kernel(coarse, fine):
-    for k in range(3):
-        widen(fine, k, spread(coarse[k]))
-
-
 def local_terms(c, state, own, fine, fx, fz, known, scale, dxy):
     r0 = 8 * c
     here, at, after = pl.ds(r0, 8), pl.ds(r0 + 8, 8), pl.ds(r0 + 16, 8)
@@ -273,9 +268,11 @@
         scale[z - 1, here] = DT * inverse(wt)
 
 
-def inside_kernel(state, fine, consts_in, own, fx, fz, known, scale, dxy, consts, sem):
+def inside_kernel(state, coarse, consts_in, own, fx, fz, known, scale, dxy, fine, consts, sem):
     fetch = pltpu.make_async_copy(consts_in, consts, sem)
     fetch.start()
+    for k in range(3):
+        widen(fine, k, spread(coarse[k]))
     for z in range(NPL):
         own[z, 8 : 8 + BX] = state[0, z]
 
@@ -681,14 +678,13 @@
     to_chip, to_core = kernel(column_kernel, [sds(16, NY)] * 2)(state, coarse)
     x_chip = lax.ppermute(to_chip, BOTH, CHIPS)
     x_core = lax.ppermute(to_core, "wide", CORES)
-    fine = kernel(spread_kernel, sds(3, BX, NY))(coarse)
     shapes = [
         sds(NPL, BX + 16, NY), sds(2, BX, NY), sds(2, BX, NY), sds(NPL, BX, NY), sds(2, BX, NY),
         sds(2, 2, BX, NY),
     ]
-    *inside, consts = kernel(
-        inside_kernel, shapes + [sds(*CONSTS.shape)], [pltpu.SemaphoreType.DMA], far=(2,)
-    )(state, fine, afar(jnp.asarray(CONSTS)))
+    *inside, fine, consts = kernel(
+        inside_kernel, shapes + [sds(3, BX, NY), sds(*CONSTS.shape)], [pltpu.SemaphoreType.DMA], far=(2,)
+    )(state, coarse, afar(jnp.asarray(CONSTS)))
     late_b, late_a = kernel(late_kernel, [sds(LATE, NY)] * 2)(state, x_chip, x_core, inside[0])
     lb = lax.ppermute(late_b, BOTH, PAIR_B)
     la = lax.ppermute(late_a, "narrow", PAIR_A)

time: 41.2 us -> 41.2 us (level)
    pallas_call x12 -> x11, Pallas kernels: 7.05 us -> 7.07 us  [call(): pl.pallas_call(body, out_shape=outs, in_specs=[HBM if i in far else VMEM...]
where the time goes in v9:
time: 41.2 us; the launch traced here: 41 us
  starting transfers between devices  16.4 us (40%)
  blocking collectives  13.4 us (33%)
  Pallas kernels  7.07 us (17%)
  waiting for transfers between devices  3.38 us (8%)
  between operations  0.73 us (2%)
    all_to_all x1, blocking collectives, on_device(): lax.all_to_all(jnp.broadcast_to(spectral[None], (NNAR, CX, CY)), 'narrow'...  13.4 us
    pallas_call x11, Pallas kernels, call(): pl.pallas_call(body, out_shape=outs, in_specs=[HBM if i in far else VMEM...  7.07 us
    ppermute x1, starting transfers between devices, on_device(): x_chip = lax.ppermute(to_chip, BOTH, CHIPS)  4.71 us
    ppermute x1, starting transfers between devices, on_device(): la = lax.ppermute(late_a, 'narrow', PAIR_A)  3.95 us
    ppermute x1, starting transfers between devices, on_device(): za = lax.ppermute(face_a, 'narrow', PAIR_A)  2.97 us
    ppermute x1, starting transfers between devices, on_device(): lax.ppermute(kernel(pass_kernel, sds(16, CY))(to_chip, by_core, consts),...  2.86 us
    ppermute x1, starting transfers between devices, on_device(): by_next = lax.ppermute(to_next, BOTH, INWARD)  1.6 us
    ppermute x1, waiting for transfers between devices, on_device(): la = lax.ppermute(late_a, 'narrow', PAIR_A)  1.2 us
  transfers between devices with their start and end apart: 9, of which 4 were waited for; matrix products, arithmetic and copies ran while one was open for 0% of the time, Pallas kernels for 11%

profile of v9, /device:TPU:8, one launch (start us, length us, event | category | flops | bytes accessed | tf_op | source)
XLA Modules:
  0.0 41.0 jit_solution(9226616214446804669)
XLA Ops:
  0.6 1.3 %stage_kernel.1 = (f32[168,512]{1,0:T(8,128)S(1)}, f32[168,512]{1,0:T(8,128)S(1)}, f32[2,4,64,512]{3,2,1,0:T(8,128)S(1)}, f32[4,16,128]{2,1,0:T(8,128)S(1)}) custom-call(f32[2,4,64,512]{3,2,1,0:T(8,128)} %state_in.1, s32[1,16,128]{2,1,0:T(8,128)} %ids_in.1, s32[1,16,128]{2,1,0:T(8,128)} %frozen_in.1, f32[1,16,128]{2,1,0:T(8,128)} %temp_in.1, f32[1,64]{1,0:T(1,128)} %bitcast.1), custom_call_target="tpu_custom_call" | custom-call | tf_op jit(solution)/shard_map/stage_kernel/pallas_call | solution.py:644
  2.0 0.1 collective-permute-start.2
  2.1 3.0 %collective-permute-start.3 = (f32[168,512]{1,0:T(8,128)S(1)}, f32[168,512]{1,0:T(8,128)S(1)}, u32[]{:S(2)}, u32[]{:S(2)}) collective-permute-start(f32[168,512]{1,0:T(8,128)S(1)} %get-tuple-element.48), channel_id=1, source_target_pairs={{0,32},{32,0},{64,96},{96,64},{128,160},{160,128},{192,224},{224,1... | collective-permute-start | bytes 1032200 | tf_op jit(solution)/shard_map/ppermute | solution.py:677
  5.1 4.7 %collective-permute-start = (f32[16,512]{1,0:T(8,128)S(1)}, f32[16,512]{1,0:T(8,128)S(1)}, u32[]{:S(2)}, u32[]{:S(2)}) collective-permute-start(f32[16,512]{1,0:T(8,128)S(1)} %get-tuple-element.38), channel_id=1, source_target_pairs={{0,31},{1,2},{2,1},{3,4},{4,3},{5,6},{6,5},{7,8},{8,7},{9,10},{10,... | collective-permute-start | bytes 98312 | tf_op jit(solution)/shard_map/ppermute | solution.py:679
  9.8 0.0 collective-permute-start.1
  9.8 1.2 %inside_kernel.1 = (f32[4,80,512]{2,1,0:T(8,128)S(1)}, f32[2,64,512]{2,1,0:T(8,128)S(1)}, f32[2,64,512]{2,1,0:T(8,128)S(1)}, f32[4,64,512]{2,1,0:T(8,128)S(1)}, ...) custom-call(f32[2,4,64,512]{3,2,1,0:T(8,128)S(1)} %get-tuple-element, ...), custom_call_target="tpu_custom_call" | custom-call | tf_op jit(solution)/shard_map/inside_kernel/pallas_call | solution.py:644
  11.0 0.8 %collective-permute-done.x_chip = f32[16,512]{1,0:T(8,128)S(1)} collective-permute-done((f32[16,512]{1,0:T(8,128)S(1)}, f32[16,512]{1,0:T(8,128)S(1)}, u32[]{:S(2)}, u32[]{:S(2)}) %collective-permute-start) | collective-permute-done | bytes 32800 | tf_op jit(solution)/shard_map/ppermute | solution.py:679
  11.7 0.0 collective-permute-done.1.x_core
  11.7 0.1 collective-permute-start.4
  11.8 3.9 %collective-permute-start.5 = (f32[48,512]{1,0:T(8,128)S(1)}, f32[48,512]{1,0:T(8,128)S(1)}, u32[]{:S(2)}, u32[]{:S(2)}) collective-permute-start(f32[48,512]{1,0:T(8,128)S(1)} %get-tuple-element.50), channel_id=1, source_target_pairs={{0,32},{32,0},{64,96},{96,64},{128,160},{160,128},{192,224},{224,1... | collective-permute-start | bytes 294920 | tf_op jit(solution)/shard_map/ppermute | solution.py:690
  15.8 0.3 edge_kernel.1
  16.1 0.0 collective-permute-done.2.zb
  16.1 0.0 collective-permute-done.3.za
  16.1 1.3 %phase_kernel.1 = (f32[4,64,512]{2,1,0:T(8,128)S(1)}, f32[16,128]{1,0:T(8,128)S(1)}, f32[16,512]{1,0:T(8,128)S(1)}) custom-call(f32[4,16,128]{2,1,0:T(8,128)S(1)} %get-tuple-element.36.coarse, f32[4,80,512]{2,1,0:T(8,128)S(1)} %get-tuple-element.46.own, f32[3,64,512]{2,1,0:T(8,128)S(1)} %get-tuple-element.37.fine, f32[2,64,512]{2,1,0:T(8,128)S(1)} %get-tuple-element.52.fx12, ...), custom_call_target="tpu_custom_call" | custom-call | tf_op jit(solution)/shard_map/phase_kernel/pallas_call | solution.py:644
  17.4 0.0 collective-permute-done.4.lb
  17.4 1.2 %collective-permute-done.5.la = f32[48,512]{1,0:T(8,128)S(1)} collective-permute-done((f32[48,512]{1,0:T(8,128)S(1)}, f32[48,512]{1,0:T(8,128)S(1)}, u32[]{:S(2)}, u32[]{:S(2)}) %collective-permute-start.5) | collective-permute-done | bytes 98336 | tf_op jit(solution)/shard_map/ppermute | solution.py:690
  18.6 0.3 rim_kernel.1
  18.9 13.4 %all_to_all.5.planes = f32[8,16,128]{2,1,0:T(8,128)S(1)} all-to-all(f32[8,16,128]{2,1,0:T(8,128)S(1)} %broadcast_in_dim.2), channel_id=1, replica_groups=mesh['narrow'=8,'wide'=32] {'narrow'}, dimensions={0} | all-to-all | bytes 131072 | tf_op jit(solution)/shard_map/all_to_all | solution.py:713
  32.4 0.1 mode_kernel.1
  32.4 0.1 collective-permute-start.6
  32.5 1.2 %collective-permute-done.6.by_core = f32[16,128]{1,0:T(8,128)S(1)} collective-permute-done((f32[16,128]{1,0:T(8,128)S(1)}, f32[16,128]{1,0:T(8,128)S(1)}, u32[]{:S(2)}, u32[]{:S(2)}) %collective-permute-start.6) | collective-permute-done | bytes 8224 | tf_op jit(solution)/shard_map/ppermute | solution.py:729
  33.7 2.9 %collective-permute-start.7 = (f32[16,128]{1,0:T(8,128)S(1)}, f32[16,128]{1,0:T(8,128)S(1)}, u32[]{:S(2)}, u32[]{:S(2)}) collective-permute-start(f32[16,128]{1,0:T(8,128)S(1)} %pass_kernel.1), channel_id=1, source_target_pairs={{0,32},{1,2},{2,1},{3,4},{4,3},{5,6},{6,5},{7,8},{8,7},{9,10},{10,... | collective-permute-start | bytes 24584 | tf_op jit(solution)/shard_map/ppermute | solution.py:731
  36.6 1.6 %collective-permute-start.8 = (f32[8,128]{1,0:T(8,128)S(1)}, f32[8,128]{1,0:T(8,128)S(1)}, u32[]{:S(2)}, u32[]{:S(2)}) collective-permute-start(f32[8,128]{1,0:T(8,128)S(1)} %get-tuple-element.67), channel_id=1, source_target_pairs={{0,1},{1,3},{2,0},{3,5},{4,2},{5,7},{6,4},{7,9},{8,6},{9,11},{10,8... | collective-permute-start | bytes 12296 | tf_op jit(solution)/shard_map/ppermute | solution.py:730
  38.2 1.7 %solute_kernel.1 = f32[2,4,64,512]{3,2,1,0:T(8,128)} custom-call(f32[2,4,64,512]{3,2,1,0:T(8,128)S(1)} %get-tuple-element.35.state, f32[4,80,512]{2,1,0:T(8,128)S(1)} %get-tuple-element.46.own, f32[16,512]{1,0:T(8,128)S(1)} %collective-permute-done.x_chip, f32[16,512]{1,0:T(8,128)S(1)} %collective-permute-done.1.x_core, ...), custom_call_target="tpu_custom_call" | custom-call | tf_op jit(solution)/shard_map/solute_kernel/pallas_call | solution.py:644
  39.9 0.3 collective-permute-done.8.by_next
  40.2 0.0 collective-permute-done.7.by_chip
  40.2 0.8 %solve_kernel.1 = f32[1,16,128]{2,1,0:T(8,128)} custom-call(f32[16,8,128]{2,1,0:T(8,128)S(1)} %get-tuple-element.64.f, f32[16,128]{1,0:T(8,128)S(1)} %collective-permute-done.7.by_chip, f32[16,128]{1,0:T(8,128)S(1)} %collective-permute-done.6.by_core, f32[8,128]{1,0:T(8,128)S(1)} %collective-permute-done.8.by_next, ...), custom_call_target="tpu_custom_call" | custom-call | tf_op jit(solution)/shard_map/solve_kernel/pallas_call | solution.py:644
  (4 shorter events, 0.1 us)
Async XLA Ops:
  2.0 14.1 %collective-permute-start.2 = (f32[168,512]{1,0:T(8,128)S(1)}, f32[168,512]{1,0:T(8,128)S(1)}, u32[]{:S(2)}, u32[]{:S(2)}) collective-permute-start(f32[168,512]{1,0:T(8,128)S(1)} %get-tuple-element.47), channel_id=1, source_target_pairs={{0,1},{1,0},{2,3},{3,2},{4,5},{5,4},{6,7},{7,6},{8,9},{9,8},{10,11... | collective-permute-start | bytes 1032200 | tf_op jit(solution)/shard_map/ppermute | solution.py:676
  2.1 14.0 %collective-permute-start.3 = (f32[168,512]{1,0:T(8,128)S(1)}, f32[168,512]{1,0:T(8,128)S(1)}, u32[]{:S(2)}, u32[]{:S(2)}) collective-permute-start(f32[168,512]{1,0:T(8,128)S(1)} %get-tuple-element.48), channel_id=1, source_target_pairs={{0,32},{32,0},{64,96},{96,64},{128,160},{160,128},{192,224},{224,1... | collective-permute-start | bytes 1032200 | tf_op jit(solution)/shard_map/ppermute | solution.py:677
  5.1 6.7 %collective-permute-start = (f32[16,512]{1,0:T(8,128)S(1)}, f32[16,512]{1,0:T(8,128)S(1)}, u32[]{:S(2)}, u32[]{:S(2)}) collective-permute-start(f32[16,512]{1,0:T(8,128)S(1)} %get-tuple-element.38), channel_id=1, source_target_pairs={{0,31},{1,2},{2,1},{3,4},{4,3},{5,6},{6,5},{7,8},{8,7},{9,10},{10,... | collective-permute-start | bytes 98312 | tf_op jit(solution)/shard_map/ppermute | solution.py:679
  9.8 1.9 %collective-permute-start.1 = (f32[16,512]{1,0:T(8,128)S(1)}, f32[16,512]{1,0:T(8,128)S(1)}, u32[]{:S(2)}, u32[]{:S(2)}) collective-permute-start(f32[16,512]{1,0:T(8,128)S(1)} %get-tuple-element.39), channel_id=1, source_target_pairs={{0,1},{1,0},{2,3},{3,2},{4,5},{5,4},{6,7},{7,6},{8,9},{9,8},{10,11... | collective-permute-start | bytes 98312 | tf_op jit(solution)/shard_map/ppermute | solution.py:680
  11.7 5.7 %collective-permute-start.4 = (f32[48,512]{1,0:T(8,128)S(1)}, f32[48,512]{1,0:T(8,128)S(1)}, u32[]{:S(2)}, u32[]{:S(2)}) collective-permute-start(f32[48,512]{1,0:T(8,128)S(1)} %get-tuple-element.49), channel_id=1, source_target_pairs={{0,1},{1,0},{2,3},{3,2},{4,5},{5,4},{6,7},{7,6},{8,9},{9,8},{10,11... | collective-permute-start | bytes 294920 | tf_op jit(solution)/shard_map/ppermute | solution.py:689
  11.8 6.8 %collective-permute-start.5 = (f32[48,512]{1,0:T(8,128)S(1)}, f32[48,512]{1,0:T(8,128)S(1)}, u32[]{:S(2)}, u32[]{:S(2)}) collective-permute-start(f32[48,512]{1,0:T(8,128)S(1)} %get-tuple-element.50), channel_id=1, source_target_pairs={{0,32},{32,0},{64,96},{96,64},{128,160},{160,128},{192,224},{224,1... | collective-permute-start | bytes 294920 | tf_op jit(solution)/shard_map/ppermute | solution.py:690
  32.4 1.3 %collective-permute-start.6 = (f32[16,128]{1,0:T(8,128)S(1)}, f32[16,128]{1,0:T(8,128)S(1)}, u32[]{:S(2)}, u32[]{:S(2)}) collective-permute-start(f32[16,128]{1,0:T(8,128)S(1)} %get-tuple-element.66), channel_id=1, source_target_pairs={{0,1},{1,0},{2,3},{3,2},{4,5},{5,4},{6,7},{7,6},{8,9},{9,8},{10,11... | collective-permute-start | bytes 24584 | tf_op jit(solution)/shard_map/ppermute | solution.py:729
  33.7 6.5 %collective-permute-start.7 = (f32[16,128]{1,0:T(8,128)S(1)}, f32[16,128]{1,0:T(8,128)S(1)}, u32[]{:S(2)}, u32[]{:S(2)}) collective-permute-start(f32[16,128]{1,0:T(8,128)S(1)} %pass_kernel.1), channel_id=1, source_target_pairs={{0,32},{1,2},{2,1},{3,4},{4,3},{5,6},{6,5},{7,8},{8,7},{9,10},{10,... | collective-permute-start | bytes 24584 | tf_op jit(solution)/shard_map/ppermute | solution.py:731
  36.6 3.6 %collective-permute-start.8 = (f32[8,128]{1,0:T(8,128)S(1)}, f32[8,128]{1,0:T(8,128)S(1)}, u32[]{:S(2)}, u32[]{:S(2)}) collective-permute-start(f32[8,128]{1,0:T(8,128)S(1)} %get-tuple-element.67), channel_id=1, source_target_pairs={{0,1},{1,3},{2,0},{3,5},{4,2},{5,7},{6,4},{7,9},{8,6},{9,11},{10,8... | collective-permute-start | bytes 12296 | tf_op jit(solution)/shard_map/ppermute | solution.py:730
